TPU v7x, 32 devices: a whole 2x2x4 slice. The times are simulated.
32 devices in a mesh: wide: 8 (over y, x, core), narrow: 4 (over z).
Axes of the slice: x: 2, y: 2, z: 4, core: 2. Of those that a mesh axis runs over, the one named last changes fastest.
Arguments:
- tokens: bfloat16 [16384, 768], P('wide'), may hold values from -6 to 6
- lengths: int32 [8], replicated, may hold values from 1 to 4096, 16384 in all
- masked: int32 [16384], P('wide'), may hold values 0 or 1
- attention_in: float32 [768, 2304], P('wide', 'narrow'), may hold values from -0.21875 to 0.21875
- attention_out: float32 [768, 768], P('narrow', 'wide'), may hold values from -0.875 to 0.875
- geglu_in: float32 [768, 2, 1152], P('wide', None, 'narrow'), may hold values from -0.21875 to 0.21875
- geglu_out: float32 [1152, 768], P('narrow', 'wide'), may hold values from -0.1875 to 0.1875
- gain_attention: float32 [768], P('wide'), may hold values from 0.1 to 1.9
- gain_feedforward: float32 [768], P('wide'), may hold values from 0.1 to 1.9
- out_grad: bfloat16 [16384, 768], P('wide'), may hold values from -6 to 6
Outputs:
- output: bfloat16 [16384, 768], P('wide')
- tokens_grad: float32 [16384, 768], P('wide')
- attention_in_grad: float32 [768, 2304], P('wide', 'narrow')
- attention_out_grad: float32 [768, 768], P('narrow', 'wide')
- geglu_in_grad: float32 [768, 2, 1152], P('wide', None, 'narrow')
- geglu_out_grad: float32 [1152, 768], P('narrow', 'wide')
- gain_attention_grad: float32 [768], P('wide')
- gain_feedforward_grad: float32 [768], P('wide')
Inputs may be any that keep to these rules, and one draw needn't show every extreme that they name: `lengths`: lengths of the 8 documents packed one after another into the 16384 tokens; they sum to 16384, and one of them is 4096 long.
All inputs are finite; a program needn't handle non-finite values. No bound on the sum of `masked` on one device may be relied on, other than what follows from the above.
Results may differ from a plain program's by a relative error of at most 0.015.
The roundings to bfloat16 on the way count: a program that leaves them out, or rounds other values in their place, can miss the bound.
Values may be sent and summed in bfloat16 or wider, within the bound.
A program may use at most 128 MiB of HBM per device.

v0:
```python
import math

import jax
import jax.numpy as jnp
from jax import lax
from jax.sharding import PartitionSpec as P

HEAD_DIM = 64
WINDOW = 128


EPSILON = 1e-05
THETA = 10000.0
NEG_LARGE = -1e30


def extended(block, sides, width):
    for axis, dim in sides:
        count = lax.axis_size(axis)
        forward = [(i, i + 1) for i in range(count - 1)]
        backward = [(target, source) for source, target in forward]
        low = lax.ppermute(
            lax.slice_in_dim(block, block.shape[dim] - width, None, axis=dim), axis, forward
        )
        high = lax.ppermute(lax.slice_in_dim(block, 0, width, axis=dim), axis, backward)
        block = jnp.concatenate([low, block, high], axis=dim)
    return block


def layer_norm(values, gain):
    row_mean = jnp.mean(values, axis=-1, keepdims=True)
    centred = values - row_mean
    row_var = jnp.mean(centred * centred, axis=-1, keepdims=True)
    return centred * lax.rsqrt(row_var + EPSILON) * gain


def rotary(values, cosine, sine):
    half_dim = values.shape[-1] // 2
    turned = jnp.concatenate([-values[..., half_dim:], values[..., :half_dim]], axis=-1)
    return values * cosine + turned * sine


def rotary_tables(positions, head_dim):
    freq_index = jnp.arange(head_dim // 2).astype(jnp.float32)
    inverse = jnp.power(jnp.float32(THETA), -2.0 * freq_index / head_dim)
    angles = positions.astype(jnp.float32)[:, None] * inverse[None, :]
    cosine = jnp.cos(angles)
    sine = jnp.sin(angles)
    return (jnp.concatenate([cosine, cosine], axis=-1), jnp.concatenate([sine, sine], axis=-1))


def document_tables(lengths, token_index):
    doc_ends = jnp.cumsum(lengths)
    finished = doc_ends[None, :] <= token_index[:, None]
    doc_number = jnp.sum(finished.astype(jnp.int32), axis=1)
    doc_start = jnp.sum(jnp.where(finished, lengths[None, :], 0), axis=1)
    doc_number = jnp.where(token_index < 0, -1, doc_number)
    return (doc_number, token_index - doc_start)


def geglu_act(gate_part, up_part):
    return jax.nn.gelu(gate_part) * up_part


def block_mask(query_docs, key_docs, block_rows, reach):
    half_reach = reach // 2
    gap = (
        jnp.arange(block_rows, dtype=jnp.int32)[:, None]
        + half_reach
        - jnp.arange(block_rows + reach, dtype=jnp.int32)[None, :]
    )
    return (query_docs[:, None] == key_docs[None, :]) & (gap >= -half_reach) & (gap <= half_reach)


def per_device(
    tokens,
    lengths,
    masked,
    attention_in,
    attention_out,
    geglu_in,
    geglu_out,
    gain_attention,
    gain_feedforward,
    out_grad,
):
    tok_rows = tokens.shape[0]
    head_dim = HEAD_DIM
    reach = WINDOW
    half_reach = reach // 2
    local_heads = attention_in.shape[1] // (3 * head_dim)
    block_most = 512
    block_rows = min(block_most, tok_rows)
    block_count = tok_rows // block_rows
    score_scale = 1.0 / math.sqrt(head_dim)
    full_in, full_out, full_geglu_in, full_geglu_out, full_gain_one, full_gain_two = (
        lax.all_gather(attention_in.astype(jnp.bfloat16), "wide", axis=0, tiled=True),
        lax.all_gather(attention_out.astype(jnp.bfloat16), "wide", axis=1, tiled=True),
        lax.all_gather(geglu_in.astype(jnp.bfloat16), "wide", axis=0, tiled=True),
        lax.all_gather(geglu_out.astype(jnp.bfloat16), "wide", axis=1, tiled=True),
        lax.all_gather(gain_attention.astype(jnp.bfloat16), "wide", axis=0, tiled=True),
        lax.all_gather(gain_feedforward.astype(jnp.bfloat16), "wide", axis=0, tiled=True),
    )
    token_index = (
        lax.axis_index("wide") * tok_rows
        - half_reach
        + jnp.arange(tok_rows + reach, dtype=jnp.int32)
    )
    doc_number, positions = document_tables(lengths, token_index)
    cosine, sine = rotary_tables(positions[half_reach : half_reach + tok_rows], head_dim)
    tokens_f = tokens.astype(jnp.float32)
    normed_one_f, norm_one_pull = jax.vjp(layer_norm, tokens_f, full_gain_one.astype(jnp.float32))
    normed_one = normed_one_f.astype(jnp.bfloat16)
    projected = jnp.dot(normed_one, full_in, preferred_element_type=jnp.float32).reshape(
        tok_rows, local_heads, 3, head_dim
    )

    def turn_both(query_raw, key_raw):
        return (
            rotary(query_raw, cosine[:, None], sine[:, None]),
            rotary(key_raw, cosine[:, None], sine[:, None]),
        )

    (queries_f, keys_f), rotary_pull = jax.vjp(turn_both, projected[:, :, 0], projected[:, :, 1])
    queries = queries_f.astype(jnp.bfloat16)
    keys_low = keys_f.astype(jnp.bfloat16)
    values_low = projected[:, :, 2].astype(jnp.bfloat16)
    pair_low = jnp.stack([keys_low, values_low], axis=1)
    pair_rims = jnp.concatenate([pair_low[:half_reach], pair_low[tok_rows - half_reach :]], 0)
    rims_wide = extended(pair_rims, (("wide", 0),), half_reach)
    pair_all = jnp.concatenate(
        [rims_wide[:half_reach], pair_low, rims_wide[rims_wide.shape[0] - half_reach :]], 0
    )
    keys_all = pair_all[:, 0]
    values_all = pair_all[:, 1]

    def block_scores(block_start):
        q_block = lax.dynamic_slice_in_dim(queries, block_start, block_rows, 0)
        k_block = lax.dynamic_slice_in_dim(keys_all, block_start, block_rows + reach, 0)
        v_block = lax.dynamic_slice_in_dim(values_all, block_start, block_rows + reach, 0)
        query_docs = lax.dynamic_slice_in_dim(doc_number, block_start + half_reach, block_rows, 0)
        key_docs = lax.dynamic_slice_in_dim(doc_number, block_start, block_rows + reach, 0)
        allowed = block_mask(query_docs, key_docs, block_rows, reach)
        raw_scores = (
            jnp.einsum("qhd,khd->hqk", q_block, k_block, preferred_element_type=jnp.float32)
            * score_scale
        )
        return (q_block, k_block, v_block, jnp.where(allowed[None], raw_scores, NEG_LARGE))

    def forward_block(block_start):
        q_block, k_block, v_block, scores = block_scores(block_start)
        row_top = jnp.max(scores, axis=-1, keepdims=True)
        weights = jnp.exp(scores - row_top)
        totals = jnp.sum(weights, axis=-1, keepdims=True)
        probs_low = (weights / totals).astype(jnp.bfloat16)
        block_out = jnp.einsum(
            "hqk,khd->qhd", probs_low, v_block, preferred_element_type=jnp.float32
        )
        return (block_out, row_top + jnp.log(totals))

    block_starts = jnp.arange(block_count, dtype=jnp.int32) * block_rows
    attended_f, log_totals = lax.map(forward_block, block_starts)
    attended = attended_f.reshape(tok_rows, local_heads * head_dim).astype(jnp.bfloat16)
    attention_part = jnp.dot(attended, full_out, preferred_element_type=jnp.float32)
    attention_total = lax.psum(attention_part, "narrow")
    residual = tokens_f + attention_total
    normed_two_f, norm_two_pull = jax.vjp(layer_norm, residual, full_gain_two.astype(jnp.float32))
    normed_two = normed_two_f.astype(jnp.bfloat16)
    gate_up = jnp.einsum(
        "td,dgf->tgf", normed_two, full_geglu_in, preferred_element_type=jnp.float32
    )
    hidden_f, geglu_pull = jax.vjp(geglu_act, gate_up[:, 0], gate_up[:, 1])
    hidden = hidden_f.astype(jnp.bfloat16)
    feed_part = jnp.dot(hidden, full_geglu_out, preferred_element_type=jnp.float32)
    feed_total = lax.psum(feed_part.astype(jnp.bfloat16), "narrow").astype(jnp.float32)
    output_f = residual + feed_total
    back_in, back_out, back_geglu_in, back_geglu_out = (
        lax.all_gather(attention_in.astype(jnp.bfloat16), "wide", axis=0, tiled=True),
        lax.all_gather(attention_out.astype(jnp.bfloat16), "wide", axis=1, tiled=True),
        lax.all_gather(geglu_in.astype(jnp.bfloat16), "wide", axis=0, tiled=True),
        lax.all_gather(geglu_out.astype(jnp.bfloat16), "wide", axis=1, tiled=True),
    )
    out_cot = out_grad.astype(jnp.float32) * masked.astype(jnp.float32)[:, None]
    cot_low = out_cot.astype(jnp.bfloat16)
    geglu_out_grad = jnp.einsum("tf,td->fd", hidden, cot_low, preferred_element_type=jnp.float32)
    hidden_grad = jnp.einsum(
        "td,fd->tf", cot_low, back_geglu_out, preferred_element_type=jnp.float32
    )
    gate_grad, up_grad = geglu_pull(hidden_grad)
    gate_up_grad = jnp.stack([gate_grad, up_grad], axis=1).astype(jnp.bfloat16)
    geglu_in_grad = jnp.einsum(
        "td,tgf->dgf", normed_two, gate_up_grad, preferred_element_type=jnp.float32
    )
    normed_two_part = jnp.einsum(
        "tgf,dgf->td", gate_up_grad, back_geglu_in, preferred_element_type=jnp.float32
    )
    normed_two_grad = lax.psum(normed_two_part, "narrow")
    residual_norm_grad, gain_two_grad = norm_two_pull(normed_two_grad)
    residual_grad = out_cot + residual_norm_grad
    output = output_f.astype(jnp.bfloat16)
    residual_low = residual_grad.astype(jnp.bfloat16)
    attention_out_grad = jnp.einsum(
        "tc,td->cd", attended, residual_low, preferred_element_type=jnp.float32
    )
    attended_grad = (
        jnp.einsum("td,cd->tc", residual_low, back_out, preferred_element_type=jnp.float32)
        .astype(jnp.bfloat16)
        .reshape(tok_rows, local_heads, head_dim)
    )

    def backward_block(carry, block_items):
        key_grads, value_grads = carry
        block_start, block_lse = block_items
        q_block, k_block, v_block, scores = block_scores(block_start)
        grad_block = lax.dynamic_slice_in_dim(attended_grad, block_start, block_rows, 0)
        probs = jnp.exp(scores - block_lse)
        probs_low = probs.astype(jnp.bfloat16)
        value_part = jnp.einsum(
            "hqk,qhd->khd", probs_low, grad_block, preferred_element_type=jnp.float32
        )
        prob_grad = jnp.einsum(
            "qhd,khd->hqk", grad_block, v_block, preferred_element_type=jnp.float32
        )
        row_dot = jnp.sum(probs * prob_grad, axis=-1, keepdims=True)
        score_grad = (probs * (prob_grad - row_dot) * score_scale).astype(jnp.bfloat16)
        query_part = jnp.einsum(
            "hqk,khd->qhd", score_grad, k_block, preferred_element_type=jnp.float32
        )
        key_part = jnp.einsum(
            "hqk,qhd->khd", score_grad, q_block, preferred_element_type=jnp.float32
        )
        key_old = lax.dynamic_slice_in_dim(key_grads, block_start, block_rows + reach, 0)
        value_old = lax.dynamic_slice_in_dim(value_grads, block_start, block_rows + reach, 0)
        key_grads = lax.dynamic_update_slice_in_dim(key_grads, key_old + key_part, block_start, 0)
        value_grads = lax.dynamic_update_slice_in_dim(
            value_grads, value_old + value_part, block_start, 0
        )
        return ((key_grads, value_grads), query_part)

    zero_grads = jnp.zeros((tok_rows + reach, local_heads, head_dim), jnp.float32)
    (key_grads, value_grads), query_blocks = lax.scan(
        backward_block, (zero_grads, zero_grads), (block_starts, log_totals)
    )
    query_grads = query_blocks.reshape(tok_rows, local_heads, head_dim)
    pair_grads = jnp.stack([key_grads, value_grads], axis=1)
    grad_rims = jnp.concatenate([pair_grads[:half_reach], pair_grads[tok_rows + half_reach :]], 0)
    rims_back = extended(grad_rims.astype(jnp.bfloat16), (("wide", 0),), half_reach).astype(
        grad_rims.dtype
    )
    middle_rows = jnp.zeros((tok_rows - reach, 2, local_heads, head_dim), jnp.float32)
    returned = jnp.concatenate(
        [rims_back[:half_reach], middle_rows, rims_back[rims_back.shape[0] - half_reach :]], 0
    )
    pair_own = pair_grads[half_reach : half_reach + tok_rows] + returned
    key_grad_own = pair_own[:, 0]
    value_grad_own = pair_own[:, 1]
    query_raw_grad, key_raw_grad = rotary_pull((query_grads, key_grad_own))
    projected_grad = (
        jnp.stack([query_raw_grad, key_raw_grad, value_grad_own], axis=2)
        .reshape(tok_rows, 3 * local_heads * head_dim)
        .astype(jnp.bfloat16)
    )
    attention_in_grad = jnp.einsum(
        "td,tc->dc", normed_one, projected_grad, preferred_element_type=jnp.float32
    )
    normed_one_part = jnp.einsum(
        "tc,dc->td", projected_grad, back_in, preferred_element_type=jnp.float32
    )
    normed_one_grad = lax.psum(normed_one_part, "narrow")
    tokens_norm_grad, gain_one_grad = norm_one_pull(normed_one_grad)
    tokens_grad = residual_grad + tokens_norm_grad
    in_shard, out_shard, geglu_in_shard, geglu_out_shard, gain_one_shard, gain_two_shard = (
        lax.psum_scatter(attention_in_grad, "wide", scatter_dimension=0, tiled=True),
        lax.psum_scatter(attention_out_grad, "wide", scatter_dimension=1, tiled=True),
        lax.psum_scatter(geglu_in_grad, "wide", scatter_dimension=0, tiled=True),
        lax.psum_scatter(geglu_out_grad, "wide", scatter_dimension=1, tiled=True),
        lax.psum_scatter(gain_one_grad, "wide", scatter_dimension=0, tiled=True),
        lax.psum_scatter(gain_two_grad, "wide", scatter_dimension=0, tiled=True),
    )
    return (
        output,
        tokens_grad,
        in_shard,
        out_shard,
        geglu_in_shard,
        geglu_out_shard,
        gain_one_shard,
        gain_two_shard,
    )


def solution(mesh):
    return jax.shard_map(
        per_device,
        mesh=mesh,
        in_specs=(
            P("wide", None),
            P(),
            P("wide"),
            P("wide", "narrow"),
            P("narrow", "wide"),
            P("wide", None, "narrow"),
            P("narrow", "wide"),
            P("wide"),
            P("wide"),
            P("wide", None),
        ),
        out_specs=(
            P("wide", None),
            P("wide", None),
            P("wide", "narrow"),
            P("narrow", "wide"),
            P("wide", None, "narrow"),
            P("narrow", "wide"),
            P("wide"),
            P("wide"),
        ),
        check_vma=False,
    )
```

profile of v0, /device:TPU:0, one launch (start us, length us, event | category | flops | bytes accessed | tf_op | source)
XLA Modules:
  0.0 1263.7 jit_solution(7635133475458404542)
XLA Ops:
  11.2 15.7 %all-reduce.9 = (bf16[768]{0:T(1024)(128)(2,1)S(1)}, bf16[768]{0:T(1024)(128)(2,1)}) all-reduce(bf16[768]{0:T(1024)(128)(2,1)S(1)} %dynamic-update-slice, bf16[768]{0:T(1024)(128)(2,1)S(1)} %dynamic-update-slice.1), channel_id=1, replica_groups=mesh['wide'=8,'narrow'=4] {'wide'}, use_global_device_ids=true, to_apply=%add.4 | all-reduce | flops 1536 | bytes 6144
  31.0 9.8 all_gather.23
  65.3 10.4 all_gather.24
  82.7 51.2 %while.30 = (s32[]{:T(128)}, bf16[4,512,3,64]{1,3,2,0:T(8,128)(2,1)}, f32[4,3,512,1]{2,1,3,0:T(4,128)}, s32[4]{0:T(128)S(1)}, bf16[2176,3,64]{0,2,1:T(8,128)(2,1...) while((s32[]{:T(128)}, ...), condition=%wide.region_8.9_spmd, body=%wide.region_5.8_spmd.sunk | while | flops 265419776 | bytes 20553556 | solution.py:162
  145.3 11.1 all_gather.27
  156.3 13.0 %all_gather.26 = bf16[768,2,288]{2,1,0:T(2,128)(2,1)} all-gather(bf16[96,2,288]{2,1,0:T(2,128)(2,1)S(1)} %convert_element_type.151), channel_id=1, replica_groups=mesh['wide'=8,'narrow'=4] {'wide'}, dimensions={0}, use_global_device_ids=true | all-gather | bytes 995328 | tf_op jit(solution)/shard_map/all_gather | solution.py:99
  169.3 194.6 %all-reduce.15.cloned.1.call-done = f32[2048,768]{1,0:T(8,128)} async-done(((f32[2048,768]{1,0:T(8,128)}), f32[2048,768]{1,0:T(8,128)}) %all-reduce.15.cloned.1.call-update) | async-done | bytes 6291472 | tf_op jit(solution)/shard_map/psum | solution.py:165
  388.6 5.5 convolution_bitcast_fusion.1
  394.4 8.2 fusion.94
  402.6 202.6 %all-reduce.19.cloned.1.call-done = f32[2048,768]{1,0:T(8,128)} async-done(((f32[2048,768]{1,0:T(8,128)}), f32[2048,768]{1,0:T(8,128)}) %all-reduce.19.cloned.1.call-update) | async-done | bytes 6291472 | tf_op jit(solution)/shard_map/psum | solution.py:197
  605.2 6.2 multiply_reduce_fusion.1
  612.1 116.2 %all-reduce.17.cloned.1.call-done = bf16[2048,768]{1,0:T(8,128)(2,1)} async-done(((bf16[2048,768]{1,0:T(8,128)(2,1)}), bf16[2048,768]{1,0:T(8,128)(2,1)}) %all-reduce.17.cloned.1.call-update) | async-done | bytes 3145744 | tf_op jit(solution)/shard_map/psum | solution.py:175
  728.3 8.2 fusion.125
  743.8 196.3 %while.31 = (s32[]{:T(128)}, f32[2176,3,64]{0,2,1:T(8,128)}, f32[2176,3,64]{0,2,1:T(8,128)}, f32[4,512,3,64]{1,0,3,2:T(4,128)}, s32[4]{0:T(128)S(1)}, /*index=5*...) while((s32[]{:T(128)}, f32[2176,3,64]{0,2,1:T(8,128)}, ...), condition=%wide.region_18.19_spmd, body=%wide.region_16.18_spmd.sunk | while | flops 645124864 | bytes 67096432 | solution.py:241
  764.6 7.5 fusion.191
  772.1 7.8 fusion.189
  781.3 8.6 dynamic_update_slice.43
  814.4 7.4 fusion.191
  821.8 7.5 fusion.189
  830.8 8.6 dynamic_update_slice.43
  863.6 7.4 fusion.191
  871.1 7.5 fusion.189
  880.0 8.6 dynamic_update_slice.43
  912.2 7.4 fusion.191
  919.6 7.5 fusion.189
  928.5 8.6 dynamic_update_slice.43
  975.5 6.2 fusion.120
  981.8 6.1 reduce-scatter.13.cloned.1.call-done
  989.5 223.6 %all-reduce.21.cloned.1.call-done = f32[2048,768]{1,0:T(8,128)} async-done(((f32[2048,768]{1,0:T(8,128)}), f32[2048,768]{1,0:T(8,128)}) %all-reduce.21.cloned.1.call-update) | async-done | bytes 6291472 | tf_op jit(solution)/shard_map/psum | solution.py:269
  1220.9 13.9 %all-reduce.8 = (f32[768]{0:T(1024)S(1)}, f32[768]{0:T(1024)S(1)}) all-reduce(f32[768]{0:T(1024)S(1)} %get-tuple-element.288, f32[768]{0:T(1024)S(1)} %copy-done.49), channel_id=6, replica_groups=mesh['wide'=8,'narrow'=4] {'wide'}, use_global_device_ids=true, to_apply=%region_27.28.clone | all-reduce | flops 1536 | bytes 12288
  1235.9 10.5 add_add_fusion.2
  1246.4 10.0 reduce-scatter.9.cloned.1.call-done
  (323 shorter events, 244.5 us)
Async XLA Ops:
  7.2 22.1 %copy-start = (bf16[2048,768]{1,0:T(8,128)(2,1)S(1)}, bf16[2048,768]{1,0:T(8,128)(2,1)}, u32[]{:S(2)}) copy-start(bf16[2048,768]{1,0:T(8,128)(2,1)} %param.14) | copy-start | bytes 9437188
  7.2 356.7 %all-reduce.15.cloned.1.call-start = ((), (), s32[]{:S(2)}) async-start(), calls=%async_computation.4 | async-start | bytes 12582912 | tf_op jit(solution)/shard_map/psum | solution.py:165
  26.9 13.9 %copy-start.47 = (f32[768]{0:T(1024)}, f32[768]{0:T(1024)S(1)}, u32[]{:S(2)}) copy-start(f32[768]{0:T(1024)S(1)} %convert_element_type.136) | copy-start | bytes 9220
  29.3 14.1 %copy-start.30 = (f32[2048]{0:T(1024)}, f32[2048]{0:T(1024)S(1)}, u32[]{:S(2)}) copy-start(f32[2048]{0:T(1024)S(1)} %broadcast_multiply_fusion.2) | copy-start | bytes 24580
  30.4 13.0 %copy-start.45 = (f32[2048]{0:T(1024)}, f32[2048]{0:T(1024)S(1)}, u32[]{:S(2)}) copy-start(f32[2048]{0:T(1024)S(1)} %fusion.114) | copy-start | bytes 24580
  52.6 8.6 copy-start.34
  53.5 22.1 %collective-permute-start.1 = (bf16[64,2,3,64]{0,3,2,1:T(8,128)(2,1)}, bf16[64,2,3,64]{0,3,2,1:T(8,128)(2,1)}, u32[]{:S(2)}, u32[]{:S(2)}) collective-permute-start(bf16[64,2,3,64]{0,3,2,1:T(8,128)(2,1)} %get-tuple-element.356), channel_id=1, source_target_pairs={{4,0},{8,4},{12,8},{16,12},{20,16},{24,20},{28,24},{5,1},{9,5},{13... | collective-permute-start | bytes 147464 | tf_op jit(solution)/shard_map/ppermute | solution.py:25
  54.8 20.8 %collective-permute-start = (bf16[64,2,3,64]{0,3,2,1:T(8,128)(2,1)}, bf16[64,2,3,64]{0,3,2,1:T(8,128)(2,1)}, u32[]{:S(2)}, u32[]{:S(2)}) collective-permute-start(bf16[64,2,3,64]{0,3,2,1:T(8,128)(2,1)} %get-tuple-element.357), channel_id=1, source_target_pairs={{0,4},{4,8},{8,12},{12,16},{16,20},{20,24},{24,28},{1,5},{5,9},{9,... | collective-permute-start | bytes 147464 | tf_op jit(solution)/shard_map/ppermute | solution.py:22
  134.0 6.6 copy-start.51
  140.6 464.6 %all-reduce.19.cloned.1.call-start = ((), (), s32[]{:S(2)}) async-start(), calls=%async_computation.6 | async-start | bytes 12582912 | tf_op jit(solution)/shard_map/psum | solution.py:197
  383.3 345.0 %all-reduce.17.cloned.1.call-start = ((), (), s32[]{:S(2)}) async-start(), calls=%async_computation.5 | async-start | bytes 6291456 | tf_op jit(solution)/shard_map/psum | solution.py:175
  388.6 583.4 %reduce-scatter.15.cloned.1.call-start = ((), (), s32[]{:S(2)}) async-start(), calls=%async_computation.11 | async-start | bytes 1327104
  394.1 579.5 %reduce-scatter.11.cloned.1.call-start = ((), (), s32[]{:S(2)}) async-start(), calls=%async_computation.9 | async-start | bytes 2654208 | tf_op jit(solution)/shard_map/reduce_scatter | solution.py:275
  402.5 585.3 %reduce-scatter.13.cloned.1.call-start = ((), (), s32[]{:S(2)}) async-start(), calls=%async_computation.10 | async-start | bytes 884736
  605.2 6.2 copy-start.44
  728.2 8.2 copy-start.9
  728.3 8.2 copy-start.36
  739.1 4.7 copy-start.10
  739.1 4.7 copy-start.52
  940.1 5.7 copy-start.11
  940.1 5.7 copy-start.21
  942.6 8.7 collective-permute-start.2
  944.3 7.1 collective-permute-start.3
  951.3 261.8 %all-reduce.21.cloned.1.call-start = ((), (), s32[]{:S(2)}) async-start(), calls=%async_computation.7 | async-start | bytes 12582912 | tf_op jit(solution)/shard_map/psum | solution.py:269
  970.9 4.6 copy-start.31
  970.9 4.6 copy-start.46
  970.9 4.6 copy-start.48
  971.0 285.4 %reduce-scatter.9.cloned.1.call-start = ((), (), s32[]{:S(2)}) async-start(), calls=%async_computation.8 | async-start | bytes 2211840 | tf_op jit(solution)/shard_map/reduce_scatter | solution.py:273
  989.5 227.5 %copy-start.42 = (f32[2048]{0:T(1024)S(1)}, f32[2048]{0:T(1024)}, u32[]{:S(2)}) copy-start(f32[2048]{0:T(1024)} %copy-done.41) | copy-start | bytes 24580
  1213.1 4.6 copy-start.4
  1217.7 18.2 %copy-start.37 = (f32[2048]{0:T(1024)S(1)}, f32[2048]{0:T(1024)}, u32[]{:S(2)}) copy-start(f32[2048]{0:T(1024)} %convert_element_type.158) | copy-start | bytes 24580
  1217.8 18.2 %copy-start.39 = (f32[2048]{0:T(1024)S(1)}, f32[2048]{0:T(1024)}, u32[]{:S(2)}) copy-start(f32[2048]{0:T(1024)} %copy-done.38) | copy-start | bytes 24580
  (44 other events, 84.1 us)
Sparse Core Ops, SparseCore 0:
  140.7 223.1 all-reduce.14
  383.4 221.7 all-reduce.18
  608.2 120.0 all-reduce.16
  731.3 35.7 reduce-scatter.14
  770.7 42.4 reduce-scatter.10
  951.4 36.4 reduce-scatter.12
  990.2 222.8 all-reduce.20
  1217.1 39.2 reduce-scatter.8
where the time goes:
time: 1270 us; the launch traced here: 1260 us
  waiting for transfers between devices  753 us (59%)
  matrix products  168 us (13%)
  local copies, waits for them, and re-layouts  134 us (11%)
  blocking collectives  73.8 us (6%)
  other arithmetic  73.1 us (6%)
  loops' own time  36.5 us (3%)
  between operations  16.5 us (1%)
    psum x1, waiting for transfers between devices, per_device(): normed_one_grad = lax.psum(normed_one_part, 'narrow')  224 us
    psum x1, waiting for transfers between devices, per_device(): normed_two_grad = lax.psum(normed_two_part, 'narrow')  203 us
    psum x1, waiting for transfers between devices, per_device(): attention_total = lax.psum(attention_part, 'narrow')  195 us
    psum x1, waiting for transfers between devices, per_device(): lax.psum(feed_part.astype(jnp.bfloat16), 'narrow').astype(jnp.float32)  116 us
    dynamic_update_slice x8, local copies, waits for them, and re-layouts, per_device(): attended_f, log_totals = lax.map(forward_block, block_starts)  40.1 us
    dot_general x4, matrix products, backward_block(): jnp.einsum('hqk,qhd->khd', score_grad, q_block, preferred_element_type=jn...  30.4 us
    dot_general x4, matrix products, backward_block(): jnp.einsum('hqk,khd->qhd', score_grad, k_block, preferred_element_type=jn...  29.7 us
    unnamed x2, blocking collectives  29.6 us
  transfers between devices with their start and end apart: 12, of which 6 were waited for; matrix products, arithmetic and copies ran while one was open for 22% of the time, Pallas kernels for 0%

commit v1 on v0

v1 whole, which is shorter than its diff:
```python
import math

import jax
import jax.numpy as jnp
from jax import lax
from jax.sharding import PartitionSpec as P

HEAD_DIM = 64
WINDOW = 128
HALF = WINDOW // 2
BLOCK = 128

EPSILON = 1e-05
THETA = 10000.0
NEG_LARGE = -1e30
F32 = jnp.float32
BF16 = jnp.bfloat16


def layer_norm(values, gain):
    row_mean = jnp.mean(values, axis=-1, keepdims=True)
    centred = values - row_mean
    row_var = jnp.mean(centred * centred, axis=-1, keepdims=True)
    return centred * lax.rsqrt(row_var + EPSILON) * gain


def rotary(values, cosine, sine):
    half_dim = values.shape[-1] // 2
    turned = jnp.concatenate([-values[..., half_dim:], values[..., :half_dim]], axis=-1)
    return values * cosine + turned * sine


def rotary_back(values, cosine, sine):
    half_dim = values.shape[-1] // 2
    turned = jnp.concatenate([values[..., half_dim:], -values[..., :half_dim]], axis=-1)
    return values * cosine + turned * sine


def rotary_tables(positions, head_dim):
    freq_index = jnp.arange(head_dim // 2).astype(F32)
    inverse = jnp.power(F32(THETA), -2.0 * freq_index / head_dim)
    angles = positions.astype(F32)[:, None] * inverse[None, :]
    cosine = jnp.cos(angles)
    sine = jnp.sin(angles)
    return (jnp.concatenate([cosine, cosine], axis=-1), jnp.concatenate([sine, sine], axis=-1))


def document_tables(lengths, token_index):
    doc_ends = jnp.cumsum(lengths)
    finished = doc_ends[None, :] <= token_index[:, None]
    doc_number = jnp.sum(finished.astype(jnp.int32), axis=1)
    doc_start = jnp.sum(jnp.where(finished, lengths[None, :], 0), axis=1)
    doc_number = jnp.where(token_index < 0, -1, doc_number)
    return (doc_number, token_index - doc_start)


def geglu_act(gate_part, up_part):
    return jax.nn.gelu(gate_part) * up_part


def gathered(shard, wide_axis, narrow_axis):
    whole = lax.all_gather(shard.astype(BF16), "wide", axis=wide_axis, tiled=True)
    return lax.all_gather(whole, "narrow", axis=narrow_axis, tiled=True)


def dot(a, b, dims):
    return lax.dot_general(a, b, (dims, ((), ())), preferred_element_type=F32)


def per_device(tokens, lengths, masked, attention_in, attention_out, geglu_in, geglu_out,
               gain_attention, gain_feedforward, out_grad):
    wide, narrow = lax.axis_size("wide"), lax.axis_size("narrow")
    w, n = lax.axis_index("wide"), lax.axis_index("narrow")
    tok_rows, width = tokens.shape
    rows = tok_rows // narrow
    all_rows = rows + WINDOW
    heads = attention_in.shape[1] * narrow // (3 * HEAD_DIM)
    scale = 1.0 / math.sqrt(HEAD_DIM)

    w_in = gathered(attention_in, 0, 1)
    w_out = gathered(attention_out, 1, 0)
    w_gin = gathered(geglu_in, 0, 2)
    w_gout = gathered(geglu_out, 1, 0)
    gains = lax.all_gather(jnp.stack([gain_attention, gain_feedforward]).astype(BF16), "wide", axis=1, tiled=True).astype(F32)

    up = [(i, i + 1) for i in range(wide - 1)]
    down = [(i + 1, i) for i in range(wide - 1)]
    low = lax.ppermute(tokens[tok_rows - HALF:], "wide", up)
    high = lax.ppermute(tokens[:HALF], "wide", down)
    tokens_ext = jnp.concatenate([low, tokens, high], 0)
    mine_ext = lax.dynamic_slice_in_dim(tokens_ext, n * rows, all_rows, 0)
    token_index = w * tok_rows + n * rows - HALF + jnp.arange(all_rows, dtype=jnp.int32)
    doc_number, positions = document_tables(lengths, token_index)
    cosine, sine = rotary_tables(positions, HEAD_DIM)
    cosine, sine = cosine[:, None], sine[:, None]
    out_cot = (lax.dynamic_slice_in_dim(out_grad, n * rows, rows, 0).astype(F32)
               * lax.dynamic_slice_in_dim(masked, n * rows, rows, 0).astype(F32)[:, None])
    x_all = mine_ext.astype(F32)
    x = x_all[HALF:HALF + rows]

    n1_all = layer_norm(x_all, gains[0]).astype(BF16)
    _, norm_one_pull = jax.vjp(layer_norm, x, gains[0])
    n1 = n1_all[HALF:HALF + rows]
    projected = dot(n1_all, w_in, ((1,), (0,))).reshape(all_rows, heads, 3, HEAD_DIM)
    queries = rotary(projected[HALF:HALF + rows, :, 0], cosine[HALF:HALF + rows], sine[HALF:HALF + rows]).astype(BF16)
    keys = rotary(projected[:, :, 1], cosine, sine).astype(BF16)
    values = projected[:, :, 2].astype(BF16)

    blocks = rows // BLOCK
    q = queries.reshape(blocks, BLOCK, heads, HEAD_DIM)

    def windows(a):
        return jnp.stack([a[i * BLOCK:i * BLOCK + BLOCK + WINDOW] for i in range(blocks)])

    k, v, kd = windows(keys), windows(values), windows(doc_number)
    qd = doc_number[HALF:HALF + rows].reshape(blocks, BLOCK)
    gap = (jnp.arange(BLOCK, dtype=jnp.int32)[:, None] + HALF
           - jnp.arange(BLOCK + WINDOW, dtype=jnp.int32)[None, :])
    allowed = (qd[:, :, None] == kd[:, None, :]) & (jnp.abs(gap) <= HALF)
    scores = jnp.einsum("bqhd,bkhd->bhqk", q, k, preferred_element_type=F32) * scale
    scores = jnp.where(allowed[:, None], scores, NEG_LARGE)
    top = jnp.max(scores, axis=-1, keepdims=True)
    weights = jnp.exp(scores - top)
    probs = weights / jnp.sum(weights, axis=-1, keepdims=True)
    probs_low = probs.astype(BF16)
    attended = jnp.einsum("bhqk,bkhd->bqhd", probs_low, v, preferred_element_type=F32).reshape(rows, heads * HEAD_DIM).astype(BF16)
    residual = x + dot(attended, w_out, ((1,), (0,)))
    n2_f, norm_two_pull = jax.vjp(layer_norm, residual, gains[1])
    n2 = n2_f.astype(BF16)
    gate = dot(n2, w_gin[:, 0], ((1,), (0,)))
    up_part = dot(n2, w_gin[:, 1], ((1,), (0,)))
    hidden_f, geglu_pull = jax.vjp(geglu_act, gate, up_part)
    hidden = hidden_f.astype(BF16)
    output = (residual + dot(hidden, w_gout, ((1,), (0,)))).astype(BF16)
    output = lax.all_gather(output, "narrow", axis=0, tiled=True)

    cot_low = out_cot.astype(BF16)
    geglu_out_grad = dot(hidden, cot_low, ((0,), (0,)))
    hidden_grad = dot(cot_low, w_gout, ((1,), (1,)))
    gate_grad, up_grad = geglu_pull(hidden_grad)
    gate_grad, up_grad = gate_grad.astype(BF16), up_grad.astype(BF16)
    geglu_in_grad = jnp.stack([dot(n2, gate_grad, ((0,), (0,))), dot(n2, up_grad, ((0,), (0,)))], axis=1)
    n2_grad = dot(gate_grad, w_gin[:, 0], ((1,), (1,))) + dot(up_grad, w_gin[:, 1], ((1,), (1,)))
    residual_norm_grad, gain_two_grad = norm_two_pull(n2_grad)
    residual_grad = out_cot + residual_norm_grad
    residual_low = residual_grad.astype(BF16)
    attention_out_grad = dot(attended, residual_low, ((0,), (0,)))
    attended_grad = dot(residual_low, w_out, ((1,), (1,))).astype(BF16).reshape(blocks, BLOCK, heads, HEAD_DIM)

    v_grad = jnp.einsum("bhqk,bqhd->bkhd", probs_low, attended_grad, preferred_element_type=F32)
    p_grad = jnp.einsum("bqhd,bkhd->bhqk", attended_grad, v, preferred_element_type=F32)
    row_dot = jnp.sum(probs * p_grad, axis=-1, keepdims=True)
    s_grad = (probs * (p_grad - row_dot) * scale).astype(BF16)
    q_grad = jnp.einsum("bhqk,bkhd->bqhd", s_grad, k, preferred_element_type=F32).reshape(rows, heads, HEAD_DIM)
    k_grad = jnp.einsum("bhqk,bqhd->bkhd", s_grad, q, preferred_element_type=F32)

    def overlapped(a):
        total = jnp.zeros((all_rows, heads, HEAD_DIM), F32)
        for i in range(blocks):
            total = total + jnp.pad(a[i], ((i * BLOCK, all_rows - i * BLOCK - BLOCK - WINDOW), (0, 0), (0, 0)))
        return total

    pair = jnp.stack([overlapped(k_grad), overlapped(v_grad)], axis=1)
    devices = wide * narrow
    up_all = [(i, i + 1) for i in range(devices - 1)]
    down_all = [(i + 1, i) for i in range(devices - 1)]
    from_low = lax.ppermute(pair[all_rows - HALF:].astype(BF16), ("wide", "narrow"), up_all).astype(F32)
    from_high = lax.ppermute(pair[:HALF].astype(BF16), ("wide", "narrow"), down_all).astype(F32)
    own = pair[HALF:HALF + rows]
    own = own + jnp.concatenate([from_low, jnp.zeros((rows - WINDOW,) + own.shape[1:], F32), from_high], 0)
    c_own, s_own = cosine[HALF:HALF + rows], sine[HALF:HALF + rows]
    projected_grad = jnp.stack([rotary_back(q_grad, c_own, s_own), rotary_back(own[:, 0], c_own, s_own), own[:, 1]], axis=2)
    projected_grad = projected_grad.reshape(rows, 3 * heads * HEAD_DIM).astype(BF16)
    attention_in_grad = dot(n1, projected_grad, ((0,), (0,)))
    n1_grad = dot(projected_grad, w_in, ((1,), (1,)))
    tokens_norm_grad, gain_one_grad = norm_one_pull(n1_grad)
    tokens_grad = (residual_grad + tokens_norm_grad).astype(BF16)
    tokens_grad = lax.all_gather(tokens_grad, "narrow", axis=0, tiled=True).astype(F32)

    def scattered(grad, wide_axis, narrow_axis):
        part = lax.psum_scatter(grad.astype(BF16), "narrow", scatter_dimension=narrow_axis, tiled=True)
        return lax.psum_scatter(part, "wide", scatter_dimension=wide_axis, tiled=True).astype(F32)

    gain_sums = lax.psum_scatter(lax.psum(jnp.stack([gain_one_grad, gain_two_grad]), "narrow"), "wide", scatter_dimension=1, tiled=True)
    return (output, tokens_grad,
            scattered(attention_in_grad, 0, 1), scattered(attention_out_grad, 1, 0),
            scattered(geglu_in_grad, 0, 2), scattered(geglu_out_grad, 1, 0),
            gain_sums[0], gain_sums[1])


def solution(mesh):
    return jax.shard_map(
        per_device,
        mesh=mesh,
        in_specs=(P("wide", None), P(), P("wide"), P("wide", "narrow"), P("narrow", "wide"),
                  P("wide", None, "narrow"), P("narrow", "wide"), P("wide"), P("wide"), P("wide", None)),
        out_specs=(P("wide", None), P("wide", None), P("wide", "narrow"), P("narrow", "wide"),
                   P("wide", None, "narrow"), P("narrow", "wide"), P("wide"), P("wide")),
        check_vma=False,
    )
```

time: 1270 us -> 914 us (0.72)
  waiting for transfers between devices: 753 us -> 371 us
  local copies, waits for them, and re-layouts: 134 us -> 261 us
  loops' own time: 36.5 us -> 0 us
  other arithmetic: 73.1 us -> 39.7 us
  matrix products: 168 us -> 145 us
    psum x4 -> x0, waiting for transfers between devices: 737 us -> none  [the longest x1 224 us: per_device(): normed_one_grad = lax.psum(normed_one_part, 'narrow')]
    all_gather x0 -> x6, waiting for transfers between devices: none -> 211 us  [the longest x4 107 us: gathered(): return lax.all_gather(whole, 'narrow', axis=narrow_axis, tiled=True)]
    unnamed x117 -> x143, local copies, waits for them, and re-layouts: 21.5 us -> 199 us
    unnamed x10 -> x21, waiting for transfers between devices: 6.22 us -> 138 us
    dynamic_update_slice x16 -> x0, local copies, waits for them, and re-layouts: 67.3 us -> none  [the longest x8 40.1 us: per_device(): attended_f, log_totals = lax.map(forward_block, block_starts)]
    another operation x2 -> x0, loops' own time: 36.5 us -> none  [the longest x1 18.3 us: per_device(): attended_f, log_totals = lax.map(forward_block, block_starts)]
    unnamed x2 -> x0, blocking collectives: 29.6 us -> none
    ppermute x4, waiting for transfers between devices: 0.01 us -> 22.7 us  [the longest x1 12.7 us: per_device(): lax.ppermute(pair[all_rows - HALF:].astype(BF16), ('wide', 'narrow'), up_...]
  transfers between devices with their start and end apart: 12 -> 19, of which waited for: 6 -> 10; matrix products, arithmetic and copies ran while one was open for 22% -> 45% of each run, Pallas kernels for 0% -> 0%
where the time goes in v1:
time: 914 us; the launch traced here: 904 us
  waiting for transfers between devices  371 us (41%)
  local copies, waits for them, and re-layouts  261 us (29%)
  matrix products  145 us (16%)
  blocking collectives  63.3 us (7%)
  other arithmetic  39.7 us (4%)
  between operations  16.1 us (2%)
    unnamed x143, local copies, waits for them, and re-layouts  199 us
    unnamed x21, waiting for transfers between devices  138 us
    all_gather x4, waiting for transfers between devices, gathered(): return lax.all_gather(whole, 'narrow', axis=narrow_axis, tiled=True)  107 us
    all_gather x1, waiting for transfers between devices, per_device(): output = lax.all_gather(output, 'narrow', axis=0, tiled=True)  63.4 us
    dot_general x15, matrix products, dot(): return lax.dot_general(a, b, (dims, ((), ())), preferred_element_type=F32)  46.9 us
    all_gather x4, blocking collectives, gathered(): lax.all_gather(shard.astype(BF16), 'wide', axis=wide_axis, tiled=True)  46 us
    dot_general x1, matrix products, per_device(): jnp.einsum('bhqk,bkhd->bqhd', s_grad, k, preferred_element_type=F32)  43.7 us
    dot_general x1, matrix products, per_device(): jnp.einsum('bhqk,bqhd->bkhd', s_grad, q, preferred_element_type=F32)  43.7 us
  transfers between devices with their start and end apart: 19, of which 10 were waited for; matrix products, arithmetic and copies ran while one was open for 45% of the time, Pallas kernels for 0%

profile of v1, /device:TPU:0, one launch (start us, length us, event | category | flops | bytes accessed | tf_op | source)
XLA Modules:
  0.0 903.6 jit_solution(649539617342255536)
XLA Ops:
  8.3 11.5 %all_gather.40 = bf16[288,768]{0,1:T(8,128)(2,1)S(1)} all-gather(bf16[288,96]{0,1:T(8,128)(2,1)S(1)} %copy.124), channel_id=1, replica_groups=mesh['wide'=8,'narrow'=4] {'wide'}, dimensions={1}, use_global_device_ids=true | all-gather | bytes 497664 | tf_op jit(solution)/shard_map/all_gather | solution.py:62
  20.9 11.1 %all_gather.34 = bf16[768,576]{1,0:T(8,128)(2,1)S(1)} all-gather(bf16[96,576]{1,0:T(8,128)(2,1)S(1)} %convert_element_type.148), channel_id=1, replica_groups=mesh['wide'=8,'narrow'=4] {'wide'}, dimensions={0}, use_global_device_ids=true | all-gather | bytes 995328 | tf_op jit(solution)/shard_map/all_gather | solution.py:62
  33.5 11.0 %all_gather.38 = bf16[768,2,288]{2,1,0:T(2,128)(2,1)S(1)} all-gather(bf16[96,2,288]{2,1,0:T(2,128)(2,1)S(1)} %convert_element_type.160), channel_id=1, replica_groups=mesh['wide'=8,'narrow'=4] {'wide'}, dimensions={0}, use_global_device_ids=true | all-gather | bytes 995328 | tf_op jit(solution)/shard_map/all_gather | solution.py:62
  52.1 12.5 %all_gather.36 = bf16[192,768]{0,1:T(8,128)(2,1)S(1)} all-gather(bf16[192,96]{0,1:T(8,128)(2,1)S(1)} %copy.119), channel_id=1, replica_groups=mesh['wide'=8,'narrow'=4] {'wide'}, dimensions={1}, use_global_device_ids=true | all-gather | bytes 331776 | tf_op jit(solution)/shard_map/all_gather | solution.py:62
  68.0 7.6 all-gather
  81.4 4.7 fusion.79
  86.2 46.4 %all-gather.8.cloned.1.call-done = bf16[768,2304]{0,1:T(8,128)(2,1)} async-done(((bf16[768,576]{0,1:T(8,128)(2,1)}), bf16[768,2304]{0,1:T(8,128)(2,1)}) %all-gather.8.cloned.1.call-update) | async-done | bytes 3538960 | tf_op jit(solution)/shard_map/all_gather | solution.py:63
  132.6 5.0 fusion.109
  142.5 60.3 %all-gather.12.cloned.1.call-done = bf16[768,2,1152]{0,1,2:T(2,128)(2,1)} async-done(((bf16[768,2,288]{0,1,2:T(2,128)(2,1)}), bf16[768,2,1152]{0,1,2:T(2,128)(2,1)}) %all-gather.12.cloned.1.call-update) | async-done | bytes 3538960 | tf_op jit(solution)/shard_map/all_gather | solution.py:63
  202.8 9.3 %fusion.103 = (bf16[768,1,1152]{0,1,2:T(2,128)(2,1)}, bf16[768,1,1152]{0,1,2:T(2,128)(2,1)}) fusion(bf16[768,2,1152]{0,1,2:T(2,128)(2,1)} %all-gather.12.cloned.1.call-done), kind=kLoop, calls=%fused_computation.207 | loop fusion | bytes 7077888 | tf_op jit(solution)/shard_map/slice | solution.py:130
  212.1 8.5 copy.147
  220.6 8.5 copy.148
  263.6 4.0 fusion.28
  286.9 10.7 %copy.133 = bf16[768,2,1152]{0,1,2:T(2,128)(2,1)} copy(bf16[768,2,1152]{2,0,1:T(8,128)(2,1)} %pad_maximum_fusion.1) | data formatting | bytes 7077888 | tf_op jit(solution)/shard_map/stack | solution.py:142
  305.6 4.1 convolution_bitcast_fusion
  316.2 43.7 %fusion.31 = f32[4,256,12,64]{1,3,2,0:T(8,128)} fusion(f32[4,12,128,256]{3,2,1,0:T(8,128)} %fusion.73, bf16[4,128,12,64]{1,0,3,2:T(4,128)(2,1)} %copy-done.7, f32[4,12,128,256]{3,2,1,0:T(8,128)} %copy-done.57, f32[4,12,128]{2,1,0:T(8,128)} %copy-done.60), kind=kOutput, calls=%fused_computation.56 | convolution fusion | flops 212343040 | bytes 16539648 | tf_op jit(solution)/shard_map/bhqk,bqhd->bkhd/dot_general | solution.py:155
  363.6 43.7 %fusion.11 = f32[4,12,64,128]{3,2,1,0:T(8,128)} fusion(f32[4,12,128,256]{3,2,1,0:T(8,128)} %fusion.73, bf16[1,256,12,64]{1,3,2,0:T(8,128)(2,1)} %get-tuple-element.102, bf16[1,256,12,64]{1,3,2,0:T(8,128)(2,1)} %get-tuple-element.103, bf16[1,256,12,64]{1,3,2,0:T(8,128)(2,1)} %get-tuple-element.104, bf16[1,256,12,64]{1,3,2,0:T(8,128)(2,1)} %get-tuple-element.101, ...), kind=kOutput, calls=%fused_computation.20 | convolution fusion | flops 214702336 | bytes 15753216 | tf_op jit(solution)/shard_map/bhqk,bkhd->bqhd/dot_general | solution.py:154
  420.6 12.7 %collective-permute-done.2 = bf16[64,2,12,64]{0,3,2,1:T(8,128)(2,1)S(1)} collective-permute-done((bf16[64,2,12,64]{0,3,2,1:T(8,128)(2,1)S(1)}, bf16[64,2,12,64]{0,3,2,1:T(8,128)(2,1)S(1)}, u32[]{:S(2)}, u32[]{:S(2)}) %collective-permute-start.2) | collective-permute-done | bytes 196640 | tf_op jit(solution)/shard_map/ppermute | solution.py:167
  433.3 10.0 %collective-permute-done.3 = bf16[64,2,12,64]{0,3,2,1:T(8,128)(2,1)S(1)} collective-permute-done((bf16[64,2,12,64]{0,3,2,1:T(8,128)(2,1)S(1)}, bf16[64,2,12,64]{0,3,2,1:T(8,128)(2,1)S(1)}, u32[]{:S(2)}, u32[]{:S(2)}) %collective-permute-start.3) | collective-permute-done | bytes 196640 | tf_op jit(solution)/shard_map/ppermute | solution.py:168
  454.9 6.0 multiply_reduce_fusion.3
  471.4 32.6 %all-reduce.11.cloned.1.call-done = bf16[768,2,1152]{0,1,2:T(2,128)(2,1)} async-done(((bf16[768,2,1152]{0,1,2:T(2,128)(2,1)}), bf16[768,2,1152]{0,1,2:T(2,128)(2,1)}) %all-reduce.11.cloned.1.call-update) | async-done | bytes 3538960
  505.8 42.8 %copy.141 = bf16[768,2,288]{1,2,0:T(8,128)(2,1)} copy(bf16[768,2,288]{0,1,2:T(2,128)(2,1)S(1)} %constant_dynamic-slice_fusion) | data formatting | bytes 1769472
  548.6 82.6 %reshape.298 = bf16[768,576]{1,0:T(8,128)(2,1)} reshape(bf16[768,288,2]{2,1,0:T(8,128)(2,1)} %bitcast.174) | data formatting | bytes 1769472
  639.1 9.7 %psum.8 = f32[2,96]{1,0:T(2,128)S(1)} all-reduce(f32[2,96]{1,0:T(2,128)S(1)} %copy.146), channel_id=1, replica_groups=mesh['wide'=8,'narrow'=4] {'narrow'}, use_global_device_ids=true, to_apply=%region_26.27 | all-reduce | flops 192 | bytes 1536 | tf_op jit(solution)/shard_map/psum | solution.py:184
  650.9 33.9 %reduce-scatter.31.cloned.1.call-done = bf16[96,288]{1,0:T(8,128)(2,1)} async-done(((bf16[768,288]{1,0:T(8,128)(2,1)}), bf16[96,288]{1,0:T(8,128)(2,1)}) %reduce-scatter.31.cloned.1.call-update) | async-done | bytes 55312
  686.5 63.4 %all-gather.16.cloned.1.call-done = bf16[2048,768]{1,0:T(8,128)(2,1)} async-done(((bf16[512,768]{1,0:T(8,128)(2,1)}), bf16[2048,768]{1,0:T(8,128)(2,1)}) %all-gather.16.cloned.1.call-update) | async-done | bytes 3145744 | tf_op jit(solution)/shard_map/all_gather | solution.py:135
  749.9 38.0 %reduce-scatter.29.cloned.1.call-done = bf16[96,576]{1,0:T(8,128)(2,1)} async-done(((bf16[768,576]{1,0:T(8,128)(2,1)}), bf16[96,576]{1,0:T(8,128)(2,1)}) %reduce-scatter.29.cloned.1.call-update) | async-done | bytes 110608
  787.9 15.5 %reshape.299 = bf16[96,288,2]{2,1,0:T(8,128)(2,1)} reshape(bf16[96,576]{1,0:T(8,128)(2,1)} %reduce-scatter.29.cloned.1.call-done) | data formatting | bytes 221184
  803.4 7.8 copy.142
  812.0 40.8 %all-gather.18.cloned.1.call-done = bf16[2048,768]{1,0:T(8,128)(2,1)} async-done(((bf16[512,768]{1,0:T(8,128)(2,1)}), bf16[2048,768]{1,0:T(8,128)(2,1)}) %all-gather.18.cloned.1.call-update) | async-done | bytes 3145744 | tf_op jit(solution)/shard_map/all_gather | solution.py:178
  852.8 5.1 convert_element_type.176
  857.9 33.0 %reduce-scatter.25.cloned.1.call-done = bf16[96,576]{1,0:T(8,128)(2,1)} async-done(((bf16[768,576]{1,0:T(8,128)(2,1)}), bf16[96,576]{1,0:T(8,128)(2,1)}) %reduce-scatter.25.cloned.1.call-update) | async-done | bytes 110608
  (290 shorter events, 151.0 us)
Async XLA Ops:
  7.2 13.7 %copy-start.41 = (f32[96,576]{1,0:T(8,128)S(1)}, f32[96,576]{1,0:T(8,128)}, u32[]{:S(2)}) copy-start(f32[96,576]{1,0:T(8,128)} %param.13) | copy-start | bytes 663556
  7.2 74.2 %all-gather.14.cloned.1.call-start = ((), (), s32[]{:S(2)}) async-start(), calls=%async_computation.11 | async-start | bytes 2211840 | tf_op jit(solution)/shard_map/all_gather | solution.py:63
  20.8 111.9 %all-gather.8.cloned.1.call-start = ((), (), s32[]{:S(2)}) async-start(), calls=%async_computation.8 | async-start | bytes 4423680 | tf_op jit(solution)/shard_map/all_gather | solution.py:63
  20.9 12.5 %copy-start.40 = (f32[96,2,288]{2,1,0:T(2,128)S(1)}, f32[96,2,288]{2,1,0:T(2,128)}, u32[]{:S(2)}) copy-start(f32[96,2,288]{2,1,0:T(2,128)} %param.15) | copy-start | bytes 663556
  33.3 169.5 %all-gather.12.cloned.1.call-start = ((), (), s32[]{:S(2)}) async-start(), calls=%async_computation.10 | async-start | bytes 4423680 | tf_op jit(solution)/shard_map/all_gather | solution.py:63
  44.4 7.6 copy-start.43
  44.4 21.1 %copy-start.54 = (s32[8]{0:T(128)S(1)}, s32[8]{0:T(128)}, u32[]{:S(2)}) copy-start(s32[8]{0:T(128)} %param.11) | copy-start | bytes 100
  47.4 20.6 %copy-start.52 = (f32[96]{0:T(128)S(1)}, f32[96]{0:T(128)}, u32[]{:S(2)}) copy-start(f32[96]{0:T(128)} %param.18) | copy-start | bytes 1156
  47.4 20.6 %copy-start.53 = (f32[96]{0:T(128)S(1)}, f32[96]{0:T(128)}, u32[]{:S(2)}) copy-start(f32[96]{0:T(128)} %param.17) | copy-start | bytes 1156
  47.4 209.7 %all-gather.10.cloned.1.call-start = ((), (), s32[]{:S(2)}) async-start(), calls=%async_computation.9 | async-start | bytes 1474560 | tf_op jit(solution)/shard_map/all_gather | solution.py:63
  48.4 30.3 %collective-permute-start = (bf16[64,768]{1,0:T(8,128)(2,1)S(1)}, bf16[64,768]{1,0:T(8,128)(2,1)S(1)}, u32[]{:S(2)}, u32[]{:S(2)}) collective-permute-start(bf16[64,768]{1,0:T(8,128)(2,1)S(1)} %get-tuple-element.85), channel_id=1, source_target_pairs={{0,4},{4,8},{8,12},{12,16},{16,20},{20,24},{24,28},{1,5},{5,9},{9,... | collective-permute-start | bytes 294920 | tf_op jit(solution)/shard_map/ppermute | solution.py:88
  50.7 28.0 %collective-permute-start.1 = (bf16[64,768]{1,0:T(8,128)(2,1)S(1)}, bf16[64,768]{1,0:T(8,128)(2,1)S(1)}, u32[]{:S(2)}, u32[]{:S(2)}) collective-permute-start(bf16[64,768]{1,0:T(8,128)(2,1)S(1)} %get-tuple-element.86), channel_id=1, source_target_pairs={{4,0},{8,4},{12,8},{16,12},{20,16},{24,20},{28,24},{5,1},{9,5},{13... | collective-permute-start | bytes 294920 | tf_op jit(solution)/shard_map/ppermute | solution.py:89
  65.5 396.5 %reduce-scatter.21.cloned.1.call-start = ((), (), s32[]{:S(2)}) async-start(), calls=%async_computation.15 | async-start | bytes 1474560 | tf_op jit(solution)/shard_map/reduce_scatter | solution.py:181
  66.4 14.0 %copy-start.30 = (f32[512,64]{0,1:T(8,128)}, f32[512,64]{0,1:T(8,128)S(1)}, u32[]{:S(2)}) copy-start(f32[512,64]{0,1:T(8,128)S(1)} %fusion.82) | copy-start | bytes 393220
  67.2 13.2 %copy-start.32 = (f32[512,64]{0,1:T(8,128)}, f32[512,64]{0,1:T(8,128)S(1)}, u32[]{:S(2)}) copy-start(f32[512,64]{0,1:T(8,128)S(1)} %fusion.81) | copy-start | bytes 393220
  78.7 197.8 %copy-start.46 = (f32[512]{0:T(512)}, f32[512]{0:T(512)S(1)}, u32[]{:S(2)}) copy-start(f32[512]{0:T(512)S(1)} %dynamic-slice_convert_fusion) | copy-start | bytes 6148
  81.4 51.2 %copy-start.35 = (bf16[640,768]{1,0:T(8,128)(2,1)}, bf16[640,768]{1,0:T(8,128)(2,1)S(1)}, u32[]{:S(2)}) copy-start(bf16[640,768]{1,0:T(8,128)(2,1)S(1)} %multiply_convert_fusion.3) | copy-start | bytes 2949124
  276.5 187.5 %reduce-scatter.23.cloned.1.call-start = ((), (), s32[]{:S(2)}) async-start(), calls=%async_computation.16 | async-start | bytes 2211840 | tf_op jit(solution)/shard_map/reduce_scatter | solution.py:181
  280.5 223.6 %all-reduce.11.cloned.1.call-start = ((), (), s32[]{:S(2)}) async-start(), calls=%async_computation.22 | async-start | bytes 7077888
  363.6 272.4 %reduce-scatter.19.cloned.1.call-start = ((), (), s32[]{:S(2)}) async-start(), calls=%async_computation.14 | async-start | bytes 4423680 | tf_op jit(solution)/shard_map/reduce_scatter | solution.py:181
  417.4 15.8 %collective-permute-start.2 = (bf16[64,2,12,64]{0,3,2,1:T(8,128)(2,1)S(1)}, bf16[64,2,12,64]{0,3,2,1:T(8,128)(2,1)S(1)}, u32[]{:S(2)}, u32[]{:S(2)}) collective-permute-start(bf16[64,2,12,64]{0,3,2,1:T(8,128)(2,1)S(1)} %get-tuple-element.91), channel_id=1, source_target_pairs={{0,1},{1,2},{2,3},{3,4},{4,5},{5,6},{6,7},{7,8},{8,9},{9,10},{10,1... | collective-permute-start | bytes 589832 | tf_op jit(solution)/shard_map/ppermute | solution.py:167
  418.9 24.5 %collective-permute-start.3 = (bf16[64,2,12,64]{0,3,2,1:T(8,128)(2,1)S(1)}, bf16[64,2,12,64]{0,3,2,1:T(8,128)(2,1)S(1)}, u32[]{:S(2)}, u32[]{:S(2)}) collective-permute-start(bf16[64,2,12,64]{0,3,2,1:T(8,128)(2,1)S(1)} %get-tuple-element.92), channel_id=1, source_target_pairs={{1,0},{2,1},{3,2},{4,3},{5,4},{6,5},{7,6},{8,7},{9,8},{10,9},{11,1... | collective-permute-start | bytes 589832 | tf_op jit(solution)/shard_map/ppermute | solution.py:168
  453.0 185.3 %reduce-scatter.33.cloned.1.call-start = ((), (), s32[]{:S(2)}) async-start(), calls=%async_computation.21 | async-start | bytes 442368
  461.9 187.5 %reduce-scatter.27.cloned.1.call-start = ((), (), s32[]{:S(2)}) async-start(), calls=%async_computation.18 | async-start | bytes 442368
  463.9 220.9 %reduce-scatter.31.cloned.1.call-start = ((), (), s32[]{:S(2)}) async-start(), calls=%async_computation.20 | async-start | bytes 663552
  466.1 283.8 %all-gather.16.cloned.1.call-start = ((), (), s32[]{:S(2)}) async-start(), calls=%async_computation.12 | async-start | bytes 3932160 | tf_op jit(solution)/shard_map/all_gather | solution.py:135
  470.1 317.8 %reduce-scatter.29.cloned.1.call-start = ((), (), s32[]{:S(2)}) async-start(), calls=%async_computation.19 | async-start | bytes 1105920
  548.6 82.7 %copy-start.45 = (f32[512]{0:T(512)S(1)}, f32[512]{0:T(512)}, u32[]{:S(2)}) copy-start(f32[512]{0:T(512)} %copy-done.44) | copy-start | bytes 6148
  548.6 83.4 %copy-start.29 = (f32[512,768]{1,0:T(8,128)S(1)}, f32[512,768]{1,0:T(8,128)}, u32[]{:S(2)}) copy-start(f32[512,768]{1,0:T(8,128)} %get-tuple-element.120) | copy-start | bytes 4718596
  548.6 83.4 %copy-start.51 = (f32[512]{0:T(512)S(1)}, f32[512]{0:T(512)}, u32[]{:S(2)}) copy-start(f32[512]{0:T(512)} %copy-done.50) | copy-start | bytes 6148
  631.2 221.6 %all-gather.18.cloned.1.call-start = ((), (), s32[]{:S(2)}) async-start(), calls=%async_computation.13 | async-start | bytes 3932160 | tf_op jit(solution)/shard_map/all_gather | solution.py:178
  635.9 255.0 %reduce-scatter.25.cloned.1.call-start = ((), (), s32[]{:S(2)}) async-start(), calls=%async_computation.17 | async-start | bytes 1105920
  (48 other events, 112.5 us)
Sparse Core Ops, SparseCore 0:
  20.9 40.6 all-gather.13
  63.7 68.8 all-gather.7
  134.2 68.5 all-gather.11
  204.8 29.0 all-gather.9
  276.6 27.7 reduce-scatter.20
  306.6 37.0 reduce-scatter.22
  363.7 140.2 all-reduce.10
  507.0 65.3 reduce-scatter.18
  575.8 34.0 reduce-scatter.32
  613.1 33.8 reduce-scatter.26
  650.4 34.3 reduce-scatter.30
  686.3 63.4 all-gather.15
  753.4 34.4 reduce-scatter.28
  789.3 63.4 all-gather.17
  856.5 34.3 reduce-scatter.24

commit v2 on v1

v2 whole, which is shorter than its diff:
```python
import functools
import itertools
import math

import jax
import jax.numpy as jnp
import numpy as np
from jax import lax
from jax.experimental import pallas as pl
from jax.experimental.pallas import tpu as pltpu
from jax.sharding import PartitionSpec as P

MESH = pl.DeviceIdType.MESH
HEAD_DIM = 64
WINDOW = 128
HALF = WINDOW // 2
BLOCK = 128
SPAN = BLOCK + WINDOW
GAIN_LANES = 32
EPSILON = 1e-05
THETA = 10000.0
NEG_LARGE = -1e30
F32 = jnp.float32
BF16 = jnp.bfloat16
GELU_A = math.sqrt(2.0 / math.pi)
GELU_B = 0.044715


def round_up(value, unit):
    return -(-value // unit) * unit


def dot(a, b, ca, cb):
    return lax.dot_general(a, b, (((ca,), (cb,)), ((), ())), preferred_element_type=F32)


class Sizes:
    def __init__(self, wide, narrow, tok_rows, width, heads_width, hidden, docs):
        self.W, self.N, self.T, self.D, self.F, self.docs = wide, narrow, tok_rows, width, hidden, docs
        self.R = tok_rows // narrow
        self.E = self.R + WINDOW
        self.NB = self.R // BLOCK
        self.pairs = width // 128
        self.SH = width // wide
        self.RS = round_up(self.SH, 16)
        self.QN, self.FN = heads_width // narrow, hidden // narrow
        self.bits = (wide // 2).bit_length() - 1
        first = GAIN_LANES + 3 * self.QN
        self.real = first + self.QN + 3 * self.FN
        self.LA = round_up(first, 128)
        self.lanes = round_up(self.real, 128)
        self.O0 = self.LA - first
        cut_a = (self.LA // 256) * 128
        mid = self.LA + ((self.lanes - self.LA) // 256) * 128
        self.cuts = [(0, cut_a), (cut_a, self.LA), (self.LA, mid), (mid, self.lanes)]
        self.C = len(self.cuts)
        self.CA = 2
        self.MB = min(self.R, 256)
        self.blocks = self.R // self.MB
        self.FC = 384 if hidden % 384 == 0 else hidden
        self.HT = max(1, 192 // (2 * self.SH))
        self.TM = self.HT * 2 * self.SH


def combos(bit_list):
    out = []
    for mask in range(1 << len(bit_list)):
        out.append([b for i, b in enumerate(bit_list) if mask >> i & 1])
    return out


def layer_kernel(z, names, lengths, tokens, cot, freq, pk, out, tg, gp, *scratch):
    s = dict(zip(names, scratch))
    W, N, T, D, F, R, E, NB = z.W, z.N, z.T, z.D, z.F, z.R, z.E, z.NB
    C, SH, RS, N2 = z.C, z.SH, z.RS, z.N // 2
    wb = [s[f"wb{c}"] for c in range(C)]
    r0 = [s[f"r0{c}"] for c in range(C)]
    r1 = [s[f"r1{c}"] for c in range(C)]
    rz = [s[f"rz{c}"] for c in range(C)]
    w, n = lax.axis_index("wide"), lax.axis_index("narrow")
    core, hi = lax.rem(w, 2), lax.div(w, 2)
    place = n + core * (N - 1 - 2 * n)
    ahead = 1 - 2 * core
    first, last = place == 0, place == N - 1
    has_prev = jnp.logical_or(place > 0, w > 0)
    has_next = jnp.logical_or(place < N - 1, w < W - 1)
    prev_dev = (jnp.where(first, w - 1, w), jnp.where(first, n, n - ahead))
    next_dev = (jnp.where(last, w + 1, w), jnp.where(last, n, n + ahead))
    sib_dev = (w + 1 - 2 * core, n)

    def around(k):
        return lax.rem(n + k + N, N)

    def flip(value, bit_list):
        for b in bit_list:
            value = value + (1 - 2 * lax.rem(lax.div(hi, 1 << b), 2)) * (1 << b)
        return value

    def bit_dev(b):
        return (2 * flip(hi, [b]) + core, n)

    pending = []

    def copy_to(src, dst, send, recv, dev):
        return pltpu.make_async_remote_copy(src_ref=src, dst_ref=dst, send_sem=send, recv_sem=recv, device_id=dev, device_id_type=MESH)

    def send(src, dst, send_sem, recv_sem, dev):
        c = copy_to(src, dst, send_sem, recv_sem, dev)
        c.start()
        pending.append(c)

    def arrived(dst, send_sem, recv_sem, dev):
        copy_to(dst, dst, send_sem, recv_sem, dev).wait_recv()

    barrier = pltpu.get_barrier_semaphore()
    partners = [(w, around(k)) for k in range(1, N)] + [bit_dev(b) for b in range(z.bits)] + [sib_dev]
    for dev in partners:
        pl.semaphore_signal(barrier, inc=1, device_id=dev, device_id_type=MESH)

    @pl.when(has_prev)
    def _():
        pl.semaphore_signal(barrier, inc=1, device_id=prev_dev, device_id_type=MESH)

    @pl.when(has_next)
    def _():
        pl.semaphore_signal(barrier, inc=1, device_id=next_dev, device_id_type=MESH)

    pl.semaphore_wait(barrier, len(partners) + has_prev.astype(jnp.int32) + has_next.astype(jnp.int32))

    half_refs = [pl.ds(h * N2, N2) for h in range(2)]
    gather_order = [list(range(z.bits))[::-1], list(range(z.bits))]

    def z_start(c):
        lo, up = z.cuts[c]
        src = pk.at[:, lo:up]
        pltpu.make_async_copy(src, wb[c].at[n, hi, core], s["l_own"].at[c]).start()
        for k in range(1, N):
            send(src, wb[c].at[n, hi, core], s["zs"].at[c, k - 1], s["zr"].at[c, k - 1], (w, around(k)))

    def z_wait(c):
        lo, up = z.cuts[c]
        pltpu.make_async_copy(pk.at[:, lo:up], wb[c].at[n, hi, core], s["l_own"].at[c]).wait()
        for k in range(1, N):
            arrived(wb[c].at[around(-k), hi, core], s["zs"].at[c, k - 1], s["zr"].at[c, k - 1], (w, around(-k)))

    def s_start(c, t):
        for h in range(2):
            b = gather_order[h][t]
            for i, combo in enumerate(combos(gather_order[h][:t])):
                ref = wb[c].at[half_refs[h], flip(hi, combo), core]
                slot = (1 << t) - 1 + i
                send(ref, ref, s["ss"].at[c, h, slot], s["sr"].at[c, h, slot], bit_dev(b))

    def s_wait(c, t):
        for h in range(2):
            b = gather_order[h][t]
            for i, combo in enumerate(combos(gather_order[h][:t])):
                ref = wb[c].at[half_refs[h], flip(hi, combo + [b]), core]
                slot = (1 << t) - 1 + i
                arrived(ref, s["ss"].at[c, h, slot], s["sr"].at[c, h, slot], bit_dev(b))

    def d_start(c):
        for h in range(2):
            ref = wb[c].at[half_refs[h], :, core]
            send(ref, ref, s["ds"].at[c, h], s["dr"].at[c, h], sib_dev)

    def d_wait(c):
        for h in range(2):
            arrived(wb[c].at[half_refs[h], :, 1 - core], s["ds"].at[c, h], s["dr"].at[c, h], sib_dev)

    stages = z.bits + 2

    def gather_step(t):
        for st in reversed(range(stages)):
            c = t - st
            if not 0 <= c < C:
                continue
            if st == 0:
                z_wait(c)
            elif st <= z.bits:
                s_wait(c, st - 1)
            else:
                d_wait(c)
            if st < z.bits:
                s_start(c, st)
            elif st == z.bits:
                d_start(c)

    for c in range(C):
        z_start(c)

    xin = s["xin"]
    own = pltpu.make_async_copy(tokens.at[pl.ds(pl.multiple_of(place * R, 16), R)], xin.at[pl.ds(HALF, R)], s["l_tok"].at[0])
    own.start()

    def low_copy():
        return pltpu.make_async_copy(tokens.at[pl.ds(pl.multiple_of(place * R - HALF, 16), HALF)], xin.at[pl.ds(0, HALF)], s["l_tok"].at[1])

    def high_copy():
        return pltpu.make_async_copy(tokens.at[pl.ds(pl.multiple_of(place * R + R, 16), HALF)], xin.at[pl.ds(HALF + R, HALF)], s["l_tok"].at[2])

    def halo_to_next():
        return copy_to(tokens.at[pl.ds(T - HALF, HALF)], xin.at[pl.ds(0, HALF)], s["hs"].at[0], s["hr"].at[0], (w + 1, n))

    def halo_to_prev():
        return copy_to(tokens.at[pl.ds(0, HALF)], xin.at[pl.ds(HALF + R, HALF)], s["hs"].at[1], s["hr"].at[1], (w - 1, n))

    zeros_halo = jnp.zeros((HALF, D), BF16)

    @pl.when(place > 0)
    def _():
        low_copy().start()

    @pl.when(place < N - 1)
    def _():
        high_copy().start()

    @pl.when(jnp.logical_and(last, w < W - 1))
    def _():
        halo_to_next().start()

    @pl.when(jnp.logical_and(first, w > 0))
    def _():
        halo_to_prev().start()

    @pl.when(jnp.logical_and(first, w == 0))
    def _():
        xin[0:HALF, :] = zeros_halo

    @pl.when(jnp.logical_and(last, w == W - 1))
    def _():
        xin[HALF + R:, :] = zeros_halo

    base = w * T + place * R
    ends, total = [], jnp.int32(0)
    for d in range(z.docs):
        total = total + lengths[d]
        ends.append(total)
    cos_t, sin_t, bias_t = s["cos"], s["sin"], s["bias"]
    lane = lax.broadcasted_iota(jnp.int32, (BLOCK, 128), 1)
    low_half = lax.rem(lane, HEAD_DIM) < HEAD_DIM // 2

    def table_rows(i, carry):
        r = pl.multiple_of(i * BLOCK, BLOCK)
        t = base - HALF + r + lax.broadcasted_iota(jnp.int32, (BLOCK, 128), 0)
        start = jnp.zeros((BLOCK, 128), jnp.int32)
        for d in range(z.docs):
            start = start + jnp.where(t >= ends[d], lengths[d], 0)
        angle = (t - start).astype(F32) * freq[0:1, :]
        cos_t[pl.ds(r, BLOCK), :] = jnp.cos(angle)
        sine = jnp.sin(angle)
        sin_t[pl.ds(r, BLOCK), :] = jnp.where(low_half, -sine, sine)
        return carry

    lax.fori_loop(0, E // BLOCK, table_rows, 0)

    def bias_rows(b, carry):
        tk = base - HALF + b * BLOCK + lax.broadcasted_iota(jnp.int32, (SPAN, BLOCK), 0)
        tq = base + b * BLOCK + lax.broadcasted_iota(jnp.int32, (SPAN, BLOCK), 1)
        dk = jnp.where(tk < 0, -1, 0)
        dq = jnp.zeros((SPAN, BLOCK), jnp.int32)
        for d in range(z.docs):
            dk = dk + jnp.where(tk >= ends[d], 1, 0)
            dq = dq + jnp.where(tq >= ends[d], 1, 0)
        near = jnp.abs(tk - tq) <= HALF
        bias_t[b] = jnp.where(jnp.logical_and(dk == dq, near), 0.0, NEG_LARGE).astype(F32)
        return carry

    lax.fori_loop(0, NB, bias_rows, 0)

    own.wait()

    @pl.when(place > 0)
    def _():
        low_copy().wait()

    @pl.when(place < N - 1)
    def _():
        high_copy().wait()

    @pl.when(jnp.logical_and(first, w > 0))
    def _():
        halo_to_next().wait_recv()

    @pl.when(jnp.logical_and(last, w < W - 1))
    def _():
        halo_to_prev().wait_recv()

    @pl.when(jnp.logical_and(last, w < W - 1))
    def _():
        halo_to_next().wait_send()

    @pl.when(jnp.logical_and(first, w > 0))
    def _():
        halo_to_prev().wait_send()

    a_ready = z.CA - 1 + stages - 1
    for t in range(a_ready + 1):
        gather_step(t)

    wqkv, wot, wg, wu, wgo = s["wqkv"], s["wot"], s["wg"], s["wu"], s["wgo"]
    gcol, grow, gsum = s["gcol"], s["grow"], s["gsum"]

    def shard_pair(c, nn, i):
        a, b = wb[c][nn, i, 0], wb[c][nn, i, 1]
        if SH % 16 == 0:
            return jnp.concatenate([a[:SH], b[:SH]], axis=0)
        return jnp.concatenate([a.astype(F32)[:SH], b.astype(F32)[:SH]], axis=0).astype(BF16)

    def part(lo, up, nn, i):
        return jnp.concatenate([shard_pair(c, nn, i) for c in range(lo, up)], axis=1)

    QN, FN = z.QN, z.FN

    def unpack_a(i, carry):
        r = pl.multiple_of(i * 2 * SH, 16)
        a = [part(0, z.CA, nn, i) for nn in range(N)]
        for k in range(3):
            at = GAIN_LANES + k * QN
            wqkv[pl.ds(r, 2 * SH), k * D:(k + 1) * D] = jnp.concatenate([v[:, at:at + QN] for v in a], axis=1)
        gcol[pl.ds(r, 2 * SH), :] = a[0][:, 0:128].astype(F32)
        return carry

    lax.fori_loop(0, W // 2, unpack_a, 0)
    grow[...] = gcol[...].T[0:8, :]
    gsum[...] = jnp.zeros((8, D), F32)

    def normed(x):
        centred = x - jnp.mean(x, axis=-1, keepdims=True)
        rstd = lax.rsqrt(jnp.mean(centred * centred, axis=-1, keepdims=True) + EPSILON)
        return centred * rstd, rstd

    n1, qkv = s["n1"], s["qkv"]

    def norm_rows(i, carry):
        r = pl.multiple_of(i * BLOCK, BLOCK)
        hat, _ = normed(xin[pl.ds(r, BLOCK), :].astype(F32))
        n1[pl.ds(r, BLOCK), :] = (hat * grow[0:1, :]).astype(BF16)
        return carry

    lax.fori_loop(0, E // BLOCK, norm_rows, 0)

    def partner_lanes(x):
        lanes = lax.broadcasted_iota(jnp.int32, x.shape, 1)
        return jnp.where(lax.rem(lanes, HEAD_DIM) < HEAD_DIM // 2, pltpu.roll(x, 128 - HEAD_DIM // 2, 1), pltpu.roll(x, HEAD_DIM // 2, 1))

    def project_turned(ct, carry):
        at = pl.multiple_of(ct * 128, 128)
        y = dot(n1[...], wqkv[:, pl.ds(at, 128)], 1, 0)
        y = y * cos_t[...] + partner_lanes(y) * sin_t[...]
        y = y * jnp.where(ct < D // 128, F32(1.0 / math.sqrt(HEAD_DIM)), F32(1.0))
        qkv[:, pl.ds(at, 128)] = y.astype(BF16)
        return carry

    lax.fori_loop(0, 2 * D // 128, project_turned, 0)

    def project(ct, carry):
        at = pl.multiple_of(2 * D + ct * 256, 128)
        qkv[:, pl.ds(at, 256)] = dot(n1[...], wqkv[:, pl.ds(at, 256)], 1, 0).astype(BF16)
        return carry

    lax.fori_loop(0, D // 256, project, 0)
    gather_step(a_ready + 1)

    att, stat = s["att"], s["stat"]
    lane_row = lax.broadcasted_iota(jnp.int32, (BLOCK, 128), 1)
    keep_one = jnp.where(lane_row < HEAD_DIM, 1.0, 0.0).astype(BF16)
    keep_two = jnp.where(lane_row < HEAD_DIM, 0.0, 1.0).astype(BF16)

    def stacked(x):
        return jnp.concatenate([x * keep_one, x * keep_two], axis=0)

    def unstacked(x):
        return jnp.concatenate([x[:HEAD_DIM, :BLOCK], x[HEAD_DIM:, BLOCK:]], axis=0).T

    def unit_refs(j, b):
        lanes = [pl.ds(pl.multiple_of(k * D + j * 128, 128), 128) for k in range(3)]
        return lanes, pl.ds(pl.multiple_of(b * BLOCK, BLOCK), SPAN), pl.ds(pl.multiple_of(b * BLOCK + HALF, 16), BLOCK)

    def unit_scores(j, b):
        (lq, lk, lv), keys, queries = unit_refs(j, b)
        qs = stacked(qkv[queries, lq])
        kp, vp = qkv[keys, lk], qkv[keys, lv]
        pen = bias_t[b]
        return qs, kp, vp, dot(kp, qs, 1, 1) + jnp.concatenate([pen, pen], axis=1)

    def attend(u, carry):
        j, b = lax.div(u, NB), lax.rem(u, NB)
        _, _, vp, scores = unit_scores(j, b)
        top = jnp.max(scores, axis=0, keepdims=True)
        weights = jnp.exp(scores - top)
        inv = 1.0 / jnp.sum(weights, axis=0, keepdims=True)
        stat[u, 0:1, :] = top
        stat[u, 1:2, :] = inv
        got = unstacked(dot(vp, (weights * inv).astype(BF16), 0, 0))
        att[pl.ds(pl.multiple_of(b * BLOCK, BLOCK), BLOCK), pl.ds(pl.multiple_of(j * 128, 128), 128)] = got.astype(BF16)
        return carry

    lax.fori_loop(0, z.pairs * NB, attend, 0)
    for t in range(a_ready + 2, C + stages - 1):
        gather_step(t)

    def unpack_b(i, carry):
        r = pl.multiple_of(i * 2 * SH, 16)
        a = [shard_pair(z.CA - 1, nn, i)[:, z.LA - z.O0 - z.cuts[z.CA - 1][0]:] for nn in range(N)] if z.O0 else None
        bs = [part(z.CA, C, nn, i) for nn in range(N)]
        o_rest = QN - z.O0
        wot[pl.ds(r, 2 * SH), :] = jnp.concatenate(
            [x for nn in range(N) for x in (([a[nn]] if z.O0 else []) + [bs[nn][:, :o_rest]])], axis=1)
        for k, ref in enumerate((wg, wu, wgo)):
            at = o_rest + k * FN
            ref[pl.ds(r, 2 * SH), :] = jnp.concatenate([v[:, at:at + FN] for v in bs], axis=1)
        return carry

    lax.fori_loop(0, W // 2, unpack_b, 0)

    ost, n2, res, resg = s["ost"], s["n2"], s["resr"], s["resg"]
    hid, dgate, dup, datt = s["hid"], s["dgate"], s["dup"], s["datt"]
    MB, FC = z.MB, z.FC

    def norm_back(hat, rstd, e, gain):
        eg = e * gain
        return rstd * (eg - jnp.mean(eg, axis=-1, keepdims=True) - hat * jnp.mean(eg * hat, axis=-1, keepdims=True))

    def token_copies(stage, dest, rb, key):
        src = stage.at[pl.ds(pl.multiple_of(rb * MB, 16), MB)]
        dst = dest.at[pl.ds(pl.multiple_of(place * R + rb * MB, 16), MB)]
        local = pltpu.make_async_copy(src, dst, s[key + "l"].at[rb])
        remote = [copy_to(src, dst, s[key + "s"].at[rb, k - 1], s[key + "r"].at[rb, k - 1], (w, around(k))) for k in range(1, N)]
        return local, remote

    def token_arrivals(dest, rb, key):
        for k in range(1, N):
            source = around(-k)
            theirs = source + core * (N - 1 - 2 * source)
            ref = dest.at[pl.ds(pl.multiple_of(theirs * R + rb * MB, 16), MB)]
            arrived(ref, s[key + "s"].at[rb, k - 1], s[key + "r"].at[rb, k - 1], (w, source))

    def feed(rb, carry):
        r = pl.multiple_of(rb * MB, 16)
        rows = pl.ds(r, MB)
        x = xin[pl.ds(pl.multiple_of(rb * MB + HALF, 16), MB), :].astype(F32)
        residual = x + dot(att[rows, :], wot[...], 1, 1)
        hat, rstd = normed(residual)
        gain = grow[1:2, :]
        n2v = (hat * gain).astype(BF16)
        n2[rows, :] = n2v
        cotv = cot[rows, :]
        total_out, e = residual, None
        for f in range(0, F, FC):
            gate = dot(n2v, wg[:, f:f + FC], 1, 0)
            upv = dot(n2v, wu[:, f:f + FC], 1, 0)
            dh = dot(cotv, wgo[:, f:f + FC], 1, 0)
            sq = gate * gate
            th = jnp.tanh(GELU_A * (gate * (1.0 + GELU_B * sq)))
            half = 0.5 * (1.0 + th)
            act = gate * half
            slope = half + (0.5 * GELU_A) * gate * (1.0 - th * th) * (1.0 + (3.0 * GELU_B) * sq)
            hv = (act * upv).astype(BF16)
            dgv = (dh * upv * slope).astype(BF16)
            duv = (dh * act).astype(BF16)
            hid[rows, f:f + FC] = hv
            dgate[rows, f:f + FC] = dgv
            dup[rows, f:f + FC] = duv
            total_out = total_out + dot(hv, wgo[:, f:f + FC], 1, 1)
            more = dot(dgv, wg[:, f:f + FC], 1, 1) + dot(duv, wu[:, f:f + FC], 1, 1)
            e = more if e is None else e + more
        ost[rows, :] = total_out.astype(BF16)
        local, remote = token_copies(ost, out, rb, "o")
        local.start()
        for c in remote:
            c.start()
        gsum[1:2, :] = gsum[1:2, :] + jnp.sum(e * hat, axis=0, keepdims=True)
        grad = cotv.astype(F32) + norm_back(hat, rstd, e, gain)
        resg[rows, :] = grad
        low = grad.astype(BF16)
        res[rows, :] = low
        datt[rows, :] = dot(low, wot[...], 1, 0).astype(BF16)
        return carry

    lax.fori_loop(0, z.blocks, feed, 0)

    for c in pending:
        c.wait_send()
    pending.clear()

    def store_rows(c, nn, i, k, value):
        if RS > SH:
            value = jnp.concatenate([value, jnp.zeros((RS - SH, value.shape[1]), F32)], axis=0)
        wb[c][nn, i, k] = value.astype(BF16)

    HT, TM = z.HT, z.TM
    owx = s["owx"]

    def store_part(chunks, nn, t, value):
        lo = z.cuts[chunks[0]][0]
        for c in chunks:
            a, b = z.cuts[c]
            for i in range(HT):
                for k in range(2):
                    at = (2 * i + k) * SH
                    store_rows(c, nn, t * HT + i, k, value[at:at + SH, a - lo:b - lo])

    def grads_b(t, carry):
        r = pl.multiple_of(t * TM, 16)
        cols = pl.ds(pl.multiple_of(t * TM, 128), TM) if TM % 128 == 0 else None
        gg = dot(s["n2t"][pl.ds(r, TM), :], dgate[...], 1, 0)
        gu = dot(s["n2t"][pl.ds(r, TM), :], dup[...], 1, 0)
        go = dot(s["ct"][pl.ds(r, TM), :], hid[...], 1, 0)
        gw = dot(s["rt"][pl.ds(r, TM), :], att[...], 1, 0)
        if z.O0:
            firsts = [gw[:, nn * QN:nn * QN + z.O0] for nn in range(N)]
            spare = owx.shape[1] - N * z.O0
            if spare:
                firsts.append(jnp.zeros((TM, spare), F32))
            owx[pl.ds(r, TM), :] = jnp.concatenate(firsts, axis=1)
        for nn in range(N):
            pieces = [gw[:, nn * QN + z.O0:(nn + 1) * QN]] + [v[:, nn * FN:(nn + 1) * FN] for v in (gg, gu, go)]
            if z.lanes > z.real:
                pieces.append(jnp.zeros((TM, z.lanes - z.real), F32))
            store_part(list(range(z.CA, C)), nn, t, jnp.concatenate(pieces, axis=1))
        return carry

    def transposed(dst, src, row0):
        def body(i, carry):
            at = pl.multiple_of(i * 128, 128)
            dst[pl.ds(at, 128), :] = src[row0:row0 + R, pl.ds(at, 128)].astype(F32).T.astype(BF16)
            return carry

        lax.fori_loop(0, D // 128, body, 0)

    transposed(s["n2t"], n2, 0)
    transposed(s["ct"], cot, 0)
    transposed(s["rt"], res, 0)
    lax.fori_loop(0, D // TM, grads_b, 0)

    scatter_order = [list(range(z.bits)), list(range(z.bits))[::-1]]

    def slot_base(t):
        return sum(1 << (z.bits - 1 - u) for u in range(t))

    def r0_start(c):
        send(wb[c].at[:, :, 1 - core], r0[c], s["g0s"].at[c], s["g0r"].at[c], sib_dev)

    def r0_finish(c):
        arrived(r0[c], s["g0s"].at[c], s["g0r"].at[c], sib_dev)

        def body(i, carry):
            for nn in range(N):
                wb[c][nn, i, core] = (wb[c][nn, i, core].astype(F32) + r0[c][nn, i].astype(F32)).astype(BF16)
            return carry

        lax.fori_loop(0, W // 2, body, 0)

    def r1_start(c, t):
        for h in range(2):
            b = scatter_order[h][t]
            for i, combo in enumerate(combos(scatter_order[h][t + 1:])):
                slot = slot_base(t) + i
                send(wb[c].at[half_refs[h], flip(hi, combo + [b]), core], r1[c].at[h, slot], s["g1s"].at[c, h, slot], s["g1r"].at[c, h, slot], bit_dev(b))

    def r1_finish(c, t):
        for h in range(2):
            b = scatter_order[h][t]
            for i, combo in enumerate(combos(scatter_order[h][t + 1:])):
                slot = slot_base(t) + i
                arrived(r1[c].at[h, slot], s["g1s"].at[c, h, slot], s["g1r"].at[c, h, slot], bit_dev(b))
                hv = flip(hi, combo)
                for nn in range(N2):
                    at = h * N2 + nn
                    wb[c][at, hv, core] = (wb[c][at, hv, core].astype(F32) + r1[c][h, slot, nn].astype(F32)).astype(BF16)

    def rz_start(c):
        for k in range(1, N):
            send(wb[c].at[around(k), hi, core], rz[c].at[k - 1], s["g2s"].at[c, k - 1], s["g2r"].at[c, k - 1], (w, around(k)))

    def rz_finish(c):
        total_g = wb[c][n, hi, core].astype(F32)
        for k in range(1, N):
            arrived(rz[c].at[k - 1], s["g2s"].at[c, k - 1], s["g2r"].at[c, k - 1], (w, around(-k)))
            total_g = total_g + rz[c][k - 1].astype(F32)
        lo, up = z.cuts[c]
        gp[:, lo:up] = total_g

    def scatter_advance(chunks, st):
        for c in chunks:
            if st == 0:
                r0_start(c)
            elif st == 1:
                r0_finish(c)
                if z.bits:
                    r1_start(c, 0)
                else:
                    rz_start(c)
            elif st <= z.bits + 1:
                r1_finish(c, st - 2)
                if st - 1 < z.bits:
                    r1_start(c, st - 1)
                else:
                    rz_start(c)
            else:
                rz_finish(c)

    part_a, part_b = list(range(z.CA)), list(range(z.CA, C))
    scatter_advance(part_b, 0)

    dkv, edge, rim, rimr = s["dkv"], s["edge"], s["rim"], s["rimr"]
    dk_ref, dv_ref = dkv.at[0], dkv.at[1]

    def attend_back(j, carry):
        dkv[...] = jnp.zeros((2, E, 128), F32)

        def one(b, inner):
            u = j * NB + b
            (lq, lk, lv), keys, queries = unit_refs(j, b)
            qs, kp, vp, scores = unit_scores(j, b)
            probs = jnp.exp(scores - stat[u, 0:1, :]) * stat[u, 1:2, :]
            gs = stacked(datt[pl.ds(pl.multiple_of(b * BLOCK, BLOCK), BLOCK), pl.ds(pl.multiple_of(j * 128, 128), 128)])
            prob_grad = dot(vp, gs, 1, 1)
            row_dot = jnp.sum(probs * prob_grad, axis=0, keepdims=True)
            score_grad = (probs * (prob_grad - row_dot)).astype(BF16)
            dv_ref[keys, :] = dv_ref[keys, :] + dot(probs.astype(BF16), gs, 1, 0)
            dk_ref[keys, :] = dk_ref[keys, :] + dot(score_grad, qs, 1, 0)
            dq = unstacked(dot(kp, score_grad, 0, 0)) * F32(1.0 / math.sqrt(HEAD_DIM))
            dq = dq * cos_t[queries, :] - partner_lanes(dq) * sin_t[queries, :]
            qkv[queries, lq] = dq.astype(BF16)
            return inner

        lax.fori_loop(0, NB, one, 0)
        (_, lk, lv), _, _ = unit_refs(j, 0)
        lj = pl.ds(pl.multiple_of(j * 128, 128), 128)
        for k, ref in enumerate((dk_ref, dv_ref)):
            wide_lanes = pl.ds(pl.multiple_of(k * D + j * 128, 128), 128)
            rim[0, :, wide_lanes] = ref[0:HALF, :].astype(BF16)
            rim[1, :, wide_lanes] = ref[E - HALF:, :].astype(BF16)
            edge[0, :, wide_lanes] = ref[HALF:WINDOW, :]
            edge[1, :, wide_lanes] = ref[R:R + HALF, :]
        mid = slice(HALF, HALF + R)
        dk = dk_ref[mid, :]
        qkv[mid, lk] = (dk * cos_t[mid, :] - partner_lanes(dk) * sin_t[mid, :]).astype(BF16)
        qkv[mid, lv] = dv_ref[mid, :].astype(BF16)
        return carry

    half_pairs = z.pairs // 2
    lax.fori_loop(0, half_pairs, attend_back, 0)
    scatter_advance(part_b, 1)
    lax.fori_loop(half_pairs, z.pairs, attend_back, 0)

    def rim_to_prev():
        return copy_to(rim.at[0], rimr.at[1], s["rs"].at[0], s["rr"].at[1], prev_dev)

    def rim_to_next():
        return copy_to(rim.at[1], rimr.at[0], s["rs"].at[1], s["rr"].at[0], next_dev)

    @pl.when(has_prev)
    def _():
        rim_to_prev().start()

    @pl.when(has_next)
    def _():
        rim_to_next().start()

    @pl.when(jnp.logical_not(has_prev))
    def _():
        rimr[0] = jnp.zeros((HALF, 2 * D), BF16)

    @pl.when(jnp.logical_not(has_next))
    def _():
        rimr[1] = jnp.zeros((HALF, 2 * D), BF16)

    for st in range(2, z.bits + 2):
        scatter_advance(part_b, st)

    @pl.when(has_prev)
    def _():
        rim_to_next().wait_recv()

    @pl.when(has_next)
    def _():
        rim_to_prev().wait_recv()

    @pl.when(has_prev)
    def _():
        rim_to_prev().wait_send()

    @pl.when(has_next)
    def _():
        rim_to_next().wait_send()

    for side, row in ((0, HALF), (1, R)):
        rows = slice(row, row + HALF)
        for j in range(z.pairs):
            lk = slice(j * 128, (j + 1) * 128)
            lv = slice(D + j * 128, D + (j + 1) * 128)
            dk = edge[side, :, lk] + rimr[side, :, lk].astype(F32)
            dv = edge[side, :, lv] + rimr[side, :, lv].astype(F32)
            dk = dk * cos_t[rows, :] - partner_lanes(dk) * sin_t[rows, :]
            qkv[rows, D + j * 128:D + (j + 1) * 128] = dk.astype(BF16)
            qkv[rows, 2 * D + j * 128:2 * D + (j + 1) * 128] = dv.astype(BF16)

    tst = n2

    def input_grad(rb, carry):
        rows = pl.ds(pl.multiple_of(rb * MB, 16), MB)
        ext = pl.ds(pl.multiple_of(rb * MB + HALF, 16), MB)
        e = dot(qkv[ext, :], wqkv[...], 1, 1)
        hat, rstd = normed(xin[ext, :].astype(F32))
        gsum[0:1, :] = gsum[0:1, :] + jnp.sum(e * hat, axis=0, keepdims=True)
        tst[rows, :] = (resg[rows, :] + norm_back(hat, rstd, e, grow[0:1, :])).astype(BF16)
        local, remote = token_copies(tst, tg, rb, "t")
        local.start()
        for c in remote:
            c.start()
        return carry

    lax.fori_loop(0, z.blocks, input_grad, 0)

    gcol[...] = jnp.concatenate([gsum[...], jnp.zeros((120, D), F32)], axis=0).T
    transposed(s["n2t"], n1, HALF)

    def grads_a(t, carry):
        r = pl.multiple_of(t * TM, 16)
        g = [dot(s["n2t"][pl.ds(r, TM), :], qkv[HALF:HALF + R, k * D:(k + 1) * D], 1, 0) for k in range(3)]
        gains = gcol[pl.ds(r, TM), 0:GAIN_LANES]
        for nn in range(N):
            pieces = [gains] + [v[:, nn * QN:(nn + 1) * QN] for v in g]
            if z.O0:
                pieces.append(owx[pl.ds(r, TM), nn * z.O0:(nn + 1) * z.O0])
            store_part(part_a, nn, t, jnp.concatenate(pieces, axis=1))
        return carry

    lax.fori_loop(0, D // TM, grads_a, 0)
    scatter_advance(part_a, 0)
    scatter_advance(part_b, z.bits + 2)
    for st in range(1, z.bits + 3):
        scatter_advance(part_a, st)

    def token_end(stage, dest, key):
        def body(rb, carry):
            local, remote = token_copies(stage, dest, rb, key)
            local.wait()
            for c in remote:
                c.wait_send()
            token_arrivals(dest, rb, key)
            return carry

        lax.fori_loop(0, z.blocks, body, 0)

    for c in pending:
        c.wait_send()
    token_end(ost, out, "o")
    token_end(tst, tg, "t")


def run_layer(z, lengths, tokens, cot, freq, pk):
    shapes, names = [], []

    def vmem(name, shape, dtype):
        names.append(name)
        shapes.append(pltpu.VMEM(shape, dtype))

    def sems(name, *shape):
        names.append(name)
        shapes.append(pltpu.SemaphoreType.DMA(shape))

    W, N, D, F, R, E, C = z.W, z.N, z.D, z.F, z.R, z.E, z.C
    for c, (lo, up) in enumerate(z.cuts):
        vmem(f"wb{c}", (N, W // 2, 2, z.RS, up - lo), BF16)
        vmem(f"r0{c}", (N, W // 2, z.RS, up - lo), BF16)
        vmem(f"r1{c}", (2, W // 2 - 1, N // 2, z.RS, up - lo), BF16)
        vmem(f"rz{c}", (N - 1, z.RS, up - lo), BF16)
    vmem("xin", (E, D), BF16)
    vmem("n1", (E, D), BF16)
    vmem("qkv", (E, 3 * D), BF16)
    vmem("wqkv", (D, 3 * D), BF16)
    vmem("wot", (D, D), BF16)
    for name in ("wg", "wu", "wgo"):
        vmem(name, (D, F), BF16)
    vmem("gcol", (D, 128), F32)
    vmem("grow", (8, D), F32)
    vmem("gsum", (8, D), F32)
    vmem("owx", (D, round_up(max(N * z.O0, 1), 128)), F32)
    vmem("cos", (E, 128), F32)
    vmem("sin", (E, 128), F32)
    vmem("bias", (z.NB, SPAN, BLOCK), F32)
    vmem("stat", (z.pairs * z.NB, 8, 2 * BLOCK), F32)
    for name in ("att", "ost", "n2", "resr", "datt"):
        vmem(name, (R, D), BF16)
    for name in ("n2t", "ct", "rt"):
        vmem(name, (D, R), BF16)
    vmem("resg", (R, D), F32)
    for name in ("hid", "dgate", "dup"):
        vmem(name, (R, F), BF16)
    vmem("dkv", (2, E, 128), F32)
    vmem("edge", (2, HALF, 2 * D), F32)
    vmem("rim", (2, HALF, 2 * D), BF16)
    vmem("rimr", (2, HALF, 2 * D), BF16)
    sems("l_own", C)
    sems("l_tok", 3)
    for name in ("zs", "zr", "g2s", "g2r"):
        sems(name, C, N - 1)
    for name in ("ss", "sr", "g1s", "g1r"):
        sems(name, C, 2, W // 2 - 1)
    for name in ("ds", "dr"):
        sems(name, C, 2)
    for name in ("g0s", "g0r"):
        sems(name, C)
    for name in ("hs", "hr", "rs", "rr"):
        sems(name, 2)
    for name in ("ol", "tl"):
        sems(name, z.blocks)
    for name in ("os", "or", "ts", "tr"):
        sems(name, z.blocks, N - 1)
    hbm = pl.BlockSpec(memory_space=pl.ANY)
    vm = pl.BlockSpec(memory_space=pltpu.VMEM)
    return pl.pallas_call(
        functools.partial(layer_kernel, z, names),
        out_shape=(
            jax.ShapeDtypeStruct((z.T, D), BF16),
            jax.ShapeDtypeStruct((z.T, D), BF16),
            jax.ShapeDtypeStruct((z.RS, z.lanes), F32),
        ),
        in_specs=[pl.BlockSpec(memory_space=pltpu.SMEM), hbm, vm, vm, vm],
        out_specs=(hbm, hbm, vm),
        scratch_shapes=shapes,
        compiler_params=pltpu.CompilerParams(collective_id=0, has_side_effects=True, vmem_limit_bytes=VMEM_BYTES),
    )(lengths, tokens, cot, freq, pk)


VMEM_BYTES = 64 * 1024 * 1024 - 1024 * 64


def per_device(tokens, lengths, masked, attention_in, attention_out, geglu_in, geglu_out, gain_attention, gain_feedforward, out_grad):
    wide, narrow = lax.axis_size("wide"), lax.axis_size("narrow")
    w, n = lax.axis_index("wide"), lax.axis_index("narrow")
    z = Sizes(wide, narrow, tokens.shape[0], tokens.shape[1], attention_out.shape[0] * narrow, geglu_out.shape[0] * narrow, lengths.shape[0])
    place = jnp.where(lax.rem(w, 2) == 0, n, narrow - 1 - n)
    cot = lax.dynamic_slice_in_dim(out_grad, place * z.R, z.R, 0)
    mask = lax.dynamic_slice_in_dim(masked, place * z.R, z.R, 0)
    cot = jnp.where((mask == 1)[:, None], cot, jnp.zeros((), BF16))
    heads = z.QN // HEAD_DIM
    w_in = attention_in.astype(BF16).reshape(z.SH, heads, 3, HEAD_DIM)
    gains = jnp.stack([gain_attention, gain_feedforward], axis=1).astype(BF16)
    pk = jnp.concatenate(
        [jnp.pad(gains, ((0, 0), (0, GAIN_LANES - 2)))]
        + [w_in[:, :, k].reshape(z.SH, z.QN) for k in range(3)]
        + [attention_out.astype(BF16).T, geglu_in[:, 0].astype(BF16), geglu_in[:, 1].astype(BF16), geglu_out.astype(BF16).T],
        axis=1,
    )
    pk = jnp.pad(pk, ((0, z.RS - z.SH), (0, z.lanes - z.real)))
    j = np.arange(128) % (HEAD_DIM // 2)
    freq = jnp.asarray(np.broadcast_to((THETA ** (-2.0 * j / HEAD_DIM)).astype(np.float32)[None], (8, 128)))
    out, tg, gp = run_layer(z, lengths, tokens, cot, freq, pk)
    gp = gp[: z.SH]
    at = GAIN_LANES

    def take(count):
        nonlocal at
        value = gp[:, at:at + count]
        at += count
        return value

    in_grad = jnp.stack([take(z.QN).reshape(z.SH, heads, HEAD_DIM) for _ in range(3)], axis=2).reshape(z.SH, 3 * z.QN)
    out_w_grad = take(z.QN).T
    gate_up = jnp.stack([take(z.FN), take(z.FN)], axis=1)
    down = take(z.FN).T
    return (out, tg.astype(F32), in_grad, out_w_grad, gate_up, down, gp[:, 0], gp[:, 1])


def solution(mesh):
    return jax.shard_map(
        per_device,
        mesh=mesh,
        in_specs=(P("wide", None), P(), P("wide"), P("wide", "narrow"), P("narrow", "wide"), P("wide", None, "narrow"),
                  P("narrow", "wide"), P("wide"), P("wide"), P("wide", None)),
        out_specs=(P("wide", None), P("wide", None), P("wide", "narrow"), P("narrow", "wide"), P("wide", None, "narrow"),
                   P("narrow", "wide"), P("wide"), P("wide")),
        check_vma=False,
    )
```

time: 914 us -> 275 us (0.30)
  the two profiles are of different devices: /device:TPU:0 before, /device:TPU:24 now
where the time goes in v2:
time: 275 us
  Pallas kernels  249 us (91%)
  local copies, waits for them, and re-layouts  15.8 us (6%)
  other arithmetic  9.8 us (4%)
    pallas_call x1, Pallas kernels, run_layer(): pl.pallas_call(functools.partial(layer_kernel, z, names), out_shape=(jax....  249 us
    unnamed x17, local copies, waits for them, and re-layouts  8.13 us

profile of v2, /device:TPU:24, one launch (start us, length us, event | category | flops | bytes accessed | tf_op | source)
XLA Modules:
  0.0 274.9 jit_solution(7964319048576759083)
XLA Ops:
  0.6 0.0 copy-start.3
  0.6 0.0 copy-start.2
  0.7 0.8 dynamic-slice_compare_fusion
  1.5 2.2 dynamic-slice_select_fusion.cot
  3.7 0.7 convert_bitcast_fusion.2
  4.4 0.1 copy.48
  4.5 1.1 copy.49
  5.6 0.1 copy.53
  5.7 0.1 copy.54
  5.8 0.1 copy.55
  5.9 1.0 copy.50
  6.9 1.0 copy.65
  7.9 0.1 copy.52
  8.1 1.0 concatenate.3.pk
  9.0 0.0 copy-done.3
  9.0 0.6 jit_solution_.3.freq
  9.6 248.5 %shard_map.170 = (bf16[2048,768]{1,0:T(8,128)(2,1)}, bf16[2048,768]{1,0:T(8,128)(2,1)}, f32[96,1664]{1,0:T(8,128)}) custom-call(s32[8]{0:T(128)} %lengths.1, bf16[2048,768]{1,0:T(8,128)(2,1)} %tokens.1, bf16[512,768]{1,0:T(8,128)(2,1)} %dynamic-slice_select_fusion.cot, f32[8,128]{1,0:T(8,128)} %jit_solution_.3.freq, bf16[96,1664]{1,0:T(8,128)(2,1)} %concatenate.3.pk), custom_call_target="tpu_custom_call" | custom-call | tf_op jit(solution)/shard_map/pallas_call | solution.py:816
  258.1 0.0 copy-start.1
  258.1 5.1 %convert_element_type.28 = f32[2048,768]{1,0:T(8,128)} convert(bf16[2048,768]{1,0:T(8,128)(2,1)} %get-tuple-element.12) | non-fusion elementwise | flops 1572864 | bytes 9437184 | tf_op jit(solution)/shard_map/convert_element_type | solution.py:867
  263.3 0.0 copy-done.1
  263.3 0.8 slice_bitcast_fusion.3
  264.1 1.2 copy.58
  265.3 0.7 copy.57
  266.0 0.1 copy.56
  266.1 0.9 pad_maximum_fusion
  267.1 0.9 copy.60
  267.9 0.7 copy.61
  268.6 1.3 slice_bitcast_fusion
  270.0 0.9 copy.62
  270.9 0.8 copy.63
  271.7 1.6 slice_reduce_fusion
  273.2 1.7 copy.67
  (9 shorter events, 0.1 us)
Async XLA Ops:
  0.6 8.4 %copy-start.3 = (f32[128]{0:T(128)S(1)}, f32[128]{0:T(128)}, u32[]{:S(2)}) copy-start(f32[128]{0:T(128)} %constant.27.clone) | copy-start | bytes 1540
  0.6 7.3 %copy-start.2 = (f32[288,96]{1,0:T(8,128)S(1)}, f32[288,96]{1,0:T(8,128)}, u32[]{:S(2)}) copy-start(f32[288,96]{1,0:T(8,128)} %param.17) | copy-start | bytes 331780
  258.1 5.2 %copy-start.1 = (f32[96,1664]{1,0:T(8,128)S(1)}, f32[96,1664]{1,0:T(8,128)}, u32[]{:S(2)}) copy-start(f32[96,1664]{1,0:T(8,128)} %get-tuple-element.13) | copy-start | bytes 1916932
  263.3 10.0 %copy-start = (bf16[2048,768]{1,0:T(8,128)(2,1)S(1)}, bf16[2048,768]{1,0:T(8,128)(2,1)}, u32[]{:S(2)}) copy-start(bf16[2048,768]{1,0:T(8,128)(2,1)} %get-tuple-element.62) | copy-start | bytes 9437188

commit v3 on v2

--- a/solution.py
+++ b/solution.py
@@ -4,7 +4,6 @@
 
 import jax
 import jax.numpy as jnp
-import numpy as np
 from jax import lax
 from jax.experimental import pallas as pl
 from jax.experimental.pallas import tpu as pltpu
@@ -41,6 +40,7 @@
         self.E = self.R + WINDOW
         self.NB = self.R // BLOCK
         self.pairs = width // 128
+        self.G = 4 if self.NB % 4 == 0 else 1
         self.SH = width // wide
         self.RS = round_up(self.SH, 16)
         self.QN, self.FN = heads_width // narrow, hidden // narrow
@@ -69,11 +69,12 @@
     return out
 
 
-def layer_kernel(z, names, lengths, tokens, cot, freq, pk, out, tg, gp, *scratch):
+def layer_kernel(z, names, lengths, tokens, grads_in, masked, w_in, w_out, w_gu, w_down, gains, out, tg, gp, *scratch):
     s = dict(zip(names, scratch))
     W, N, T, D, F, R, E, NB = z.W, z.N, z.T, z.D, z.F, z.R, z.E, z.NB
     C, SH, RS, N2 = z.C, z.SH, z.RS, z.N // 2
     wb = [s[f"wb{c}"] for c in range(C)]
+    pk, cot = s["pk"], s["cot"]
     r0 = [s[f"r0{c}"] for c in range(C)]
     r1 = [s[f"r1{c}"] for c in range(C)]
     rz = [s[f"rz{c}"] for c in range(C)]
@@ -186,12 +187,40 @@
             elif st == z.bits:
                 d_start(c)
 
-    for c in range(C):
+    def flipped(x):
+        a, b = x.shape
+        a2, b2 = round_up(a, 128), round_up(b, 128)
+        if b2 > b:
+            x = jnp.concatenate([x, jnp.zeros((a, b2 - b), F32)], axis=1)
+        if a2 > a:
+            x = jnp.concatenate([x, jnp.zeros((a2 - a, b2), F32)], axis=0)
+        return x.T[:b, :a]
+
+    def pack(lo, up, pieces):
+        have = sum(p.shape[1] for p in pieces)
+        if up - lo > have:
+            pieces = pieces + [jnp.zeros((SH, up - lo - have), F32)]
+        value = jnp.concatenate(pieces, axis=1)
+        if RS > SH:
+            value = jnp.concatenate([value, jnp.zeros((RS - SH, up - lo), F32)], axis=0)
+        pk[:, lo:up] = value.astype(BF16)
+
+    QN, FN = z.QN, z.FN
+    heads = QN // HEAD_DIM
+    raw_in, out_t = w_in[...], flipped(w_out[...])
+    gain_cols = jnp.concatenate([flipped(gains[...]), jnp.zeros((SH, GAIN_LANES - 2), F32)], axis=1)
+    pack(0, z.LA, [gain_cols] + [raw_in[:, (3 * a + k) * HEAD_DIM:(3 * a + k + 1) * HEAD_DIM] for k in range(3) for a in range(heads)] + [out_t[:, :z.O0]])
+    for c in range(z.CA):
+        z_start(c)
+    pack(z.LA, z.lanes, [out_t[:, z.O0:], w_gu[...].astype(F32), flipped(w_down[...])])
+    for c in range(z.CA, C):
         z_start(c)
 
     xin = s["xin"]
     own = pltpu.make_async_copy(tokens.at[pl.ds(pl.multiple_of(place * R, 16), R)], xin.at[pl.ds(HALF, R)], s["l_tok"].at[0])
     own.start()
+    own_cot = pltpu.make_async_copy(grads_in.at[pl.ds(pl.multiple_of(place * R, 16), R)], cot, s["l_tok"].at[3])
+    own_cot.start()
 
     def low_copy():
         return pltpu.make_async_copy(tokens.at[pl.ds(pl.multiple_of(place * R - HALF, 16), HALF)], xin.at[pl.ds(0, HALF)], s["l_tok"].at[1])
@@ -240,13 +269,18 @@
     lane = lax.broadcasted_iota(jnp.int32, (BLOCK, 128), 1)
     low_half = lax.rem(lane, HEAD_DIM) < HEAD_DIM // 2
 
+    freq_lane = lax.rem(lax.broadcasted_iota(jnp.int32, (1, 128), 1), HEAD_DIM // 2)
+    freq = jnp.zeros((1, 128), F32)
+    for d in range(HEAD_DIM // 2):
+        freq = jnp.where(freq_lane == d, F32(THETA ** (-2.0 * d / HEAD_DIM)), freq)
+
     def table_rows(i, carry):
         r = pl.multiple_of(i * BLOCK, BLOCK)
         t = base - HALF + r + lax.broadcasted_iota(jnp.int32, (BLOCK, 128), 0)
         start = jnp.zeros((BLOCK, 128), jnp.int32)
         for d in range(z.docs):
             start = start + jnp.where(t >= ends[d], lengths[d], 0)
-        angle = (t - start).astype(F32) * freq[0:1, :]
+        angle = (t - start).astype(F32) * freq
         cos_t[pl.ds(r, BLOCK), :] = jnp.cos(angle)
         sine = jnp.sin(angle)
         sin_t[pl.ds(r, BLOCK), :] = jnp.where(low_half, -sine, sine)
@@ -294,6 +328,27 @@
     def _():
         halo_to_prev().wait_send()
 
+    own_cot.wait()
+
+    def mask_rows(b, carry):
+        rows = pl.ds(pl.multiple_of(b * BLOCK, BLOCK), BLOCK)
+        keep = jnp.where(masked[pl.ds(place * NB + b, 1), :] == 1, 1.0, 0.0).astype(F32)
+        keep = jnp.broadcast_to(keep, (BLOCK, BLOCK)).T.astype(BF16)
+        cot[rows, :] = cot[rows, :] * jnp.concatenate([keep] * (D // BLOCK), axis=1)
+        return carry
+
+    lax.fori_loop(0, NB, mask_rows, 0)
+
+    def transposed(dst, src, row0):
+        def body(i, carry):
+            at = pl.multiple_of(i * 128, 128)
+            dst[pl.ds(at, 128), :] = src[row0:row0 + R, pl.ds(at, 128)].astype(F32).T.astype(BF16)
+            return carry
+
+        lax.fori_loop(0, D // 128, body, 0)
+
+    transposed(s["ct"], cot, 0)
+
     a_ready = z.CA - 1 + stages - 1
     for t in range(a_ready + 1):
         gather_step(t)
@@ -309,8 +364,6 @@
 
     def part(lo, up, nn, i):
         return jnp.concatenate([shard_pair(c, nn, i) for c in range(lo, up)], axis=1)
-
-    QN, FN = z.QN, z.FN
 
     def unpack_a(i, carry):
         r = pl.multiple_of(i * 2 * SH, 16)
@@ -345,14 +398,16 @@
         return jnp.where(lax.rem(lanes, HEAD_DIM) < HEAD_DIM // 2, pltpu.roll(x, 128 - HEAD_DIM // 2, 1), pltpu.roll(x, HEAD_DIM // 2, 1))
 
     def project_turned(ct, carry):
-        at = pl.multiple_of(ct * 128, 128)
-        y = dot(n1[...], wqkv[:, pl.ds(at, 128)], 1, 0)
-        y = y * cos_t[...] + partner_lanes(y) * sin_t[...]
-        y = y * jnp.where(ct < D // 128, F32(1.0 / math.sqrt(HEAD_DIM)), F32(1.0))
-        qkv[:, pl.ds(at, 128)] = y.astype(BF16)
-        return carry
-
-    lax.fori_loop(0, 2 * D // 128, project_turned, 0)
+        at = pl.multiple_of(ct * 256, 128)
+        y = dot(n1[...], wqkv[:, pl.ds(at, 256)], 1, 0)
+        scale = jnp.where(ct < D // 256, F32(1.0 / math.sqrt(HEAD_DIM)), F32(1.0))
+        for k in range(2):
+            part_y = y[:, k * 128:(k + 1) * 128]
+            part_y = (part_y * cos_t[...] + partner_lanes(part_y) * sin_t[...]) * scale
+            qkv[:, pl.ds(pl.multiple_of(at + k * 128, 128), 128)] = part_y.astype(BF16)
+        return carry
+
+    lax.fori_loop(0, 2 * D // 256, project_turned, 0)
 
     def project(ct, carry):
         at = pl.multiple_of(2 * D + ct * 256, 128)
@@ -384,19 +439,24 @@
         pen = bias_t[b]
         return qs, kp, vp, dot(kp, qs, 1, 1) + jnp.concatenate([pen, pen], axis=1)
 
-    def attend(u, carry):
-        j, b = lax.div(u, NB), lax.rem(u, NB)
-        _, _, vp, scores = unit_scores(j, b)
-        top = jnp.max(scores, axis=0, keepdims=True)
-        weights = jnp.exp(scores - top)
-        inv = 1.0 / jnp.sum(weights, axis=0, keepdims=True)
-        stat[u, 0:1, :] = top
-        stat[u, 1:2, :] = inv
-        got = unstacked(dot(vp, (weights * inv).astype(BF16), 0, 0))
-        att[pl.ds(pl.multiple_of(b * BLOCK, BLOCK), BLOCK), pl.ds(pl.multiple_of(j * 128, 128), 128)] = got.astype(BF16)
-        return carry
-
-    lax.fori_loop(0, z.pairs * NB, attend, 0)
+    G = z.G
+
+    def attend(v, carry):
+        j, g = lax.div(v, NB // G), lax.rem(v, NB // G)
+        for i in range(G):
+            b = g * G + i
+            u = j * NB + b
+            _, _, vp, scores = unit_scores(j, b)
+            top = jnp.max(scores, axis=0, keepdims=True)
+            weights = jnp.exp(scores - top)
+            inv = 1.0 / jnp.sum(weights, axis=0, keepdims=True)
+            stat[u, 0:1, :] = top
+            stat[u, 1:2, :] = inv
+            got = unstacked(dot(vp, (weights * inv).astype(BF16), 0, 0))
+            att[pl.ds(pl.multiple_of(b * BLOCK, BLOCK), BLOCK), pl.ds(pl.multiple_of(j * 128, 128), 128)] = got.astype(BF16)
+        return carry
+
+    lax.fori_loop(0, z.pairs * (NB // G), attend, 0)
     for t in range(a_ready + 2, C + stages - 1):
         gather_step(t)
 
@@ -422,19 +482,57 @@
         eg = e * gain
         return rstd * (eg - jnp.mean(eg, axis=-1, keepdims=True) - hat * jnp.mean(eg * hat, axis=-1, keepdims=True))
 
-    def token_copies(stage, dest, rb, key):
-        src = stage.at[pl.ds(pl.multiple_of(rb * MB, 16), MB)]
-        dst = dest.at[pl.ds(pl.multiple_of(place * R + rb * MB, 16), MB)]
-        local = pltpu.make_async_copy(src, dst, s[key + "l"].at[rb])
-        remote = [copy_to(src, dst, s[key + "s"].at[rb, k - 1], s[key + "r"].at[rb, k - 1], (w, around(k))) for k in range(1, N)]
-        return local, remote
-
-    def token_arrivals(dest, rb, key):
-        for k in range(1, N):
-            source = around(-k)
-            theirs = source + core * (N - 1 - 2 * source)
-            ref = dest.at[pl.ds(pl.multiple_of(theirs * R + rb * MB, 16), MB)]
-            arrived(ref, s[key + "s"].at[rb, k - 1], s[key + "r"].at[rb, k - 1], (w, source))
+    def line_rows(dest, m, rb):
+        theirs = m + core * (N - 1 - 2 * m)
+        return dest.at[pl.ds(pl.multiple_of(theirs * R + rb * MB, 16), MB)]
+
+    def behind(side):
+        return n if side == 0 else N - 1 - n
+
+    def line_copy(dest, rb, key, side, k, stage=None):
+        step = 1 - 2 * side
+        ref = line_rows(dest, n - step * k, rb)
+        src = ref if stage is None else stage.at[pl.ds(pl.multiple_of(rb * MB, 16), MB)]
+        return copy_to(src, ref, s[key + "s"].at[rb, side, k], s[key + "r"].at[rb, side, k], (w, n + step))
+
+    def own_copy(stage, dest, rb, key):
+        return pltpu.make_async_copy(stage.at[pl.ds(pl.multiple_of(rb * MB, 16), MB)], line_rows(dest, n, rb), s[key + "l"].at[rb])
+
+    def token_send(stage, dest, rb, key):
+        own_copy(stage, dest, rb, key).start()
+        for side in range(2):
+            @pl.when(behind(side) < N - 1)
+            def _():
+                line_copy(dest, rb, key, side, 0, stage).start()
+
+    def token_forward(dest, key, k):
+        def body(rb, carry):
+            for side in range(2):
+                step = 1 - 2 * side
+
+                @pl.when(behind(side) >= k)
+                def _():
+                    arrived(line_rows(dest, n - step * k, rb), s[key + "s"].at[rb, side, k - 1], s[key + "r"].at[rb, side, k - 1], (w, n - step))
+
+                if k < N - 1:
+                    @pl.when(jnp.logical_and(behind(side) >= k, behind(side) < N - 1))
+                    def _():
+                        line_copy(dest, rb, key, side, k).start()
+            return carry
+
+        lax.fori_loop(0, z.blocks, body, 0)
+
+    def token_end(stage, dest, key):
+        def body(rb, carry):
+            own_copy(stage, dest, rb, key).wait()
+            for side in range(2):
+                for k in range(N - 1):
+                    @pl.when(jnp.logical_and(behind(side) >= k, behind(side) < N - 1))
+                    def _():
+                        line_copy(dest, rb, key, side, k).wait_send()
+            return carry
+
+        lax.fori_loop(0, z.blocks, body, 0)
 
     def feed(rb, carry):
         r = pl.multiple_of(rb * MB, 16)
@@ -466,10 +564,7 @@
             more = dot(dgv, wg[:, f:f + FC], 1, 1) + dot(duv, wu[:, f:f + FC], 1, 1)
             e = more if e is None else e + more
         ost[rows, :] = total_out.astype(BF16)
-        local, remote = token_copies(ost, out, rb, "o")
-        local.start()
-        for c in remote:
-            c.start()
+        token_send(ost, out, rb, "o")
         gsum[1:2, :] = gsum[1:2, :] + jnp.sum(e * hat, axis=0, keepdims=True)
         grad = cotv.astype(F32) + norm_back(hat, rstd, e, gain)
         resg[rows, :] = grad
@@ -521,16 +616,7 @@
             store_part(list(range(z.CA, C)), nn, t, jnp.concatenate(pieces, axis=1))
         return carry
 
-    def transposed(dst, src, row0):
-        def body(i, carry):
-            at = pl.multiple_of(i * 128, 128)
-            dst[pl.ds(at, 128), :] = src[row0:row0 + R, pl.ds(at, 128)].astype(F32).T.astype(BF16)
-            return carry
-
-        lax.fori_loop(0, D // 128, body, 0)
-
     transposed(s["n2t"], n2, 0)
-    transposed(s["ct"], cot, 0)
     transposed(s["rt"], res, 0)
     lax.fori_loop(0, D // TM, grads_b, 0)
 
@@ -570,63 +656,98 @@
                     at = h * N2 + nn
                     wb[c][at, hv, core] = (wb[c][at, hv, core].astype(F32) + r1[c][h, slot, nn].astype(F32)).astype(BF16)
 
-    def rz_start(c):
-        for k in range(1, N):
-            send(wb[c].at[around(k), hi, core], rz[c].at[k - 1], s["g2s"].at[c, k - 1], s["g2r"].at[c, k - 1], (w, around(k)))
+    def rz_copy(c, side, d):
+        step = 1 - 2 * side
+        return copy_to(wb[c].at[n + step * (1 + d), hi, core], rz[c].at[side, d], s["g2s"].at[c, side, d], s["g2r"].at[c, side, d], (w, n + step))
+
+    def rz_round(c, r):
+        for side in range(2):
+            step = 1 - 2 * side
+
+            @pl.when(behind(side) == r)
+            def _():
+                if r > 0:
+                    for d in range(N - r):
+                        arrived(rz[c].at[side, d], s["g2s"].at[c, side, d], s["g2r"].at[c, side, d], (w, n - step))
+                    for d in range(1, N - r):
+                        m = n + step * d
+                        wb[c][m, hi, core] = (wb[c][m, hi, core].astype(F32) + rz[c][side, d].astype(F32)).astype(BF16)
+                for d in range(N - 1 - r):
+                    rz_copy(c, side, d).start()
+
+    def rz_sent(c):
+        for side in range(2):
+            for r in range(N - 1):
+                @pl.when(behind(side) == r)
+                def _():
+                    for d in range(N - 1 - r):
+                        rz_copy(c, side, d).wait_send()
 
     def rz_finish(c):
-        total_g = wb[c][n, hi, core].astype(F32)
-        for k in range(1, N):
-            arrived(rz[c].at[k - 1], s["g2s"].at[c, k - 1], s["g2r"].at[c, k - 1], (w, around(-k)))
-            total_g = total_g + rz[c][k - 1].astype(F32)
         lo, up = z.cuts[c]
-        gp[:, lo:up] = total_g
+        gp[:, lo:up] = wb[c][n, hi, core].astype(F32)
+        for side in range(2):
+            @pl.when(behind(side) > 0)
+            def _():
+                gp[:, lo:up] = gp[:, lo:up] + rz[c][side, 0].astype(F32)
+
+    last_stage = z.bits + 1 + N
 
     def scatter_advance(chunks, st):
         for c in chunks:
             if st == 0:
                 r0_start(c)
-            elif st == 1:
-                r0_finish(c)
-                if z.bits:
-                    r1_start(c, 0)
+            elif st <= z.bits + 1:
+                if st == 1:
+                    r0_finish(c)
                 else:
-                    rz_start(c)
-            elif st <= z.bits + 1:
-                r1_finish(c, st - 2)
-                if st - 1 < z.bits:
+                    r1_finish(c, st - 2)
+                if st <= z.bits:
                     r1_start(c, st - 1)
                 else:
-                    rz_start(c)
+                    rz_round(c, 0)
             else:
-                rz_finish(c)
+                rz_round(c, st - z.bits - 1)
+                if st == last_stage - 1:
+                    rz_finish(c)
 
     part_a, part_b = list(range(z.CA)), list(range(z.CA, C))
     scatter_advance(part_b, 0)
+    token_forward(out, "o", 1)
 
     dkv, edge, rim, rimr = s["dkv"], s["edge"], s["rim"], s["rimr"]
     dk_ref, dv_ref = dkv.at[0], dkv.at[1]
 
     def attend_back(j, carry):
-        dkv[...] = jnp.zeros((2, E, 128), F32)
-
-        def one(b, inner):
-            u = j * NB + b
-            (lq, lk, lv), keys, queries = unit_refs(j, b)
-            qs, kp, vp, scores = unit_scores(j, b)
-            probs = jnp.exp(scores - stat[u, 0:1, :]) * stat[u, 1:2, :]
-            gs = stacked(datt[pl.ds(pl.multiple_of(b * BLOCK, BLOCK), BLOCK), pl.ds(pl.multiple_of(j * 128, 128), 128)])
-            prob_grad = dot(vp, gs, 1, 1)
-            row_dot = jnp.sum(probs * prob_grad, axis=0, keepdims=True)
-            score_grad = (probs * (prob_grad - row_dot)).astype(BF16)
-            dv_ref[keys, :] = dv_ref[keys, :] + dot(probs.astype(BF16), gs, 1, 0)
-            dk_ref[keys, :] = dk_ref[keys, :] + dot(score_grad, qs, 1, 0)
-            dq = unstacked(dot(kp, score_grad, 0, 0)) * F32(1.0 / math.sqrt(HEAD_DIM))
-            dq = dq * cos_t[queries, :] - partner_lanes(dq) * sin_t[queries, :]
-            qkv[queries, lq] = dq.astype(BF16)
+        dkv[:, 0:BLOCK, :] = jnp.zeros((2, BLOCK, 128), F32)
+
+        def group(g, inner):
+            tails = None
+            for i in range(G):
+                b = g * G + i
+                u = j * NB + b
+                (lq, lk, lv), keys, queries = unit_refs(j, b)
+                qs, kp, vp, scores = unit_scores(j, b)
+                probs = jnp.exp(scores - stat[u, 0:1, :]) * stat[u, 1:2, :]
+                gs = stacked(datt[pl.ds(pl.multiple_of(b * BLOCK, BLOCK), BLOCK), pl.ds(pl.multiple_of(j * 128, 128), 128)])
+                prob_grad = dot(vp, gs, 1, 1)
+                row_dot = jnp.sum(probs * prob_grad, axis=0, keepdims=True)
+                score_grad = (probs * (prob_grad - row_dot)).astype(BF16)
+                parts = (dot(score_grad, qs, 1, 0), dot(probs.astype(BF16), gs, 1, 0))
+                dq = unstacked(dot(kp, score_grad, 0, 0)) * F32(1.0 / math.sqrt(HEAD_DIM))
+                dq = dq * cos_t[queries, :] - partner_lanes(dq) * sin_t[queries, :]
+                qkv[queries, lq] = dq.astype(BF16)
+                here = pl.ds(pl.multiple_of(b * BLOCK, BLOCK), BLOCK)
+                for k in range(2):
+                    before = dkv[k, here, :] if tails is None else tails[k]
+                    dkv[k, here, :] = before + parts[k][:BLOCK]
+                tails = [x[BLOCK:] for x in parts]
+            after = pl.ds(pl.multiple_of(g * G * BLOCK + G * BLOCK, BLOCK), BLOCK)
+            for k in range(2):
+                dkv[k, after, :] = tails[k]
             return inner
 
-        lax.fori_loop(0, NB, one, 0)
+        lax.fori_loop(0, NB // G, group, 0)
         (_, lk, lv), _, _ = unit_refs(j, 0)
         lj = pl.ds(pl.multiple_of(j * 128, 128), 128)
         for k, ref in enumerate((dk_ref, dv_ref)):
@@ -644,6 +765,8 @@
     half_pairs = z.pairs // 2
     lax.fori_loop(0, half_pairs, attend_back, 0)
     scatter_advance(part_b, 1)
+    if N > 2:
+        token_forward(out, "o", 2)
     lax.fori_loop(half_pairs, z.pairs, attend_back, 0)
 
     def rim_to_prev():
@@ -668,6 +791,8 @@
     def _():
         rimr[1] = jnp.zeros((HALF, 2 * D), BF16)
 
+    for k in range(3, N):
+        token_forward(out, "o", k)
     for st in range(2, z.bits + 2):
         scatter_advance(part_b, st)
 
@@ -707,10 +832,7 @@
         hat, rstd = normed(xin[ext, :].astype(F32))
         gsum[0:1, :] = gsum[0:1, :] + jnp.sum(e * hat, axis=0, keepdims=True)
         tst[rows, :] = (resg[rows, :] + norm_back(hat, rstd, e, grow[0:1, :])).astype(BF16)
-        local, remote = token_copies(tst, tg, rb, "t")
-        local.start()
-        for c in remote:
-            c.start()
+        token_send(tst, tg, rb, "t")
         return carry
 
     lax.fori_loop(0, z.blocks, input_grad, 0)
@@ -731,28 +853,26 @@
 
     lax.fori_loop(0, D // TM, grads_a, 0)
     scatter_advance(part_a, 0)
-    scatter_advance(part_b, z.bits + 2)
-    for st in range(1, z.bits + 3):
+    for st in range(z.bits + 2, last_stage):
+        scatter_advance(part_b, st)
+    for st in range(1, z.bits + 1):
         scatter_advance(part_a, st)
-
-    def token_end(stage, dest, key):
-        def body(rb, carry):
-            local, remote = token_copies(stage, dest, rb, key)
-            local.wait()
-            for c in remote:
-                c.wait_send()
-            token_arrivals(dest, rb, key)
-            return carry
-
-        lax.fori_loop(0, z.blocks, body, 0)
+    token_forward(tg, "t", 1)
+    scatter_advance(part_a, z.bits + 1)
+    for k in range(2, N):
+        token_forward(tg, "t", k)
+    for st in range(z.bits + 2, last_stage):
+        scatter_advance(part_a, st)
 
     for c in pending:
         c.wait_send()
+    for c in range(C):
+        rz_sent(c)
     token_end(ost, out, "o")
     token_end(tst, tg, "t")
 
 
-def run_layer(z, lengths, tokens, cot, freq, pk):
+def run_layer(z, *args):
     shapes, names = [], []
 
     def vmem(name, shape, dtype):
@@ -768,7 +888,7 @@
         vmem(f"wb{c}", (N, W // 2, 2, z.RS, up - lo), BF16)
         vmem(f"r0{c}", (N, W // 2, z.RS, up - lo), BF16)
         vmem(f"r1{c}", (2, W // 2 - 1, N // 2, z.RS, up - lo), BF16)
-        vmem(f"rz{c}", (N - 1, z.RS, up - lo), BF16)
+        vmem(f"rz{c}", (2, N - 1, z.RS, up - lo), BF16)
     vmem("xin", (E, D), BF16)
     vmem("n1", (E, D), BF16)
     vmem("qkv", (E, 3 * D), BF16)
@@ -784,7 +904,8 @@
     vmem("sin", (E, 128), F32)
     vmem("bias", (z.NB, SPAN, BLOCK), F32)
     vmem("stat", (z.pairs * z.NB, 8, 2 * BLOCK), F32)
-    for name in ("att", "ost", "n2", "resr", "datt"):
+    vmem("pk", (z.RS, z.lanes), BF16)
+    for name in ("att", "ost", "n2", "resr", "datt", "cot"):
         vmem(name, (R, D), BF16)
     for name in ("n2t", "ct", "rt"):
         vmem(name, (D, R), BF16)
@@ -796,9 +917,11 @@
     vmem("rim", (2, HALF, 2 * D), BF16)
     vmem("rimr", (2, HALF, 2 * D), BF16)
     sems("l_own", C)
-    sems("l_tok", 3)
-    for name in ("zs", "zr", "g2s", "g2r"):
+    sems("l_tok", 4)
+    for name in ("zs", "zr"):
         sems(name, C, N - 1)
+    for name in ("g2s", "g2r"):
+        sems(name, C, 2, N - 1)
     for name in ("ss", "sr", "g1s", "g1r"):
         sems(name, C, 2, W // 2 - 1)
     for name in ("ds", "dr"):
@@ -810,7 +933,7 @@
     for name in ("ol", "tl"):
         sems(name, z.blocks)
     for name in ("os", "or", "ts", "tr"):
-        sems(name, z.blocks, N - 1)
+        sems(name, z.blocks, 2, N - 1)
     hbm = pl.BlockSpec(memory_space=pl.ANY)
     vm = pl.BlockSpec(memory_space=pltpu.VMEM)
     return pl.pallas_call(
@@ -820,51 +943,108 @@
             jax.ShapeDtypeStruct((z.T, D), BF16),
             jax.ShapeDtypeStruct((z.RS, z.lanes), F32),
         ),
-        in_specs=[pl.BlockSpec(memory_space=pltpu.SMEM), hbm, vm, vm, vm],
+        in_specs=[pl.BlockSpec(memory_space=pltpu.SMEM), hbm, hbm] + [vm] * 6,
         out_specs=(hbm, hbm, vm),
         scratch_shapes=shapes,
         compiler_params=pltpu.CompilerParams(collective_id=0, has_side_effects=True, vmem_limit_bytes=VMEM_BYTES),
-    )(lengths, tokens, cot, freq, pk)
+    )(*args)
 
 
 VMEM_BYTES = 64 * 1024 * 1024 - 1024 * 64
+
+
+def finish_kernel(z, tg, out, gp, o_out, o_tg, o_in, o_ow, o_gu, o_dn, o_gains, low, full, s_in, s_out, s_copy):
+    rows = low.shape[1]
+    steps = z.T // rows
+    whole = pltpu.make_async_copy(out, o_out, s_copy)
+    whole.start()
+
+    def load(i):
+        return pltpu.make_async_copy(tg.at[pl.ds(i * rows, rows)], low.at[i % 2], s_in.at[i % 2])
+
+    def store(i):
+        return pltpu.make_async_copy(full.at[i % 2], o_tg.at[pl.ds(i * rows, rows)], s_out.at[i % 2])
+
+    load(0).start()
+    for i in range(steps):
+        if i + 1 < steps:
+            load(i + 1).start()
+        load(i).wait()
+        if i >= 2:
+            store(i - 2).wait()
+        full[i % 2] = low[i % 2].astype(F32)
+        store(i).start()
+        if i == 0:
+            unpack_grads(z, gp, o_in, o_ow, o_gu, o_dn, o_gains)
+    for i in range(max(0, steps - 2), steps):
+        store(i).wait()
+    whole.wait()
+
+
+def unpack_grads(z, gp, o_in, o_ow, o_gu, o_dn, o_gains):
+    SH, QN, FN = z.SH, z.QN, z.FN
+    heads = QN // HEAD_DIM
+    value = gp[...][:SH]
+
+    def flipped(x):
+        a, b = x.shape
+        a2, b2 = round_up(a, 128), round_up(b, 128)
+        if b2 > b:
+            x = jnp.concatenate([x, jnp.zeros((a, b2 - b), F32)], axis=1)
+        if a2 > a:
+            x = jnp.concatenate([x, jnp.zeros((a2 - a, b2), F32)], axis=0)
+        return x.T[:b, :a]
+
+    at = GAIN_LANES
+    o_in[...] = jnp.concatenate(
+        [value[:, at + k * QN + a * HEAD_DIM:at + k * QN + (a + 1) * HEAD_DIM] for a in range(heads) for k in range(3)], axis=1)
+    at += 3 * QN
+    o_ow[...] = flipped(value[:, at:at + QN])
+    at += QN
+    for k in range(2):
+        o_gu[:, k, :] = value[:, at + k * FN:at + (k + 1) * FN]
+    at += 2 * FN
+    o_dn[...] = flipped(value[:, at:at + FN])
+    o_gains[...] = flipped(value[:, :128])[0:8, :]
+
+
+def finish(z, tg, out, gp):
+    rows = 256
+    hbm = pl.BlockSpec(memory_space=pl.ANY)
+    vm = pl.BlockSpec(memory_space=pltpu.VMEM)
+    return pl.pallas_call(
+        functools.partial(finish_kernel, z),
+        out_shape=(
+            jax.ShapeDtypeStruct((z.T, z.D), BF16),
+            jax.ShapeDtypeStruct((z.T, z.D), F32),
+            jax.ShapeDtypeStruct((z.SH, 3 * z.QN), F32),
+            jax.ShapeDtypeStruct((z.QN, z.SH), F32),
+            jax.ShapeDtypeStruct((z.SH, 2, z.FN), F32),
+            jax.ShapeDtypeStruct((z.FN, z.SH), F32),
+            jax.ShapeDtypeStruct((8, z.SH), F32),
+        ),
+        in_specs=[hbm, hbm, vm],
+        out_specs=(hbm, hbm, vm, vm, vm, vm, vm),
+        scratch_shapes=[
+            pltpu.VMEM((2, rows, z.D), BF16),
+            pltpu.VMEM((2, rows, z.D), F32),
+            pltpu.SemaphoreType.DMA((2,)),
+            pltpu.SemaphoreType.DMA((2,)),
+            pltpu.SemaphoreType.DMA,
+        ],
+        compiler_params=pltpu.CompilerParams(vmem_limit_bytes=32 * 1024 * 1024),
+    )(tg, out, gp)
 
 
 def per_device(tokens, lengths, masked, attention_in, attention_out, geglu_in, geglu_out, gain_attention, gain_feedforward, out_grad):
     wide, narrow = lax.axis_size("wide"), lax.axis_size("narrow")
-    w, n = lax.axis_index("wide"), lax.axis_index("narrow")
     z = Sizes(wide, narrow, tokens.shape[0], tokens.shape[1], attention_out.shape[0] * narrow, geglu_out.shape[0] * narrow, lengths.shape[0])
-    place = jnp.where(lax.rem(w, 2) == 0, n, narrow - 1 - n)
-    cot = lax.dynamic_slice_in_dim(out_grad, place * z.R, z.R, 0)
-    mask = lax.dynamic_slice_in_dim(masked, place * z.R, z.R, 0)
-    cot = jnp.where((mask == 1)[:, None], cot, jnp.zeros((), BF16))
-    heads = z.QN // HEAD_DIM
-    w_in = attention_in.astype(BF16).reshape(z.SH, heads, 3, HEAD_DIM)
-    gains = jnp.stack([gain_attention, gain_feedforward], axis=1).astype(BF16)
-    pk = jnp.concatenate(
-        [jnp.pad(gains, ((0, 0), (0, GAIN_LANES - 2)))]
-        + [w_in[:, :, k].reshape(z.SH, z.QN) for k in range(3)]
-        + [attention_out.astype(BF16).T, geglu_in[:, 0].astype(BF16), geglu_in[:, 1].astype(BF16), geglu_out.astype(BF16).T],
-        axis=1,
-    )
-    pk = jnp.pad(pk, ((0, z.RS - z.SH), (0, z.lanes - z.real)))
-    j = np.arange(128) % (HEAD_DIM // 2)
-    freq = jnp.asarray(np.broadcast_to((THETA ** (-2.0 * j / HEAD_DIM)).astype(np.float32)[None], (8, 128)))
-    out, tg, gp = run_layer(z, lengths, tokens, cot, freq, pk)
-    gp = gp[: z.SH]
-    at = GAIN_LANES
-
-    def take(count):
-        nonlocal at
-        value = gp[:, at:at + count]
-        at += count
-        return value
-
-    in_grad = jnp.stack([take(z.QN).reshape(z.SH, heads, HEAD_DIM) for _ in range(3)], axis=2).reshape(z.SH, 3 * z.QN)
-    out_w_grad = take(z.QN).T
-    gate_up = jnp.stack([take(z.FN), take(z.FN)], axis=1)
-    down = take(z.FN).T
-    return (out, tg.astype(F32), in_grad, out_w_grad, gate_up, down, gp[:, 0], gp[:, 1])
+    gate_up = geglu_in.astype(BF16).reshape(z.SH, 2 * z.FN)
+    gains = jnp.stack([gain_attention, gain_feedforward])
+    out, tg, gp = run_layer(
+        z, lengths, tokens, out_grad, masked.reshape(-1, 128), attention_in, attention_out, gate_up, geglu_out, gains)
+    out, tg, g_in, g_out, g_gu, g_down, g_gains = finish(z, tg, out, gp)
+    return (out, tg, g_in, g_out, g_gu, g_down, g_gains[0], g_gains[1])
 
 
 def solution(mesh):

time: 275 us -> 213 us (0.77)
  the two profiles are of different devices: /device:TPU:24 before, /device:TPU:0 now
where the time goes in v3:
time: 213 us
  Pallas kernels  204 us (96%)
  local copies, waits for them, and re-layouts  6.17 us (3%)
  other arithmetic  2.31 us (1%)
    pallas_call x1, Pallas kernels, run_layer(): pl.pallas_call(functools.partial(layer_kernel, z, names), out_shape=(jax....  198 us
    pallas_call x1, Pallas kernels, finish(): pl.pallas_call(functools.partial(finish_kernel, z), out_shape=(jax.ShapeD...  5.88 us
    unnamed x6, local copies, waits for them, and re-layouts  4.85 us

profile of v3, /device:TPU:0, one launch (start us, length us, event | category | flops | bytes accessed | tf_op | source)
XLA Modules:
  0.0 212.8 jit_solution(8494337707553444919)
XLA Ops:
  0.6 1.2 pad_maximum_fusion.gains
  1.9 1.1 convert_element_type.3
  2.9 0.8 reshape.23.w_gu
  3.7 197.8 %shard_map.161 = (bf16[2048,768]{1,0:T(8,128)(2,1)}, bf16[2048,768]{1,0:T(8,128)(2,1)}, f32[96,1664]{1,0:T(8,128)}) custom-call(s32[8]{0:T(128)} %lengths.1, bf16[2048,768]{1,0:T(8,128)(2,1)} %tokens.1, bf16[2048,768]{1,0:T(8,128)(2,1)} %grads_in.1, s32[16,128]{1,0:T(8,128)} %bitcast.7, f32[96,576]{1,0:T(8,128)} %w_in.1, f32[192,96]{1,0:T(8,128)} %w_out.1, ...), custom_call_target="tpu_custom_call" | custom-call | tf_op jit(solution)/shard_map/pallas_call | solution.py:939
  201.6 0.0 copy-start
  201.6 1.9 copy-done
  203.4 0.0 copy-start.1
  203.4 1.9 copy-done.1
  205.3 0.0 copy-start.2
  205.3 1.1 copy-done.2
  206.4 5.9 %shard_map.162 = (bf16[2048,768]{1,0:T(8,128)(2,1)}, f32[2048,768]{1,0:T(8,128)}, f32[96,576]{1,0:T(8,128)}, f32[192,96]{1,0:T(8,128)}, f32[96,2,288]{2,1,0:T(2,...) custom-call(bf16[2048,768]{1,0:T(8,128)(2,1)S(1)} %copy-done.1, bf16[2048,768]{1,0:T(8,128)(2,1)S(1)} %copy-done, ...), custom_call_target="tpu_custom_call" | custom-call | tf_op jit(solution)/shard_map/pallas_call | solution.py:1015
  212.3 0.5 slice_bitcast_fusion
Async XLA Ops:
  201.6 1.9 copy-start
  203.4 1.9 copy-start.1
  205.3 1.1 copy-start.2

commit v4 on v3

--- a/solution.py
+++ b/solution.py
@@ -14,6 +14,7 @@
 WINDOW = 128
 HALF = WINDOW // 2
 BLOCK = 128
+FINISH_ROWS = 256
 SPAN = BLOCK + WINDOW
 GAIN_LANES = 32
 EPSILON = 1e-05
@@ -69,7 +70,7 @@
     return out
 
 
-def layer_kernel(z, names, lengths, tokens, grads_in, masked, w_in, w_out, w_gu, w_down, gains, out, tg, gp, *scratch):
+def layer_kernel(z, names, lengths, tokens, grads_in, masked, w_in, w_out, w_gu, w_down, gain_one, gain_two, out, tg, gp, *scratch):
     s = dict(zip(names, scratch))
     W, N, T, D, F, R, E, NB = z.W, z.N, z.T, z.D, z.F, z.R, z.E, z.NB
     C, SH, RS, N2 = z.C, z.SH, z.RS, z.N // 2
@@ -87,6 +88,9 @@
     has_next = jnp.logical_or(place < N - 1, w < W - 1)
     prev_dev = (jnp.where(first, w - 1, w), jnp.where(first, n, n - ahead))
     next_dev = (jnp.where(last, w + 1, w), jnp.where(last, n, n + ahead))
+    at_end = jnp.logical_or(first, last)
+    low_block = jnp.logical_and(at_end, w > 0)
+    high_block = jnp.logical_and(at_end, w < W - 1)
     sib_dev = (w + 1 - 2 * core, n)
 
     def around(k):
@@ -118,74 +122,14 @@
     for dev in partners:
         pl.semaphore_signal(barrier, inc=1, device_id=dev, device_id_type=MESH)
 
-    @pl.when(has_prev)
-    def _():
-        pl.semaphore_signal(barrier, inc=1, device_id=prev_dev, device_id_type=MESH)
-
-    @pl.when(has_next)
-    def _():
-        pl.semaphore_signal(barrier, inc=1, device_id=next_dev, device_id_type=MESH)
-
-    pl.semaphore_wait(barrier, len(partners) + has_prev.astype(jnp.int32) + has_next.astype(jnp.int32))
-
-    half_refs = [pl.ds(h * N2, N2) for h in range(2)]
-    gather_order = [list(range(z.bits))[::-1], list(range(z.bits))]
-
-    def z_start(c):
-        lo, up = z.cuts[c]
-        src = pk.at[:, lo:up]
-        pltpu.make_async_copy(src, wb[c].at[n, hi, core], s["l_own"].at[c]).start()
-        for k in range(1, N):
-            send(src, wb[c].at[n, hi, core], s["zs"].at[c, k - 1], s["zr"].at[c, k - 1], (w, around(k)))
-
-    def z_wait(c):
-        lo, up = z.cuts[c]
-        pltpu.make_async_copy(pk.at[:, lo:up], wb[c].at[n, hi, core], s["l_own"].at[c]).wait()
-        for k in range(1, N):
-            arrived(wb[c].at[around(-k), hi, core], s["zs"].at[c, k - 1], s["zr"].at[c, k - 1], (w, around(-k)))
-
-    def s_start(c, t):
-        for h in range(2):
-            b = gather_order[h][t]
-            for i, combo in enumerate(combos(gather_order[h][:t])):
-                ref = wb[c].at[half_refs[h], flip(hi, combo), core]
-                slot = (1 << t) - 1 + i
-                send(ref, ref, s["ss"].at[c, h, slot], s["sr"].at[c, h, slot], bit_dev(b))
-
-    def s_wait(c, t):
-        for h in range(2):
-            b = gather_order[h][t]
-            for i, combo in enumerate(combos(gather_order[h][:t])):
-                ref = wb[c].at[half_refs[h], flip(hi, combo + [b]), core]
-                slot = (1 << t) - 1 + i
-                arrived(ref, s["ss"].at[c, h, slot], s["sr"].at[c, h, slot], bit_dev(b))
-
-    def d_start(c):
-        for h in range(2):
-            ref = wb[c].at[half_refs[h], :, core]
-            send(ref, ref, s["ds"].at[c, h], s["dr"].at[c, h], sib_dev)
-
-    def d_wait(c):
-        for h in range(2):
-            arrived(wb[c].at[half_refs[h], :, 1 - core], s["ds"].at[c, h], s["dr"].at[c, h], sib_dev)
-
-    stages = z.bits + 2
-
-    def gather_step(t):
-        for st in reversed(range(stages)):
-            c = t - st
-            if not 0 <= c < C:
-                continue
-            if st == 0:
-                z_wait(c)
-            elif st <= z.bits:
-                s_wait(c, st - 1)
-            else:
-                d_wait(c)
-            if st < z.bits:
-                s_start(c, st)
-            elif st == z.bits:
-                d_start(c)
+    @pl.when(low_block)
+    def _():
+        pl.semaphore_signal(barrier, inc=1, device_id=(w - 1, n), device_id_type=MESH)
+
+    @pl.when(high_block)
+    def _():
+        pl.semaphore_signal(barrier, inc=1, device_id=(w + 1, n), device_id_type=MESH)
+
 
     def flipped(x):
         a, b = x.shape
@@ -208,13 +152,85 @@
     QN, FN = z.QN, z.FN
     heads = QN // HEAD_DIM
     raw_in, out_t = w_in[...], flipped(w_out[...])
-    gain_cols = jnp.concatenate([flipped(gains[...]), jnp.zeros((SH, GAIN_LANES - 2), F32)], axis=1)
+    gain_rows = jnp.concatenate([gain_one[...], gain_two[...], jnp.zeros((6, SH), F32)], axis=0)
+    gain_cols = jnp.concatenate([flipped(gain_rows), jnp.zeros((SH, GAIN_LANES - 8), F32)], axis=1)
     pack(0, z.LA, [gain_cols] + [raw_in[:, (3 * a + k) * HEAD_DIM:(3 * a + k + 1) * HEAD_DIM] for k in range(3) for a in range(heads)] + [out_t[:, :z.O0]])
-    for c in range(z.CA):
-        z_start(c)
-    pack(z.LA, z.lanes, [out_t[:, z.O0:], w_gu[...].astype(F32), flipped(w_down[...])])
-    for c in range(z.CA, C):
-        z_start(c)
+    pl.semaphore_wait(barrier, len(partners) + low_block.astype(jnp.int32) + high_block.astype(jnp.int32))
+
+    half_refs = [pl.ds(h * N2, N2) for h in range(2)]
+    gather_order = [list(range(z.bits))[::-1], list(range(z.bits))]
+
+    def z_start(c):
+        lo, up = z.cuts[c]
+        src = pk.at[:, lo:up]
+        pltpu.make_async_copy(src, wb[c].at[n, hi, core], s["l_own"].at[c]).start()
+        for k in range(1, N):
+            send(src, wb[c].at[n, hi, core], s["zs"].at[c, k - 1], s["zr"].at[c, k - 1], (w, around(k)))
+
+    def z_wait(c):
+        lo, up = z.cuts[c]
+        pltpu.make_async_copy(pk.at[:, lo:up], wb[c].at[n, hi, core], s["l_own"].at[c]).wait()
+        for k in range(1, N):
+            arrived(wb[c].at[around(-k), hi, core], s["zs"].at[c, k - 1], s["zr"].at[c, k - 1], (w, around(-k)))
+
+    def s_start(c, t):
+        for h in range(2):
+            b = gather_order[h][t]
+            for i, combo in enumerate(combos(gather_order[h][:t])):
+                ref = wb[c].at[half_refs[h], flip(hi, combo), core]
+                slot = (1 << t) - 1 + i
+                send(ref, ref, s["ss"].at[c, h, slot], s["sr"].at[c, h, slot], bit_dev(b))
+
+    def s_wait(c, t):
+        for h in range(2):
+            b = gather_order[h][t]
+            for i, combo in enumerate(combos(gather_order[h][:t])):
+                ref = wb[c].at[half_refs[h], flip(hi, combo + [b]), core]
+                slot = (1 << t) - 1 + i
+                arrived(ref, s["ss"].at[c, h, slot], s["sr"].at[c, h, slot], bit_dev(b))
+
+    def d_start(c, late):
+        for h in range(2):
+            everyone = combos(gather_order[h])
+            for i, combo in enumerate(everyone):
+                if (i >= len(everyone) // 2) == late:
+                    ref = wb[c].at[half_refs[h], flip(hi, combo), core]
+                    send(ref, ref, s["ds"].at[c, h, i], s["dr"].at[c, h, i], sib_dev)
+
+    def d_wait(c):
+        for h in range(2):
+            for i, combo in enumerate(combos(gather_order[h])):
+                arrived(wb[c].at[half_refs[h], flip(hi, combo), 1 - core], s["ds"].at[c, h, i], s["dr"].at[c, h, i], sib_dev)
+
+    stages = z.bits + 2
+
+    def gather_event(c, st):
+        if st == 0:
+            z_wait(c)
+            if c + 1 < C:
+                z_start(c + 1)
+        elif st <= z.bits:
+            s_wait(c, st - 1)
+        else:
+            d_wait(c)
+        if st < z.bits:
+            s_start(c, st)
+        if st == z.bits - 1:
+            d_start(c, False)
+        if st == z.bits:
+            d_start(c, True)
+
+    steps = [[(t - st, st) for st in reversed(range(stages)) if 0 <= t - st < C] for t in range(C + stages - 1)]
+    a_step = z.CA - 1 + stages - 1
+    a_at = steps[a_step].index((z.CA - 1, stages - 1)) + 1
+
+    def gather_events(events):
+        for c, st in events:
+            gather_event(c, st)
+
+    z_start(0)
+    raw_gate, raw_up, raw_down = w_gu[:, 0, :], w_gu[:, 1, :], flipped(w_down[...])
+    pack(z.LA, z.lanes, [out_t[:, z.O0:]] + [raw_gate, raw_up, raw_down])
 
     xin = s["xin"]
     own = pltpu.make_async_copy(tokens.at[pl.ds(pl.multiple_of(place * R, 16), R)], xin.at[pl.ds(HALF, R)], s["l_tok"].at[0])
@@ -228,13 +244,13 @@
     def high_copy():
         return pltpu.make_async_copy(tokens.at[pl.ds(pl.multiple_of(place * R + R, 16), HALF)], xin.at[pl.ds(HALF + R, HALF)], s["l_tok"].at[2])
 
+    halo = s["halo"]
+
     def halo_to_next():
-        return copy_to(tokens.at[pl.ds(T - HALF, HALF)], xin.at[pl.ds(0, HALF)], s["hs"].at[0], s["hr"].at[0], (w + 1, n))
+        return copy_to(tokens.at[pl.ds(T - HALF, HALF)], halo.at[0], s["hs"].at[0], s["hr"].at[0], (w + 1, n))
 
     def halo_to_prev():
-        return copy_to(tokens.at[pl.ds(0, HALF)], xin.at[pl.ds(HALF + R, HALF)], s["hs"].at[1], s["hr"].at[1], (w - 1, n))
-
-    zeros_halo = jnp.zeros((HALF, D), BF16)
+        return copy_to(tokens.at[pl.ds(0, HALF)], halo.at[1], s["hs"].at[1], s["hr"].at[1], (w - 1, n))
 
     @pl.when(place > 0)
     def _():
@@ -244,23 +260,22 @@
     def _():
         high_copy().start()
 
-    @pl.when(jnp.logical_and(last, w < W - 1))
+    @pl.when(high_block)
     def _():
         halo_to_next().start()
 
-    @pl.when(jnp.logical_and(first, w > 0))
+    @pl.when(low_block)
     def _():
         halo_to_prev().start()
 
-    @pl.when(jnp.logical_and(first, w == 0))
-    def _():
-        xin[0:HALF, :] = zeros_halo
-
-    @pl.when(jnp.logical_and(last, w == W - 1))
-    def _():
-        xin[HALF + R:, :] = zeros_halo
-
-    base = w * T + place * R
+    @pl.when(w == 0)
+    def _():
+        halo[0] = jnp.zeros((HALF, D), BF16)
+
+    @pl.when(w == W - 1)
+    def _():
+        halo[1] = jnp.zeros((HALF, D), BF16)
+
     ends, total = [], jnp.int32(0)
     for d in range(z.docs):
         total = total + lengths[d]
@@ -274,7 +289,12 @@
     for d in range(HEAD_DIM // 2):
         freq = jnp.where(freq_lane == d, F32(THETA ** (-2.0 * d / HEAD_DIM)), freq)
 
-    def table_rows(i, carry):
+    def tables(spot):
+        base = w * T + spot * R
+        lax.fori_loop(0, E // BLOCK, functools.partial(table_rows, base), 0)
+        lax.fori_loop(0, NB, functools.partial(bias_rows, base), 0)
+
+    def table_rows(base, i, carry):
         r = pl.multiple_of(i * BLOCK, BLOCK)
         t = base - HALF + r + lax.broadcasted_iota(jnp.int32, (BLOCK, 128), 0)
         start = jnp.zeros((BLOCK, 128), jnp.int32)
@@ -286,9 +306,7 @@
         sin_t[pl.ds(r, BLOCK), :] = jnp.where(low_half, -sine, sine)
         return carry
 
-    lax.fori_loop(0, E // BLOCK, table_rows, 0)
-
-    def bias_rows(b, carry):
+    def bias_rows(base, b, carry):
         tk = base - HALF + b * BLOCK + lax.broadcasted_iota(jnp.int32, (SPAN, BLOCK), 0)
         tq = base + b * BLOCK + lax.broadcasted_iota(jnp.int32, (SPAN, BLOCK), 1)
         dk = jnp.where(tk < 0, -1, 0)
@@ -300,7 +318,9 @@
         bias_t[b] = jnp.where(jnp.logical_and(dk == dq, near), 0.0, NEG_LARGE).astype(F32)
         return carry
 
-    lax.fori_loop(0, NB, bias_rows, 0)
+    gather_events(steps[0])
+    tables(place)
+    gather_events(steps[1])
 
     own.wait()
 
@@ -312,22 +332,25 @@
     def _():
         high_copy().wait()
 
-    @pl.when(jnp.logical_and(first, w > 0))
+    @pl.when(low_block)
     def _():
         halo_to_next().wait_recv()
-
-    @pl.when(jnp.logical_and(last, w < W - 1))
+        halo_to_prev().wait_send()
+
+    @pl.when(high_block)
     def _():
         halo_to_prev().wait_recv()
-
-    @pl.when(jnp.logical_and(last, w < W - 1))
-    def _():
         halo_to_next().wait_send()
 
-    @pl.when(jnp.logical_and(first, w > 0))
-    def _():
-        halo_to_prev().wait_send()
-
+    @pl.when(first)
+    def _():
+        xin[0:HALF, :] = halo[0]
+
+    @pl.when(last)
+    def _():
+        xin[HALF + R:, :] = halo[1]
+
+    gather_events(steps[2])
     own_cot.wait()
 
     def mask_rows(b, carry):
@@ -349,29 +372,39 @@
 
     transposed(s["ct"], cot, 0)
 
-    a_ready = z.CA - 1 + stages - 1
-    for t in range(a_ready + 1):
-        gather_step(t)
+    for t in range(3, a_step):
+        gather_events(steps[t])
+    gather_events(steps[a_step][:a_at])
 
     wqkv, wot, wg, wu, wgo = s["wqkv"], s["wot"], s["wg"], s["wu"], s["wgo"]
     gcol, grow, gsum = s["gcol"], s["grow"], s["gsum"]
 
-    def shard_pair(c, nn, i):
-        a, b = wb[c][nn, i, 0], wb[c][nn, i, 1]
-        if SH % 16 == 0:
-            return jnp.concatenate([a[:SH], b[:SH]], axis=0)
-        return jnp.concatenate([a.astype(F32)[:SH], b.astype(F32)[:SH]], axis=0).astype(BF16)
-
-    def part(lo, up, nn, i):
-        return jnp.concatenate([shard_pair(c, nn, i) for c in range(lo, up)], axis=1)
+    def section(nn, i, lo, up):
+        found = []
+        for c, (a, b) in enumerate(z.cuts):
+            x, y = max(lo, a), min(up, b)
+            if x >= y:
+                continue
+            x0, y0 = (x - a) // 128 * 128, round_up(y - a, 128)
+            both = [wb[c][nn, i, k, :, x0:y0] for k in range(2)]
+            if SH % 16 == 0:
+                v = jnp.concatenate([q[:SH] for q in both], axis=0)
+            else:
+                v = jnp.concatenate([q.astype(F32)[:SH] for q in both], axis=0).astype(BF16)
+            found.append(v[:, x - a - x0:y - a - x0])
+        return found[0] if len(found) == 1 else jnp.concatenate(found, axis=1)
+
+    def place_columns(ref, r, at, sections):
+        width = sum(v.shape[1] for v in sections)
+        ref[pl.ds(r, 2 * SH), at:at + width] = jnp.concatenate(sections, axis=1)
 
     def unpack_a(i, carry):
         r = pl.multiple_of(i * 2 * SH, 16)
-        a = [part(0, z.CA, nn, i) for nn in range(N)]
+        parts = [section(nn, i, 0, z.LA) for nn in range(N)]
         for k in range(3):
             at = GAIN_LANES + k * QN
-            wqkv[pl.ds(r, 2 * SH), k * D:(k + 1) * D] = jnp.concatenate([v[:, at:at + QN] for v in a], axis=1)
-        gcol[pl.ds(r, 2 * SH), :] = a[0][:, 0:128].astype(F32)
+            place_columns(wqkv, r, k * D, [v[:, at:at + QN] for v in parts])
+        gcol[pl.ds(r, 2 * SH), :] = parts[0][:, 0:128].astype(F32)
         return carry
 
     lax.fori_loop(0, W // 2, unpack_a, 0)
@@ -390,8 +423,6 @@
         hat, _ = normed(xin[pl.ds(r, BLOCK), :].astype(F32))
         n1[pl.ds(r, BLOCK), :] = (hat * grow[0:1, :]).astype(BF16)
         return carry
-
-    lax.fori_loop(0, E // BLOCK, norm_rows, 0)
 
     def partner_lanes(x):
         lanes = lax.broadcasted_iota(jnp.int32, x.shape, 1)
@@ -407,15 +438,18 @@
             qkv[:, pl.ds(pl.multiple_of(at + k * 128, 128), 128)] = part_y.astype(BF16)
         return carry
 
-    lax.fori_loop(0, 2 * D // 256, project_turned, 0)
-
     def project(ct, carry):
         at = pl.multiple_of(2 * D + ct * 256, 128)
         qkv[:, pl.ds(at, 256)] = dot(n1[...], wqkv[:, pl.ds(at, 256)], 1, 0).astype(BF16)
         return carry
 
-    lax.fori_loop(0, D // 256, project, 0)
-    gather_step(a_ready + 1)
+    def make_qkv():
+        lax.fori_loop(0, E // BLOCK, norm_rows, 0)
+        lax.fori_loop(0, 2 * D // 256, project_turned, 0)
+        lax.fori_loop(0, D // 256, project, 0)
+
+    gather_events(steps[a_step][a_at:])
+    make_qkv()
 
     att, stat = s["att"], s["stat"]
     lane_row = lax.broadcasted_iota(jnp.int32, (BLOCK, 128), 1)
@@ -456,23 +490,32 @@
             att[pl.ds(pl.multiple_of(b * BLOCK, BLOCK), BLOCK), pl.ds(pl.multiple_of(j * 128, 128), 128)] = got.astype(BF16)
         return carry
 
-    lax.fori_loop(0, z.pairs * (NB // G), attend, 0)
-    for t in range(a_ready + 2, C + stages - 1):
-        gather_step(t)
-
-    def unpack_b(i, carry):
+    def attend_part(lo, up):
+        lax.fori_loop(lo * (NB // G), up * (NB // G), attend, 0)
+
+    half_pairs = z.pairs // 2
+    attend_part(0, half_pairs)
+    gather_events(steps[a_step + 1])
+    attend_part(half_pairs, z.pairs)
+    for t in range(a_step + 2, len(steps)):
+        gather_events(steps[t])
+
+    slices_at = GAIN_LANES + 4 * QN
+
+    def unpack_out(i, carry):
         r = pl.multiple_of(i * 2 * SH, 16)
-        a = [shard_pair(z.CA - 1, nn, i)[:, z.LA - z.O0 - z.cuts[z.CA - 1][0]:] for nn in range(N)] if z.O0 else None
-        bs = [part(z.CA, C, nn, i) for nn in range(N)]
-        o_rest = QN - z.O0
-        wot[pl.ds(r, 2 * SH), :] = jnp.concatenate(
-            [x for nn in range(N) for x in (([a[nn]] if z.O0 else []) + [bs[nn][:, :o_rest]])], axis=1)
-        for k, ref in enumerate((wg, wu, wgo)):
-            at = o_rest + k * FN
-            ref[pl.ds(r, 2 * SH), :] = jnp.concatenate([v[:, at:at + FN] for v in bs], axis=1)
-        return carry
-
-    lax.fori_loop(0, W // 2, unpack_b, 0)
+        place_columns(wot, r, 0, [section(nn, i, GAIN_LANES + 3 * QN, slices_at) for nn in range(N)])
+        return carry
+
+    def unpack_feed(i, carry):
+        r = pl.multiple_of(i * 2 * SH, 16)
+        parts = [section(nn, i, slices_at, slices_at + 3 * FN) for nn in range(N)]
+        for a, ref in enumerate((wg, wu, wgo)):
+            place_columns(ref, r, 0, [v[:, a * FN:(a + 1) * FN] for v in parts])
+        return carry
+
+    lax.fori_loop(0, W // 2, unpack_out, 0)
+    lax.fori_loop(0, W // 2, unpack_feed, 0)
 
     ost, n2, res, resg = s["ost"], s["n2"], s["resr"], s["resg"]
     hid, dgate, dup, datt = s["hid"], s["dgate"], s["dup"], s["datt"]
@@ -505,7 +548,12 @@
             def _():
                 line_copy(dest, rb, key, side, 0, stage).start()
 
+    hops = {"o": N - 2 if N > 2 else N - 1, "t": N - 1}
+
     def token_forward(dest, key, k):
+        if k > hops[key]:
+            return
+
         def body(rb, carry):
             for side in range(2):
                 step = 1 - 2 * side
@@ -514,7 +562,7 @@
                 def _():
                     arrived(line_rows(dest, n - step * k, rb), s[key + "s"].at[rb, side, k - 1], s[key + "r"].at[rb, side, k - 1], (w, n - step))
 
-                if k < N - 1:
+                if k < hops[key]:
                     @pl.when(jnp.logical_and(behind(side) >= k, behind(side) < N - 1))
                     def _():
                         line_copy(dest, rb, key, side, k).start()
@@ -526,7 +574,7 @@
         def body(rb, carry):
             own_copy(stage, dest, rb, key).wait()
             for side in range(2):
-                for k in range(N - 1):
+                for k in range(hops[key]):
                     @pl.when(jnp.logical_and(behind(side) >= k, behind(side) < N - 1))
                     def _():
                         line_copy(dest, rb, key, side, k).wait_send()
@@ -616,10 +664,6 @@
             store_part(list(range(z.CA, C)), nn, t, jnp.concatenate(pieces, axis=1))
         return carry
 
-    transposed(s["n2t"], n2, 0)
-    transposed(s["rt"], res, 0)
-    lax.fori_loop(0, D // TM, grads_b, 0)
-
     scatter_order = [list(range(z.bits)), list(range(z.bits))[::-1]]
 
     def slot_base(t):
@@ -712,8 +756,11 @@
                     rz_finish(c)
 
     part_a, part_b = list(range(z.CA)), list(range(z.CA, C))
+    transposed(s["n2t"], n2, 0)
+    transposed(s["rt"], res, 0)
+    lax.fori_loop(0, D // TM, grads_b, 0)
+
     scatter_advance(part_b, 0)
-    token_forward(out, "o", 1)
 
     dkv, edge, rim, rimr = s["dkv"], s["edge"], s["rim"], s["rimr"]
     dk_ref, dv_ref = dkv.at[0], dkv.at[1]
@@ -762,11 +809,8 @@
         qkv[mid, lv] = dv_ref[mid, :].astype(BF16)
         return carry
 
-    half_pairs = z.pairs // 2
     lax.fori_loop(0, half_pairs, attend_back, 0)
-    scatter_advance(part_b, 1)
-    if N > 2:
-        token_forward(out, "o", 2)
+    token_forward(out, "o", 1)
     lax.fori_loop(half_pairs, z.pairs, attend_back, 0)
 
     def rim_to_prev():
@@ -791,10 +835,8 @@
     def _():
         rimr[1] = jnp.zeros((HALF, 2 * D), BF16)
 
-    for k in range(3, N):
-        token_forward(out, "o", k)
-    for st in range(2, z.bits + 2):
-        scatter_advance(part_b, st)
+    scatter_advance(part_b, 1)
+    transposed(s["rt"], n1, HALF)
 
     @pl.when(has_prev)
     def _():
@@ -838,11 +880,10 @@
     lax.fori_loop(0, z.blocks, input_grad, 0)
 
     gcol[...] = jnp.concatenate([gsum[...], jnp.zeros((120, D), F32)], axis=0).T
-    transposed(s["n2t"], n1, HALF)
 
     def grads_a(t, carry):
         r = pl.multiple_of(t * TM, 16)
-        g = [dot(s["n2t"][pl.ds(r, TM), :], qkv[HALF:HALF + R, k * D:(k + 1) * D], 1, 0) for k in range(3)]
+        g = [dot(s["rt"][pl.ds(r, TM), :], qkv[HALF:HALF + R, k * D:(k + 1) * D], 1, 0) for k in range(3)]
         gains = gcol[pl.ds(r, TM), 0:GAIN_LANES]
         for nn in range(N):
             pieces = [gains] + [v[:, nn * QN:(nn + 1) * QN] for v in g]
@@ -853,22 +894,100 @@
 
     lax.fori_loop(0, D // TM, grads_a, 0)
     scatter_advance(part_a, 0)
-    for st in range(z.bits + 2, last_stage):
+    scatter_advance(part_b, 2)
+    for k in range(2, N):
+        token_forward(out, "o", k)
+    token_end(ost, out, "o")
+
+    far = N - 1 - place
+
+    def far_rows():
+        return pltpu.make_async_copy(tokens.at[pl.ds(pl.multiple_of(far * R, 16), R)], xin.at[pl.ds(HALF, R)], s["l_tok"].at[0])
+
+    def far_low():
+        return pltpu.make_async_copy(tokens.at[pl.ds(T - R - HALF, HALF)], xin.at[pl.ds(0, HALF)], s["l_tok"].at[1])
+
+    def far_high():
+        return pltpu.make_async_copy(tokens.at[pl.ds(R, HALF)], xin.at[pl.ds(HALF + R, HALF)], s["l_tok"].at[2])
+
+    def far_feed(rb, carry):
+        r = pl.multiple_of(rb * MB, 16)
+        rows = pl.ds(r, MB)
+        x = xin[pl.ds(pl.multiple_of(rb * MB + HALF, 16), MB), :].astype(F32)
+        residual = x + dot(att[rows, :], wot[...], 1, 1)
+        n2v = (normed(residual)[0] * grow[1:2, :]).astype(BF16)
+        total_out = residual
+        for f in range(0, F, FC):
+            gate = dot(n2v, wg[:, f:f + FC], 1, 0)
+            upv = dot(n2v, wu[:, f:f + FC], 1, 0)
+            act = gate * (0.5 * (1.0 + jnp.tanh(GELU_A * (gate * (1.0 + GELU_B * (gate * gate))))))
+            total_out = total_out + dot((act * upv).astype(BF16), wgo[:, f:f + FC], 1, 1)
+        ost[rows, :] = total_out.astype(BF16)
+        return carry
+
+    def far_out():
+        return pltpu.make_async_copy(ost, out.at[pl.ds(pl.multiple_of(far * R, 16), R)], s["ol"].at[0])
+
+    def far_project():
+        far_rows().start()
+
+        @pl.when(first)
+        def _():
+            far_low().start()
+            xin[HALF + R:, :] = halo[1]
+
+        @pl.when(last)
+        def _():
+            far_high().start()
+            xin[0:HALF, :] = halo[0]
+
+        tables(far)
+        far_rows().wait()
+
+        @pl.when(first)
+        def _():
+            far_low().wait()
+
+        @pl.when(last)
+        def _():
+            far_high().wait()
+
+        make_qkv()
+
+    def far_finish():
+        lax.fori_loop(0, z.blocks, far_feed, 0)
+        far_out().start()
+        far_out().wait()
+
+    def at_ends(work):
+        if N > 2:
+            pl.when(at_end)(work)
+
+    at_ends(far_project)
+    scatter_advance(part_a, 1)
+    token_forward(tg, "t", 1)
+    at_ends(lambda: attend_part(0, half_pairs))
+    for st in range(3, z.bits + 2):
         scatter_advance(part_b, st)
-    for st in range(1, z.bits + 1):
+    at_ends(lambda: attend_part(half_pairs, z.pairs))
+    scatter_advance(part_a, 2)
+    scatter_advance(part_b, z.bits + 2)
+    if N > 2:
+        token_forward(tg, "t", 2)
+    at_ends(far_finish)
+    for st in range(3, z.bits + 2):
         scatter_advance(part_a, st)
-    token_forward(tg, "t", 1)
-    scatter_advance(part_a, z.bits + 1)
-    for k in range(2, N):
-        token_forward(tg, "t", k)
+    for st in range(z.bits + 3, last_stage):
+        scatter_advance(part_b, st)
     for st in range(z.bits + 2, last_stage):
         scatter_advance(part_a, st)
+    for k in range(3, N):
+        token_forward(tg, "t", k)
 
     for c in pending:
         c.wait_send()
     for c in range(C):
         rz_sent(c)
-    token_end(ost, out, "o")
     token_end(tst, tg, "t")
 
 
@@ -890,6 +1009,7 @@
         vmem(f"r1{c}", (2, W // 2 - 1, N // 2, z.RS, up - lo), BF16)
         vmem(f"rz{c}", (2, N - 1, z.RS, up - lo), BF16)
     vmem("xin", (E, D), BF16)
+    vmem("halo", (2, HALF, D), BF16)
     vmem("n1", (E, D), BF16)
     vmem("qkv", (E, 3 * D), BF16)
     vmem("wqkv", (D, 3 * D), BF16)
@@ -925,7 +1045,7 @@
     for name in ("ss", "sr", "g1s", "g1r"):
         sems(name, C, 2, W // 2 - 1)
     for name in ("ds", "dr"):
-        sems(name, C, 2)
+        sems(name, C, 2, W // 2)
     for name in ("g0s", "g0r"):
         sems(name, C)
     for name in ("hs", "hr", "rs", "rr"):
@@ -943,7 +1063,7 @@
             jax.ShapeDtypeStruct((z.T, D), BF16),
             jax.ShapeDtypeStruct((z.RS, z.lanes), F32),
         ),
-        in_specs=[pl.BlockSpec(memory_space=pltpu.SMEM), hbm, hbm] + [vm] * 6,
+        in_specs=[pl.BlockSpec(memory_space=pltpu.SMEM), hbm, hbm] + [vm] * 7,
         out_specs=(hbm, hbm, vm),
         scratch_shapes=shapes,
         compiler_params=pltpu.CompilerParams(collective_id=0, has_side_effects=True, vmem_limit_bytes=VMEM_BYTES),
@@ -953,35 +1073,34 @@
 VMEM_BYTES = 64 * 1024 * 1024 - 1024 * 64
 
 
-def finish_kernel(z, tg, out, gp, o_out, o_tg, o_in, o_ow, o_gu, o_dn, o_gains, low, full, s_in, s_out, s_copy):
-    rows = low.shape[1]
+def finish_kernel(z, tg, out, gp, o_out, o_tg, o_in, o_ow, o_gu, o_dn, o_one, o_two, low, full, same, s_in, s_out, s_same_in, s_same_out):
+    rows = FINISH_ROWS
     steps = z.T // rows
-    whole = pltpu.make_async_copy(out, o_out, s_copy)
-    whole.start()
-
-    def load(i):
-        return pltpu.make_async_copy(tg.at[pl.ds(i * rows, rows)], low.at[i % 2], s_in.at[i % 2])
-
-    def store(i):
-        return pltpu.make_async_copy(full.at[i % 2], o_tg.at[pl.ds(i * rows, rows)], s_out.at[i % 2])
-
-    load(0).start()
+
+    def part(i):
+        return pl.ds(i * rows, rows)
+
+    loads = [pltpu.make_async_copy(tg.at[part(i)], low.at[part(i)], s_in.at[i]) for i in range(steps)]
+    same_loads = [pltpu.make_async_copy(out.at[part(i)], same.at[part(i)], s_same_in.at[i]) for i in range(steps)]
+    stores = [pltpu.make_async_copy(full.at[part(i)], o_tg.at[part(i)], s_out.at[i]) for i in range(steps)]
+    same_stores = [pltpu.make_async_copy(same.at[part(i)], o_out.at[part(i)], s_same_out.at[i]) for i in range(steps)]
     for i in range(steps):
-        if i + 1 < steps:
-            load(i + 1).start()
-        load(i).wait()
-        if i >= 2:
-            store(i - 2).wait()
-        full[i % 2] = low[i % 2].astype(F32)
-        store(i).start()
-        if i == 0:
-            unpack_grads(z, gp, o_in, o_ow, o_gu, o_dn, o_gains)
-    for i in range(max(0, steps - 2), steps):
-        store(i).wait()
-    whole.wait()
-
-
-def unpack_grads(z, gp, o_in, o_ow, o_gu, o_dn, o_gains):
+        loads[i].start()
+    for c in same_loads:
+        c.start()
+    for i in range(steps):
+        loads[i].wait()
+        full[part(i), :] = low[part(i), :].astype(F32)
+        stores[i].start()
+    for i in range(steps):
+        same_loads[i].wait()
+        same_stores[i].start()
+    unpack_grads(z, gp, o_in, o_ow, o_gu, o_dn, o_one, o_two)
+    for c in stores + same_stores:
+        c.wait()
+
+
+def unpack_grads(z, gp, o_in, o_ow, o_gu, o_dn, o_one, o_two):
     SH, QN, FN = z.SH, z.QN, z.FN
     heads = QN // HEAD_DIM
     value = gp[...][:SH]
@@ -1005,11 +1124,13 @@
         o_gu[:, k, :] = value[:, at + k * FN:at + (k + 1) * FN]
     at += 2 * FN
     o_dn[...] = flipped(value[:, at:at + FN])
-    o_gains[...] = flipped(value[:, :128])[0:8, :]
+    rows = flipped(value[:, :128])
+    o_one[...] = rows[0:1, :]
+    o_two[...] = rows[1:2, :]
 
 
 def finish(z, tg, out, gp):
-    rows = 256
+    rows = FINISH_ROWS
     hbm = pl.BlockSpec(memory_space=pl.ANY)
     vm = pl.BlockSpec(memory_space=pltpu.VMEM)
     return pl.pallas_call(
@@ -1021,30 +1142,32 @@
             jax.ShapeDtypeStruct((z.QN, z.SH), F32),
             jax.ShapeDtypeStruct((z.SH, 2, z.FN), F32),
             jax.ShapeDtypeStruct((z.FN, z.SH), F32),
-            jax.ShapeDtypeStruct((8, z.SH), F32),
+            jax.ShapeDtypeStruct((1, z.SH), F32),
+            jax.ShapeDtypeStruct((1, z.SH), F32),
         ),
         in_specs=[hbm, hbm, vm],
-        out_specs=(hbm, hbm, vm, vm, vm, vm, vm),
+        out_specs=(hbm, hbm) + (vm,) * 6,
         scratch_shapes=[
-            pltpu.VMEM((2, rows, z.D), BF16),
-            pltpu.VMEM((2, rows, z.D), F32),
-            pltpu.SemaphoreType.DMA((2,)),
-            pltpu.SemaphoreType.DMA((2,)),
-            pltpu.SemaphoreType.DMA,
+            pltpu.VMEM((z.T, z.D), BF16),
+            pltpu.VMEM((z.T, z.D), F32),
+            pltpu.VMEM((z.T, z.D), BF16),
+            pltpu.SemaphoreType.DMA((z.T // rows,)),
+            pltpu.SemaphoreType.DMA((z.T // rows,)),
+            pltpu.SemaphoreType.DMA((z.T // rows,)),
+            pltpu.SemaphoreType.DMA((z.T // rows,)),
         ],
-        compiler_params=pltpu.CompilerParams(vmem_limit_bytes=32 * 1024 * 1024),
+        compiler_params=pltpu.CompilerParams(vmem_limit_bytes=VMEM_BYTES),
     )(tg, out, gp)
 
 
 def per_device(tokens, lengths, masked, attention_in, attention_out, geglu_in, geglu_out, gain_attention, gain_feedforward, out_grad):
     wide, narrow = lax.axis_size("wide"), lax.axis_size("narrow")
     z = Sizes(wide, narrow, tokens.shape[0], tokens.shape[1], attention_out.shape[0] * narrow, geglu_out.shape[0] * narrow, lengths.shape[0])
-    gate_up = geglu_in.astype(BF16).reshape(z.SH, 2 * z.FN)
-    gains = jnp.stack([gain_attention, gain_feedforward])
+    gains = [g.reshape(1, z.SH) for g in (gain_attention, gain_feedforward)]
     out, tg, gp = run_layer(
-        z, lengths, tokens, out_grad, masked.reshape(-1, 128), attention_in, attention_out, gate_up, geglu_out, gains)
-    out, tg, g_in, g_out, g_gu, g_down, g_gains = finish(z, tg, out, gp)
-    return (out, tg, g_in, g_out, g_gu, g_down, g_gains[0], g_gains[1])
+        z, lengths, tokens, out_grad, masked.reshape(-1, 128), attention_in, attention_out, geglu_in, geglu_out, *gains)
+    out, tg, g_in, g_out, g_gu, g_down, one, two = finish(z, tg, out, gp)
+    return (out, tg, g_in, g_out, g_gu, g_down, one.reshape(z.SH), two.reshape(z.SH))
 
 
 def solution(mesh):

time: 213 us -> 189 us (0.89)
  Pallas kernels: 204 us -> 188 us
  local copies, waits for them, and re-layouts: 6.17 us -> 0 us
  other arithmetic: 2.31 us -> 0 us
    pallas_call x1, Pallas kernels: 198 us -> 179 us  [run_layer(): pl.pallas_call(functools.partial(layer_kernel, z, names), out_shape=(jax....]
    unnamed x6 -> x0, local copies, waits for them, and re-layouts: 4.85 us -> none
    pallas_call x1, Pallas kernels: 5.88 us -> 8.45 us  [finish(): pl.pallas_call(functools.partial(finish_kernel, z), out_shape=(jax.ShapeD...]
where the time goes in v4:
time: 189 us; the launch traced here: 188 us
  Pallas kernels  188 us (99%)
    pallas_call x1, Pallas kernels, run_layer(): pl.pallas_call(functools.partial(layer_kernel, z, names), out_shape=(jax....  179 us
    pallas_call x1, Pallas kernels, finish(): pl.pallas_call(functools.partial(finish_kernel, z), out_shape=(jax.ShapeD...  8.45 us

profile of v4, /device:TPU:0, one launch (start us, length us, event | category | flops | bytes accessed | tf_op | source)
XLA Modules:
  0.0 188.4 jit_solution(1751583123197689762)
XLA Ops:
  0.6 179.1 %shard_map.161 = (bf16[2048,768]{1,0:T(8,128)(2,1)}, bf16[2048,768]{1,0:T(8,128)(2,1)}, f32[96,1664]{1,0:T(8,128)}) custom-call(s32[8]{0:T(128)} %lengths.1, bf16[2048,768]{1,0:T(8,128)(2,1)} %tokens.1, bf16[2048,768]{1,0:T(8,128)(2,1)} %grads_in.1, s32[16,128]{1,0:T(8,128)} %bitcast.5, f32[96,576]{1,0:T(8,128)} %w_in.1, f32[192,96]{1,0:T(8,128)} %w_out.1, ...), custom_call_target="tpu_custom_call" | custom-call | tf_op jit(solution)/shard_map/pallas_call | solution.py:1059
  179.8 8.5 %shard_map.162 = (bf16[2048,768]{1,0:T(8,128)(2,1)}, f32[2048,768]{1,0:T(8,128)}, f32[96,576]{1,0:T(8,128)}, f32[192,96]{1,0:T(8,128)}, f32[96,2,288]{2,1,0:T(2,...) custom-call(bf16[2048,768]{1,0:T(8,128)(2,1)} %get-tuple-element.19.tg, ...), custom_call_target="tpu_custom_call" | custom-call | tf_op jit(solution)/shard_map/pallas_call | solution.py:1136

commit v5 on v4

--- a/solution.py
+++ b/solution.py
@@ -41,9 +41,10 @@
         self.E = self.R + WINDOW
         self.NB = self.R // BLOCK
         self.pairs = width // 128
-        self.G = 4 if self.NB % 4 == 0 else 1
+        self.G = next(g for g in (4 if self.R <= 512 else 2, 2, 1) if self.NB % g == 0)
         self.SH = width // wide
         self.RS = round_up(self.SH, 16)
+        self.UG = next(g for g in (1, 2, 4, 8) if g * 2 * self.SH % 16 == 0)
         self.QN, self.FN = heads_width // narrow, hidden // narrow
         self.bits = (wide // 2).bit_length() - 1
         first = GAIN_LANES + 3 * self.QN
@@ -52,10 +53,14 @@
         self.lanes = round_up(self.real, 128)
         self.O0 = self.LA - first
         cut_a = (self.LA // 256) * 128
-        mid = self.LA + ((self.lanes - self.LA) // 256) * 128
-        self.cuts = [(0, cut_a), (cut_a, self.LA), (self.LA, mid), (mid, self.lanes)]
+        tiles = (self.lanes - self.LA) // 128
+        end_one = self.LA + (3 * tiles // 8) * 128
+        end_two = end_one + (tiles // 4) * 128
+        self.cuts = [(0, cut_a), (cut_a, self.LA), (self.LA, end_one), (end_one, end_two), (end_two, self.lanes)]
         self.C = len(self.cuts)
         self.CA = 2
+        self.keep = self.R <= 512 and self.SH == self.RS
+        self.CZ = self.C - 1
         self.MB = min(self.R, 256)
         self.blocks = self.R // self.MB
         self.FC = 384 if hidden % 384 == 0 else hidden
@@ -207,7 +212,7 @@
     def gather_event(c, st):
         if st == 0:
             z_wait(c)
-            if c + 1 < C:
+            if c + 1 < z.CZ:
                 z_start(c + 1)
         elif st <= z.bits:
             s_wait(c, st - 1)
@@ -220,9 +225,80 @@
         if st == z.bits:
             d_start(c, True)
 
-    steps = [[(t - st, st) for st in reversed(range(stages)) if 0 <= t - st < C] for t in range(C + stages - 1)]
+    L = C - 1
+    l_lanes = z.cuts[L][1] - z.cuts[L][0]
+    half_lanes = [slice(0, round_up(l_lanes // 2, 128)), slice(round_up(l_lanes // 2, 128), l_lanes)]
+
+    def behind(side):
+        return n if side == 0 else N - 1 - n
+
+    def l_own():
+        return pltpu.make_async_copy(pk.at[:, z.cuts[L][0]:], wb[L].at[n, hi, core], s["l_own"].at[L])
+
+    def l_start(t):
+        for h in range(2):
+            b = gather_order[h][t]
+            for i, combo in enumerate(combos(gather_order[h][:t])):
+                ref = wb[L].at[n, flip(hi, combo), core, :, half_lanes[h]]
+                slot = (1 << t) - 1 + i
+                send(ref, ref, s["ss"].at[L, h, slot], s["sr"].at[L, h, slot], bit_dev(b))
+
+    def l_wait(t):
+        for h in range(2):
+            b = gather_order[h][t]
+            for i, combo in enumerate(combos(gather_order[h][:t])):
+                ref = wb[L].at[n, flip(hi, combo + [b]), core, :, half_lanes[h]]
+                slot = (1 << t) - 1 + i
+                arrived(ref, s["ss"].at[L, h, slot], s["sr"].at[L, h, slot], bit_dev(b))
+
+    def hop_copy(side, k):
+        step = 1 - 2 * side
+        ref = wb[L].at[n - step * k, :, core]
+        return copy_to(ref, ref, s["lzs"].at[side, k], s["lzr"].at[side, k], (w, n + step))
+
+    def core_copy(side, k, whose):
+        ref = wb[L].at[n - (1 - 2 * side) * k, :, whose]
+        return copy_to(ref, ref, s["lds"].at[side, k], s["ldr"].at[side, k], sib_dev)
+
+    def l_own_group():
+        core_copy(0, 0, core).start()
+        for side in range(2):
+            @pl.when(behind(side) < N - 1)
+            def _():
+                hop_copy(side, 0).start()
+
+    def l_hop(k):
+        for side in range(2):
+            step = 1 - 2 * side
+
+            @pl.when(behind(side) > k)
+            def _():
+                arrived(wb[L].at[n - step * (k + 1), :, core], s["lzs"].at[side, k], s["lzr"].at[side, k], (w, n - step))
+                core_copy(side, k + 1, core).start()
+
+            if k + 1 < N - 1:
+                @pl.when(jnp.logical_and(behind(side) > k, behind(side) < N - 1))
+                def _():
+                    hop_copy(side, k + 1).start()
+
+    def l_done():
+        core_copy(0, 0, 1 - core).wait_recv()
+        core_copy(0, 0, core).wait_send()
+        for side in range(2):
+            for k in range(N - 1):
+                @pl.when(behind(side) > k)
+                def _():
+                    core_copy(side, k + 1, 1 - core).wait_recv()
+                    core_copy(side, k + 1, core).wait_send()
+
+                @pl.when(jnp.logical_and(behind(side) >= k, behind(side) < N - 1))
+                def _():
+                    hop_copy(side, k).wait_send()
+
+    steps = [[(t - st, st) for st in reversed(range(stages)) if 0 <= t - st < z.CZ] for t in range(z.CZ + stages - 1)]
     a_step = z.CA - 1 + stages - 1
-    a_at = steps[a_step].index((z.CA - 1, stages - 1)) + 1
+    before_a = [[e for e in step if e[0] < z.CA or t < a_step - 1] for t, step in enumerate(steps[:a_step + 1])]
+    after_a = [[e for e in step if e not in (before_a[t] if t <= a_step else [])] for t, step in enumerate(steps)]
 
     def gather_events(events):
         for c, st in events:
@@ -231,6 +307,9 @@
     z_start(0)
     raw_gate, raw_up, raw_down = w_gu[:, 0, :], w_gu[:, 1, :], flipped(w_down[...])
     pack(z.LA, z.lanes, [out_t[:, z.O0:]] + [raw_gate, raw_up, raw_down])
+    l_own().start()
+    l_own().wait()
+    l_start(0)
 
     xin = s["xin"]
     own = pltpu.make_async_copy(tokens.at[pl.ds(pl.multiple_of(place * R, 16), R)], xin.at[pl.ds(HALF, R)], s["l_tok"].at[0])
@@ -318,9 +397,14 @@
         bias_t[b] = jnp.where(jnp.logical_and(dk == dq, near), 0.0, NEG_LARGE).astype(F32)
         return carry
 
-    gather_events(steps[0])
+    for t in range(z.bits):
+        l_wait(t)
+        if t + 1 < z.bits:
+            l_start(t + 1)
+    gather_events(before_a[0])
     tables(place)
-    gather_events(steps[1])
+    gather_events(before_a[1])
+    l_own_group()
 
     own.wait()
 
@@ -350,7 +434,7 @@
     def _():
         xin[HALF + R:, :] = halo[1]
 
-    gather_events(steps[2])
+    gather_events(before_a[2])
     own_cot.wait()
 
     def mask_rows(b, carry):
@@ -362,7 +446,11 @@
 
     lax.fori_loop(0, NB, mask_rows, 0)
 
-    def transposed(dst, src, row0):
+    def transposed(name, src, row0):
+        if not z.keep:
+            return
+        dst = s[name]
+
         def body(i, carry):
             at = pl.multiple_of(i * 128, 128)
             dst[pl.ds(at, 128), :] = src[row0:row0 + R, pl.ds(at, 128)].astype(F32).T.astype(BF16)
@@ -370,14 +458,18 @@
 
         lax.fori_loop(0, D // 128, body, 0)
 
-    transposed(s["ct"], cot, 0)
+    transposed("ct", cot, 0)
 
     for t in range(3, a_step):
-        gather_events(steps[t])
-    gather_events(steps[a_step][:a_at])
+        gather_events(before_a[t])
+    l_hop(0)
+    gather_events(before_a[a_step])
 
     wqkv, wot, wg, wu, wgo = s["wqkv"], s["wot"], s["wg"], s["wu"], s["wgo"]
     gcol, grow, gsum = s["gcol"], s["grow"], s["gsum"]
+
+    UG = z.UG
+    UR = UG * 2 * SH
 
     def section(nn, i, lo, up):
         found = []
@@ -386,7 +478,7 @@
             if x >= y:
                 continue
             x0, y0 = (x - a) // 128 * 128, round_up(y - a, 128)
-            both = [wb[c][nn, i, k, :, x0:y0] for k in range(2)]
+            both = [wb[c][nn, i * UG + a2, k, :, x0:y0] for a2 in range(UG) for k in range(2)]
             if SH % 16 == 0:
                 v = jnp.concatenate([q[:SH] for q in both], axis=0)
             else:
@@ -396,18 +488,18 @@
 
     def place_columns(ref, r, at, sections):
         width = sum(v.shape[1] for v in sections)
-        ref[pl.ds(r, 2 * SH), at:at + width] = jnp.concatenate(sections, axis=1)
+        ref[pl.ds(r, UR), at:at + width] = jnp.concatenate(sections, axis=1)
 
     def unpack_a(i, carry):
-        r = pl.multiple_of(i * 2 * SH, 16)
+        r = pl.multiple_of(i * UR, 16)
         parts = [section(nn, i, 0, z.LA) for nn in range(N)]
         for k in range(3):
             at = GAIN_LANES + k * QN
             place_columns(wqkv, r, k * D, [v[:, at:at + QN] for v in parts])
-        gcol[pl.ds(r, 2 * SH), :] = parts[0][:, 0:128].astype(F32)
-        return carry
-
-    lax.fori_loop(0, W // 2, unpack_a, 0)
+        gcol[pl.ds(r, UR), :] = parts[0][:, 0:128].astype(F32)
+        return carry
+
+    lax.fori_loop(0, W // 2 // UG, unpack_a, 0)
     grow[...] = gcol[...].T[0:8, :]
     gsum[...] = jnp.zeros((8, D), F32)
 
@@ -448,10 +540,14 @@
         lax.fori_loop(0, 2 * D // 256, project_turned, 0)
         lax.fori_loop(0, D // 256, project, 0)
 
-    gather_events(steps[a_step][a_at:])
+    for t in range(a_step):
+        gather_events(after_a[t])
+    if N > 2:
+        l_hop(1)
     make_qkv()
-
-    att, stat = s["att"], s["stat"]
+    gather_events(after_a[a_step])
+
+    att, stat = s["att"], s.get("stat")
     lane_row = lax.broadcasted_iota(jnp.int32, (BLOCK, 128), 1)
     keep_one = jnp.where(lane_row < HEAD_DIM, 1.0, 0.0).astype(BF16)
     keep_two = jnp.where(lane_row < HEAD_DIM, 0.0, 1.0).astype(BF16)
@@ -484,9 +580,13 @@
             top = jnp.max(scores, axis=0, keepdims=True)
             weights = jnp.exp(scores - top)
             inv = 1.0 / jnp.sum(weights, axis=0, keepdims=True)
-            stat[u, 0:1, :] = top
-            stat[u, 1:2, :] = inv
-            got = unstacked(dot(vp, (weights * inv).astype(BF16), 0, 0))
+            probs = weights * inv
+            if z.keep:
+                s["kept"][u] = probs
+            else:
+                stat[u, 0:1, :] = top
+                stat[u, 1:2, :] = inv
+            got = unstacked(dot(vp, probs.astype(BF16), 0, 0))
             att[pl.ds(pl.multiple_of(b * BLOCK, BLOCK), BLOCK), pl.ds(pl.multiple_of(j * 128, 128), 128)] = got.astype(BF16)
         return carry
 
@@ -494,28 +594,36 @@
         lax.fori_loop(lo * (NB // G), up * (NB // G), attend, 0)
 
     half_pairs = z.pairs // 2
-    attend_part(0, half_pairs)
-    gather_events(steps[a_step + 1])
-    attend_part(half_pairs, z.pairs)
+    third = z.pairs // 3
+    attend_part(0, third)
+    for k in range(2, N - 1):
+        l_hop(k)
+    attend_part(third, 2 * third)
+    gather_events(after_a[a_step + 1])
+    attend_part(2 * third, z.pairs)
     for t in range(a_step + 2, len(steps)):
-        gather_events(steps[t])
+        gather_events(after_a[t])
 
     slices_at = GAIN_LANES + 4 * QN
 
-    def unpack_out(i, carry):
-        r = pl.multiple_of(i * 2 * SH, 16)
-        place_columns(wot, r, 0, [section(nn, i, GAIN_LANES + 3 * QN, slices_at) for nn in range(N)])
-        return carry
-
-    def unpack_feed(i, carry):
-        r = pl.multiple_of(i * 2 * SH, 16)
-        parts = [section(nn, i, slices_at, slices_at + 3 * FN) for nn in range(N)]
-        for a, ref in enumerate((wg, wu, wgo)):
-            place_columns(ref, r, 0, [v[:, a * FN:(a + 1) * FN] for v in parts])
-        return carry
-
-    lax.fori_loop(0, W // 2, unpack_out, 0)
-    lax.fori_loop(0, W // 2, unpack_feed, 0)
+    def unpack_first(i, carry):
+        r = pl.multiple_of(i * UR, 16)
+        lo = GAIN_LANES + 3 * QN
+        parts = [section(nn, i, lo, slices_at + FN) for nn in range(N)]
+        place_columns(wot, r, 0, [v[:, :QN] for v in parts])
+        place_columns(wg, r, 0, [v[:, QN:] for v in parts])
+        return carry
+
+    def unpack_second(i, carry):
+        r = pl.multiple_of(i * UR, 16)
+        parts = [section(nn, i, slices_at + FN, slices_at + 3 * FN) for nn in range(N)]
+        place_columns(wu, r, 0, [v[:, :FN] for v in parts])
+        place_columns(wgo, r, 0, [v[:, FN:] for v in parts])
+        return carry
+
+    lax.fori_loop(0, W // 2 // UG, unpack_first, 0)
+    l_done()
+    lax.fori_loop(0, W // 2 // UG, unpack_second, 0)
 
     ost, n2, res, resg = s["ost"], s["n2"], s["resr"], s["resg"]
     hid, dgate, dup, datt = s["hid"], s["dgate"], s["dup"], s["datt"]
@@ -528,9 +636,6 @@
     def line_rows(dest, m, rb):
         theirs = m + core * (N - 1 - 2 * m)
         return dest.at[pl.ds(pl.multiple_of(theirs * R + rb * MB, 16), MB)]
-
-    def behind(side):
-        return n if side == 0 else N - 1 - n
 
     def line_copy(dest, rb, key, side, k, stage=None):
         step = 1 - 2 * side
@@ -570,11 +675,12 @@
 
         lax.fori_loop(0, z.blocks, body, 0)
 
-    def token_end(stage, dest, key):
+    def token_sent(stage, dest, key, lo, up):
         def body(rb, carry):
-            own_copy(stage, dest, rb, key).wait()
+            if lo == 0:
+                own_copy(stage, dest, rb, key).wait()
             for side in range(2):
-                for k in range(hops[key]):
+                for k in range(lo, up):
                     @pl.when(jnp.logical_and(behind(side) >= k, behind(side) < N - 1))
                     def _():
                         line_copy(dest, rb, key, side, k).wait_send()
@@ -644,13 +750,24 @@
                     at = (2 * i + k) * SH
                     store_rows(c, nn, t * HT + i, k, value[at:at + SH, a - lo:b - lo])
 
+    def turned_dot(name, src, row0, t, rhs):
+        if z.keep:
+            return dot(s[name][pl.ds(pl.multiple_of(t * TM, 16), TM), :], rhs, 1, 0)
+        return dot(src[row0:row0 + R, t * TM:(t + 1) * TM], rhs, 0, 0)
+
+    def tiles(body):
+        if z.keep:
+            lax.fori_loop(0, D // TM, body, 0)
+        else:
+            for t in range(D // TM):
+                body(t, 0)
+
     def grads_b(t, carry):
         r = pl.multiple_of(t * TM, 16)
-        cols = pl.ds(pl.multiple_of(t * TM, 128), TM) if TM % 128 == 0 else None
-        gg = dot(s["n2t"][pl.ds(r, TM), :], dgate[...], 1, 0)
-        gu = dot(s["n2t"][pl.ds(r, TM), :], dup[...], 1, 0)
-        go = dot(s["ct"][pl.ds(r, TM), :], hid[...], 1, 0)
-        gw = dot(s["rt"][pl.ds(r, TM), :], att[...], 1, 0)
+        gg = turned_dot("n2t", n2, 0, t, dgate[...])
+        gu = turned_dot("n2t", n2, 0, t, dup[...])
+        go = turned_dot("ct", cot, 0, t, hid[...])
+        gw = turned_dot("rt", res, 0, t, att[...])
         if z.O0:
             firsts = [gw[:, nn * QN:nn * QN + z.O0] for nn in range(N)]
             spare = owx.shape[1] - N * z.O0
@@ -710,14 +827,14 @@
 
             @pl.when(behind(side) == r)
             def _():
-                if r > 0:
-                    for d in range(N - r):
+                for d in reversed(range(N - r)):
+                    if r > 0:
                         arrived(rz[c].at[side, d], s["g2s"].at[c, side, d], s["g2r"].at[c, side, d], (w, n - step))
-                    for d in range(1, N - r):
-                        m = n + step * d
-                        wb[c][m, hi, core] = (wb[c][m, hi, core].astype(F32) + rz[c][side, d].astype(F32)).astype(BF16)
-                for d in range(N - 1 - r):
-                    rz_copy(c, side, d).start()
+                        if d > 0:
+                            m = n + step * d
+                            wb[c][m, hi, core] = (wb[c][m, hi, core].astype(F32) + rz[c][side, d].astype(F32)).astype(BF16)
+                    if d > 0:
+                        rz_copy(c, side, d - 1).start()
 
     def rz_sent(c):
         for side in range(2):
@@ -756,9 +873,9 @@
                     rz_finish(c)
 
     part_a, part_b = list(range(z.CA)), list(range(z.CA, C))
-    transposed(s["n2t"], n2, 0)
-    transposed(s["rt"], res, 0)
-    lax.fori_loop(0, D // TM, grads_b, 0)
+    transposed("n2t", n2, 0)
+    transposed("rt", res, 0)
+    tiles(grads_b)
 
     scatter_advance(part_b, 0)
 
@@ -774,8 +891,12 @@
                 b = g * G + i
                 u = j * NB + b
                 (lq, lk, lv), keys, queries = unit_refs(j, b)
-                qs, kp, vp, scores = unit_scores(j, b)
-                probs = jnp.exp(scores - stat[u, 0:1, :]) * stat[u, 1:2, :]
+                if z.keep:
+                    qs, kp, vp = stacked(qkv[queries, lq]), qkv[keys, lk], qkv[keys, lv]
+                    probs = s["kept"][u]
+                else:
+                    qs, kp, vp, scores = unit_scores(j, b)
+                    probs = jnp.exp(scores - stat[u, 0:1, :]) * stat[u, 1:2, :]
                 gs = stacked(datt[pl.ds(pl.multiple_of(b * BLOCK, BLOCK), BLOCK), pl.ds(pl.multiple_of(j * 128, 128), 128)])
                 prob_grad = dot(vp, gs, 1, 1)
                 row_dot = jnp.sum(probs * prob_grad, axis=0, keepdims=True)
@@ -809,9 +930,11 @@
         qkv[mid, lv] = dv_ref[mid, :].astype(BF16)
         return carry
 
-    lax.fori_loop(0, half_pairs, attend_back, 0)
+    lax.fori_loop(0, third, attend_back, 0)
     token_forward(out, "o", 1)
-    lax.fori_loop(half_pairs, z.pairs, attend_back, 0)
+    lax.fori_loop(third, 2 * third, attend_back, 0)
+    scatter_advance(part_b, 1)
+    lax.fori_loop(2 * third, z.pairs, attend_back, 0)
 
     def rim_to_prev():
         return copy_to(rim.at[0], rimr.at[1], s["rs"].at[0], s["rr"].at[1], prev_dev)
@@ -835,8 +958,7 @@
     def _():
         rimr[1] = jnp.zeros((HALF, 2 * D), BF16)
 
-    scatter_advance(part_b, 1)
-    transposed(s["rt"], n1, HALF)
+    transposed("rt", n1, HALF)
 
     @pl.when(has_prev)
     def _():
@@ -883,7 +1005,7 @@
 
     def grads_a(t, carry):
         r = pl.multiple_of(t * TM, 16)
-        g = [dot(s["rt"][pl.ds(r, TM), :], qkv[HALF:HALF + R, k * D:(k + 1) * D], 1, 0) for k in range(3)]
+        g = [turned_dot("rt", n1, HALF, t, qkv[HALF:HALF + R, k * D:(k + 1) * D]) for k in range(3)]
         gains = gcol[pl.ds(r, TM), 0:GAIN_LANES]
         for nn in range(N):
             pieces = [gains] + [v[:, nn * QN:(nn + 1) * QN] for v in g]
@@ -892,12 +1014,10 @@
             store_part(part_a, nn, t, jnp.concatenate(pieces, axis=1))
         return carry
 
-    lax.fori_loop(0, D // TM, grads_a, 0)
+    tiles(grads_a)
     scatter_advance(part_a, 0)
     scatter_advance(part_b, 2)
-    for k in range(2, N):
-        token_forward(out, "o", k)
-    token_end(ost, out, "o")
+    token_sent(ost, out, "o", 0, 1)
 
     far = N - 1 - place
 
@@ -966,20 +1086,20 @@
     at_ends(far_project)
     scatter_advance(part_a, 1)
     token_forward(tg, "t", 1)
-    at_ends(lambda: attend_part(0, half_pairs))
     for st in range(3, z.bits + 2):
         scatter_advance(part_b, st)
-    at_ends(lambda: attend_part(half_pairs, z.pairs))
+    at_ends(functools.partial(attend_part, 0, half_pairs))
+    at_ends(functools.partial(attend_part, half_pairs, z.pairs))
     scatter_advance(part_a, 2)
-    scatter_advance(part_b, z.bits + 2)
-    if N > 2:
-        token_forward(tg, "t", 2)
     at_ends(far_finish)
     for st in range(3, z.bits + 2):
         scatter_advance(part_a, st)
-    for st in range(z.bits + 3, last_stage):
+    for k in range(2, N):
+        token_forward(out, "o", k)
+    if N > 2:
+        token_forward(tg, "t", 2)
+    for st in range(z.bits + 2, last_stage):
         scatter_advance(part_b, st)
-    for st in range(z.bits + 2, last_stage):
         scatter_advance(part_a, st)
     for k in range(3, N):
         token_forward(tg, "t", k)
@@ -988,7 +1108,8 @@
         c.wait_send()
     for c in range(C):
         rz_sent(c)
-    token_end(tst, tg, "t")
+    token_sent(ost, out, "o", 1, hops["o"])
+    token_sent(tst, tg, "t", 0, hops["t"])
 
 
 def run_layer(z, *args):
@@ -1023,12 +1144,16 @@
     vmem("cos", (E, 128), F32)
     vmem("sin", (E, 128), F32)
     vmem("bias", (z.NB, SPAN, BLOCK), F32)
-    vmem("stat", (z.pairs * z.NB, 8, 2 * BLOCK), F32)
+    if z.keep:
+        vmem("kept", (z.pairs * z.NB, SPAN, 2 * BLOCK), F32)
+    else:
+        vmem("stat", (z.pairs * z.NB, 8, 2 * BLOCK), F32)
     vmem("pk", (z.RS, z.lanes), BF16)
     for name in ("att", "ost", "n2", "resr", "datt", "cot"):
         vmem(name, (R, D), BF16)
-    for name in ("n2t", "ct", "rt"):
-        vmem(name, (D, R), BF16)
+    if z.keep:
+        for name in ("n2t", "ct", "rt"):
+            vmem(name, (D, R), BF16)
     vmem("resg", (R, D), F32)
     for name in ("hid", "dgate", "dup"):
         vmem(name, (R, F), BF16)
@@ -1050,6 +1175,10 @@
         sems(name, C)
     for name in ("hs", "hr", "rs", "rr"):
         sems(name, 2)
+    for name in ("lzs", "lzr"):
+        sems(name, 2, N - 1)
+    for name in ("lds", "ldr"):
+        sems(name, 2, N)
     for name in ("ol", "tl"):
         sems(name, z.blocks)
     for name in ("os", "or", "ts", "tr"):
@@ -1086,13 +1215,11 @@
     same_stores = [pltpu.make_async_copy(same.at[part(i)], o_out.at[part(i)], s_same_out.at[i]) for i in range(steps)]
     for i in range(steps):
         loads[i].start()
-    for c in same_loads:
-        c.start()
+        same_loads[i].start()
     for i in range(steps):
         loads[i].wait()
         full[part(i), :] = low[part(i), :].astype(F32)
         stores[i].start()
-    for i in range(steps):
         same_loads[i].wait()
         same_stores[i].start()
     unpack_grads(z, gp, o_in, o_ow, o_gu, o_dn, o_one, o_two)

time: 189 us -> 181 us (0.958)
  Pallas kernels: 188 us -> 180 us
    pallas_call x1, Pallas kernels: 179 us -> 173 us  [run_layer(): pl.pallas_call(functools.partial(layer_kernel, z, names), out_shape=(jax....]
where the time goes in v5:
time: 181 us
  Pallas kernels  180 us (99%)
    pallas_call x1, Pallas kernels, run_layer(): pl.pallas_call(functools.partial(layer_kernel, z, names), out_shape=(jax....  173 us
    pallas_call x1, Pallas kernels, finish(): pl.pallas_call(functools.partial(finish_kernel, z), out_shape=(jax.ShapeD...  7.76 us

profile of v5, /device:TPU:0, one launch (start us, length us, event | category | flops | bytes accessed | tf_op | source)
XLA Modules:
  0.0 181.2 jit_solution(4273329482241614567)
XLA Ops:
  0.6 172.6 %shard_map.161 = (bf16[2048,768]{1,0:T(8,128)(2,1)}, bf16[2048,768]{1,0:T(8,128)(2,1)}, f32[96,1664]{1,0:T(8,128)}) custom-call(s32[8]{0:T(128)} %lengths.1, bf16[2048,768]{1,0:T(8,128)(2,1)} %tokens.1, bf16[2048,768]{1,0:T(8,128)(2,1)} %grads_in.1, s32[16,128]{1,0:T(8,128)} %bitcast.5, f32[96,576]{1,0:T(8,128)} %w_in.1, f32[192,96]{1,0:T(8,128)} %w_out.1, ...), custom_call_target="tpu_custom_call" | custom-call | tf_op jit(solution)/shard_map/pallas_call | solution.py:1188
  173.2 7.8 %shard_map.162 = (bf16[2048,768]{1,0:T(8,128)(2,1)}, f32[2048,768]{1,0:T(8,128)}, f32[96,576]{1,0:T(8,128)}, f32[192,96]{1,0:T(8,128)}, f32[96,2,288]{2,1,0:T(2,...) custom-call(bf16[2048,768]{1,0:T(8,128)(2,1)} %get-tuple-element.19.tg, ...), custom_call_target="tpu_custom_call" | custom-call | tf_op jit(solution)/shard_map/pallas_call | solution.py:1263

commit v6 on v5

--- a/solution.py
+++ b/solution.py
@@ -460,11 +460,6 @@
 
     transposed("ct", cot, 0)
 
-    for t in range(3, a_step):
-        gather_events(before_a[t])
-    l_hop(0)
-    gather_events(before_a[a_step])
-
     wqkv, wot, wg, wu, wgo = s["wqkv"], s["wot"], s["wg"], s["wu"], s["wgo"]
     gcol, grow, gsum = s["gcol"], s["grow"], s["gsum"]
 
@@ -490,18 +485,19 @@
         width = sum(v.shape[1] for v in sections)
         ref[pl.ds(r, UR), at:at + width] = jnp.concatenate(sections, axis=1)
 
+    def unpack_query(i, carry):
+        r = pl.multiple_of(i * UR, 16)
+        parts = [section(nn, i, 0, GAIN_LANES + QN) for nn in range(N)]
+        place_columns(wqkv, r, 0, [v[:, GAIN_LANES:] for v in parts])
+        gcol[pl.ds(r, UR), :] = jnp.concatenate([parts[0][:, :GAIN_LANES].astype(F32), jnp.zeros((UR, 128 - GAIN_LANES), F32)], axis=1)
+        return carry
+
     def unpack_a(i, carry):
         r = pl.multiple_of(i * UR, 16)
-        parts = [section(nn, i, 0, z.LA) for nn in range(N)]
-        for k in range(3):
-            at = GAIN_LANES + k * QN
-            place_columns(wqkv, r, k * D, [v[:, at:at + QN] for v in parts])
-        gcol[pl.ds(r, UR), :] = parts[0][:, 0:128].astype(F32)
-        return carry
-
-    lax.fori_loop(0, W // 2 // UG, unpack_a, 0)
-    grow[...] = gcol[...].T[0:8, :]
-    gsum[...] = jnp.zeros((8, D), F32)
+        parts = [section(nn, i, GAIN_LANES + QN, GAIN_LANES + 3 * QN) for nn in range(N)]
+        for k in range(2):
+            place_columns(wqkv, r, (k + 1) * D, [v[:, k * QN:(k + 1) * QN] for v in parts])
+        return carry
 
     def normed(x):
         centred = x - jnp.mean(x, axis=-1, keepdims=True)
@@ -535,16 +531,41 @@
         qkv[:, pl.ds(at, 256)] = dot(n1[...], wqkv[:, pl.ds(at, 256)], 1, 0).astype(BF16)
         return carry
 
+    gsum[...] = jnp.zeros((8, D), F32)
+
+    def make_query():
+        lax.fori_loop(0, E // BLOCK, norm_rows, 0)
+        lax.fori_loop(0, D // 256, project_turned, 0)
+
+    def make_key_value():
+        lax.fori_loop(D // 256, 2 * D // 256, project_turned, 0)
+        lax.fori_loop(0, D // 256, project, 0)
+
     def make_qkv():
-        lax.fori_loop(0, E // BLOCK, norm_rows, 0)
-        lax.fori_loop(0, 2 * D // 256, project_turned, 0)
-        lax.fori_loop(0, D // 256, project, 0)
-
+        make_query()
+        make_key_value()
+
+    def begin_query():
+        lax.fori_loop(0, W // 2 // UG, unpack_query, 0)
+        grow[...] = gcol[...].T[0:8, :]
+        make_query()
+
+    early = z.cuts[0][1] >= GAIN_LANES + QN
+    for t in range(3, a_step):
+        for e in before_a[t]:
+            gather_events([e])
+            if early and e == (0, stages - 1):
+                begin_query()
+    l_hop(0)
+    gather_events(before_a[a_step])
+    if not early:
+        begin_query()
+    lax.fori_loop(0, W // 2 // UG, unpack_a, 0)
     for t in range(a_step):
         gather_events(after_a[t])
     if N > 2:
         l_hop(1)
-    make_qkv()
+    make_key_value()
     gather_events(after_a[a_step])
 
     att, stat = s["att"], s.get("stat")

time: 181 us -> 179 us (0.989)
  Pallas kernels: 180 us -> 178 us
    pallas_call x1, Pallas kernels: 173 us -> 170 us  [run_layer(): pl.pallas_call(functools.partial(layer_kernel, z, names), out_shape=(jax....]
where the time goes in v6:
time: 179 us
  Pallas kernels  178 us (99%)
    pallas_call x1, Pallas kernels, run_layer(): pl.pallas_call(functools.partial(layer_kernel, z, names), out_shape=(jax....  170 us
    pallas_call x1, Pallas kernels, finish(): pl.pallas_call(functools.partial(finish_kernel, z), out_shape=(jax.ShapeD...  7.76 us

profile of v6, /device:TPU:0, one launch (start us, length us, event | category | flops | bytes accessed | tf_op | source)
XLA Modules:
  0.0 179.0 jit_solution(11907305051416628765)
XLA Ops:
  0.6 170.4 %shard_map.161 = (bf16[2048,768]{1,0:T(8,128)(2,1)}, bf16[2048,768]{1,0:T(8,128)(2,1)}, f32[96,1664]{1,0:T(8,128)}) custom-call(s32[8]{0:T(128)} %lengths.1, bf16[2048,768]{1,0:T(8,128)(2,1)} %tokens.1, bf16[2048,768]{1,0:T(8,128)(2,1)} %grads_in.1, s32[16,128]{1,0:T(8,128)} %bitcast.5, f32[96,576]{1,0:T(8,128)} %w_in.1, f32[192,96]{1,0:T(8,128)} %w_out.1, ...), custom_call_target="tpu_custom_call" | custom-call | tf_op jit(solution)/shard_map/pallas_call | solution.py:1209
  171.1 7.8 %shard_map.162 = (bf16[2048,768]{1,0:T(8,128)(2,1)}, f32[2048,768]{1,0:T(8,128)}, f32[96,576]{1,0:T(8,128)}, f32[192,96]{1,0:T(8,128)}, f32[96,2,288]{2,1,0:T(2,...) custom-call(bf16[2048,768]{1,0:T(8,128)(2,1)} %get-tuple-element.19.tg, ...), custom_call_target="tpu_custom_call" | custom-call | tf_op jit(solution)/shard_map/pallas_call | solution.py:1284
